TPU v7x, 256 devices: a whole 4x4x8 slice. The times are simulated.
256 devices in a mesh: harm: 32 (over y_lo, z, core), band: 8 (over y_hi, x).
Axes of the slice: x: 4, y: 4 (y_hi: 2, y_lo: 2; y = y_hi * 2 + y_lo), z: 8, core: 2. Of those that a mesh axis runs over, the one named last changes fastest.
Arguments:
- right_side: float32 [64, 4, 5120], P('harm'), may hold values from -50 to 50
- inv_spectra: float32 [2, 5120], replicated, may hold values from 0.1 to 10
- beam: float32 [5120], replicated, may hold values from 0.2 to 1
- m_values: int32 [64], P('harm'), may hold values from 0 to 5119, as said below
- legendre: bfloat16 [64, 2, 5120, 1024], P('harm', None, None, 'band'), may hold values from -0.078125 to 0.078125
- stencil_weights: float32 [16, 32, 8, 32, 128], P(None, 'harm', 'band'), may hold values from -0.25 to 0.5
- stencil_base: int32 [2, 32, 8, 32, 128], P(None, 'harm', 'band'), may hold values from 0 to 640, as said below
- inv_noise: float32 [2, 32, 8, 32, 128], P(None, 'harm', 'band'), may hold values from 0.25 to 4
- slot_counts: int32 [32, 8, 32], P('harm', 'band'), may hold values from 16 to 128, as said below
Outputs:
- solution_coefs: float32 [64, 4, 5120], P('harm', None, 'band')
- residual: float32 [64, 4, 5120], P('harm', None, 'band')
Inputs may be any that keep to these rules, and one draw needn't show every extreme that they name: `m_values`: distinct values. `stencil_base`: row 0 lies in 0 .. 128, row 1 in 0 .. 640. `slot_counts`: in every band some pixel owner receives 128 live slots from every device of the band.
All inputs are finite; a program needn't handle non-finite values.
Results may differ from a plain program's by a relative error of at most 0.0039.
Values may be sent and summed in bfloat16 or wider, within the bound.
No kernel may reach another device: no remote copies, remote signals or barrier semaphores. Data moves between devices by JAX's collectives and lax.ppermute only.
A program may use at most 64 MiB of HBM per device.

v0:
```python
import math

import jax
import jax.numpy as jnp
from jax import lax
from jax.sharding import PartitionSpec as P

NPHI = 20480


def extended(block, sides, width, periodic):
    for axis, dim in sides:
        count = lax.axis_size(axis)
        forward = [(i, i + 1) for i in range(count - 1)]
        if periodic:
            forward.append((count - 1, 0))
        backward = [(target, source) for source, target in forward]
        low = lax.ppermute(
            lax.slice_in_dim(block, block.shape[dim] - width, None, axis=dim), axis, forward
        )
        high = lax.ppermute(lax.slice_in_dim(block, 0, width, axis=dim), axis, backward)
        block = jnp.concatenate([low, block, high], axis=dim)
    return block


def shifted(value, axis, by):
    count = lax.axis_size(axis)
    pairs = [(i, i + by) for i in range(count) if 0 <= i + by < count]
    return lax.ppermute(value, axis, pairs)


def from_behind(block, axis, distance):
    devices = range(lax.axis_size(axis))
    route = [((i - distance) % len(devices), i) for i in devices]
    return lax.ppermute(block, axis, route)


def spin_fields(cycle_modes):
    q_real = -(cycle_modes[:, 0, 0] - cycle_modes[:, 3, 1])
    q_imag = -(cycle_modes[:, 1, 0] + cycle_modes[:, 2, 1])
    u_real = -(cycle_modes[:, 2, 0] + cycle_modes[:, 1, 1])
    u_imag = -(cycle_modes[:, 3, 0] - cycle_modes[:, 0, 1])
    return jnp.stack([q_real, q_imag, u_real, u_imag], axis=1)


def spin_adjoint(fields):
    q_real = fields[:, 0]
    q_imag = fields[:, 1]
    u_real = fields[:, 2]
    u_imag = fields[:, 3]
    plus_part = jnp.stack([-q_real, -q_imag, -u_real, -u_imag], axis=1)
    minus_part = jnp.stack([u_imag, -u_real, -q_imag, q_real], axis=1)
    return jnp.stack([plus_part, minus_part], axis=2)


def phase_tables(modes_list, pixels, cycle_length, total_modes):
    turn_count = modes_list[:, None] * pixels % cycle_length
    angles = turn_count.astype(jnp.float32) * (2.0 * math.pi / cycle_length)
    weight = jnp.where(modes_list == 0, 1.0, 2.0).astype(jnp.float32) * (2.0 * total_modes) ** (
        -0.5
    )
    return (weight[:, None] * jnp.cos(angles), weight[:, None] * jnp.sin(angles))


def local(
    right_side,
    inv_spectra,
    beam,
    m_values,
    legendre,
    stencil_weights,
    stencil_base,
    inv_noise,
    slot_counts,
):
    harm_count = lax.axis_size("harm")
    band_count = lax.axis_size("band")
    local_modes = right_side.shape[0]
    total_modes = local_modes * harm_count
    cycle_rows = legendre.shape[3]
    lmax_len = right_side.shape[2]
    phi_len = NPHI // harm_count
    slots = stencil_weights.shape[4]
    alive_slots = (
        lax.broadcasted_iota(jnp.int32, slot_counts.shape + (slots,), 3)
        < slot_counts[:, :, :, None]
    )
    sent_weights = jnp.where(alive_slots[None], stencil_weights, 0.0)
    sent_noise = jnp.where(alive_slots[None], inv_noise, 0.0)
    got_weights, got_noise, got_base = (
        lax.all_to_all(sent_weights, "harm", split_axis=3, concat_axis=1, tiled=True),
        lax.all_to_all(sent_noise, "harm", split_axis=3, concat_axis=1, tiled=True),
        lax.all_to_all(stencil_base, "harm", split_axis=3, concat_axis=1, tiled=True),
    )
    coef_in = (right_side * beam[None, None, :]).astype(jnp.bfloat16)
    cycle_modes = jnp.einsum(
        "mcl,mtlr->mctr", coef_in, legendre, preferred_element_type=jnp.float32
    )
    fields = spin_fields(cycle_modes)
    pixels = lax.axis_index("harm") * phi_len + lax.broadcasted_iota(jnp.int32, (1, phi_len), 1)
    listed = jnp.zeros((total_modes,), jnp.int32)
    piece_fields = lax.all_gather(fields, "harm", axis=0, tiled=True)
    piece_modes = lax.all_gather(m_values, "harm", axis=0, tiled=True)
    cos_tab, sin_tab = phase_tables(piece_modes, pixels, NPHI, total_modes)
    phase_table = jnp.concatenate([cos_tab, -sin_tab], axis=0)
    stacked = jnp.concatenate([piece_fields[:, 0::2], piece_fields[:, 1::2]], axis=0)
    accum = jnp.einsum("mfr,mj->frj", stacked, phase_table, precision=lax.Precision.HIGHEST)
    listed = lax.dynamic_update_slice_in_dim(listed, piece_modes, jnp.int32(0), 0)
    sky_map = accum
    sky_map = sky_map.astype(jnp.bfloat16)
    phi_padded = extended(sky_map, (("harm", 2),), 2, True)
    padded = extended(phi_padded, (("band", 1),), 2, False)
    rows_pad = padded.shape[1]
    cols_pad = padded.shape[2]
    weights = got_weights.reshape(16, -1)
    noise_gain = got_noise.reshape(2, -1)
    tile_base = got_base.reshape(2, -1)
    point_count = weights.shape[1]
    block = math.gcd(point_count, 512)
    block_count = point_count // block
    offsets = jnp.arange(4, dtype=jnp.int32)
    row_iota = lax.broadcasted_iota(jnp.int32, (1, 1, rows_pad), 2)
    col_iota = lax.broadcasted_iota(jnp.int32, (1, 1, cols_pad), 2)

    def block_step(index, spread):
        start = index * block
        block_weights = lax.dynamic_slice_in_dim(weights, start, block, 1).reshape(4, 4, block)
        block_noise = lax.dynamic_slice_in_dim(noise_gain, start, block, 1)
        block_base = lax.dynamic_slice_in_dim(tile_base, start, block, 1)
        row_hit = (row_iota == block_base[0][None, :, None] + offsets[:, None, None]).astype(
            jnp.float32
        )
        col_hit = col_iota == block_base[1][None, :, None] + offsets[:, None, None]
        row_weight = jnp.sum(block_weights[:, :, :, None] * row_hit[:, None], axis=0)
        picked = jnp.einsum(
            "cpj,fij->fcpi",
            col_hit.astype(jnp.bfloat16),
            padded,
            preferred_element_type=jnp.float32,
        )
        sampled = jnp.sum(picked * row_weight[None], axis=(1, 3))
        weighted = block_noise * sampled
        row_terms = weighted[:, None, :, None] * row_weight[None]
        return spread + jnp.einsum(
            "cpj,fcpi->fij", col_hit.astype(jnp.float32), row_terms, precision=lax.Precision.HIGHEST
        )

    spread_grid = lax.fori_loop(
        0, block_count, block_step, jnp.zeros((2, rows_pad, cols_pad), jnp.float32)
    )
    from_below = shifted(spread_grid[:, -2:, :], "band", 1)
    from_above = shifted(spread_grid[:, :2, :], "band", -1)
    spread_grid = spread_grid[:, 2:-2, :]
    spread_grid = spread_grid.at[:, :2, :].add(from_below).at[:, -2:, :].add(from_above)
    from_left = from_behind(spread_grid[:, :, -2:], "harm", 1)
    from_right = from_behind(spread_grid[:, :, :2], "harm", -1)
    back_sky = spread_grid[:, :, 2:-2]
    back_sky = back_sky.at[:, :, :2].add(from_left).at[:, :, -2:].add(from_right)
    piece_modes = listed
    cos_tab, sin_tab = phase_tables(piece_modes, pixels, NPHI, total_modes)
    real_part = jnp.einsum("frj,mj->mfr", back_sky, cos_tab, precision=lax.Precision.HIGHEST)
    imag_part = -jnp.einsum("frj,mj->mfr", back_sky, sin_tab, precision=lax.Precision.HIGHEST)
    back_fields = lax.psum_scatter(
        jnp.stack([real_part, imag_part], axis=2).reshape(
            lax.axis_size("harm") * local_modes, 4, cycle_rows
        ),
        "harm",
        scatter_dimension=0,
        tiled=True,
    )
    back_modes = spin_adjoint(back_fields).astype(jnp.bfloat16)
    harmonic = jnp.einsum(
        "mctr,mtlr->mcl", back_modes, legendre, preferred_element_type=jnp.float32
    )
    spectra = jnp.repeat(inv_spectra, 2, axis=0)
    share_len = lmax_len // band_count
    offset = lax.axis_index("band") * share_len
    own_rhs = lax.dynamic_slice_in_dim(right_side, offset, share_len, 2)
    total_harm = lax.psum(harmonic, "band")
    image_vec = spectra[None] * right_side + beam[None, None, :] * total_harm
    norm_sq, curvature = lax.psum(
        (jnp.sum(right_side * right_side), jnp.sum(right_side * image_vec)), "harm"
    )
    own_image = lax.dynamic_slice_in_dim(image_vec, offset, share_len, 2)
    step_size = norm_sq / curvature
    return (step_size * own_rhs, own_rhs - step_size * own_image)


def solution(mesh):
    placed = (
        P("harm", None, None),
        P(),
        P(),
        P("harm"),
        P("harm", None, None, "band"),
        P(None, "harm", "band", None, None),
        P(None, "harm", "band", None, None),
        P(None, "harm", "band", None, None),
        P("harm", "band", None),
    )
    return jax.shard_map(
        local,
        mesh=mesh,
        in_specs=placed,
        out_specs=(P("harm", None, "band"), P("harm", None, "band")),
        check_vma=False,
    )
```

profile of v0, /device:TPU:2, one launch (start us, length us, event | category | flops | bytes accessed | tf_op | source)
XLA Modules:
  0.0 545.1 jit_solution(14736986392382285244)
XLA Ops:
  7.9 1.4 copy_select_fusion.1
  9.3 9.9 %all-to-all-start = ((f32[2,1,1,32,128]{4,0,2,1,3:T(2,128)}), f32[2,1,1,32,128]{4,0,2,1,3:T(2,128)S(1)}, u32[]{:S(2)}, u32[]{:S(2)}) async-start(f32[2,1,1,32,128]{4,0,2,1,3:T(2,128)} %copy_select_fusion.1), calls=%async_computation | async-start | bytes 65536 | tf_op jit(solution)/shard_map/all_to_all | solution.py:92
  19.2 3.4 fusion.46
  24.2 16.9 %all-reduce = s32[64]{0:T(128)S(1)} all-reduce(s32[64]{0:T(128)S(1)} %dynamic-update-slice.12), channel_id=1, replica_groups=mesh['harm'=32,'band'=8] {'harm'}, use_global_device_ids=true, to_apply=%add | all-reduce | flops 64 | bytes 512
  42.7 4.6 all-to-all-start.2
  47.4 36.1 %all_gather.7 = f32[64,4,128]{2,1,0:T(4,128)S(1)} all-gather(f32[2,4,128]{2,1,0:T(4,128)S(1)} %copy.96), channel_id=1, replica_groups=mesh['harm'=32,'band'=8] {'harm'}, dimensions={0}, use_global_device_ids=true | all-gather | bytes 135168 | tf_op jit(solution)/shard_map/all_gather | solution.py:102
  85.8 3.5 collective-permute-start.1
  89.3 1.9 collective-permute-done
  91.4 3.4 collective-permute-start.2
  94.8 2.4 collective-permute-start.3
  97.9 5.0 all-to-all-start.1
  103.6 7.8 %all-to-all-done.1 = s32[2,1,1,32,128]{4,0,2,1,3:T(2,128)S(1)} async-done(((s32[2,1,1,32,128]{4,0,2,1,3:T(2,128)}), s32[2,1,1,32,128]{4,0,2,1,3:T(2,128)S(1)}, u32[]{:S(2)}, u32[]{:S(2)}) %all-to-all-start.1) | async-done | bytes 32800 | tf_op jit(solution)/shard_map/all_to_all | solution.py:93
  111.4 53.3 %while.19 = (s32[]{:T(128)}, f32[2,132,644]{2,1,0:T(8,128)S(1)}, f32[2,4096]{1,0:T(2,128)S(1)}, s32[2,4096]{1,0:T(2,128)S(1)}, bf16[2,132,644]{2,1,0:T(8,128)(2,...) while((s32[]{:T(128)}, f32[2,132,644]{2,1,0:T(8,128)S(1)}, ...), condition=%wide.region_5.6_spmd.clone.clone, body=%wide.region_2.5_spmd.clone.clone.sunk | while | flops 4881735680 | bytes 9507329 | solution.py:148
  111.7 1.1 multiply_reduce_fusion.6
  113.1 1.3 multiply_reduce_fusion.7
  114.5 3.6 fusion.93
  118.4 1.1 multiply_reduce_fusion.6
  119.8 1.3 multiply_reduce_fusion.7
  121.2 3.6 fusion.93
  125.0 1.1 multiply_reduce_fusion.6
  126.5 1.3 multiply_reduce_fusion.7
  127.8 3.6 fusion.93
  131.7 1.1 multiply_reduce_fusion.6
  133.1 1.3 multiply_reduce_fusion.7
  134.5 3.6 fusion.93
  139.8 1.3 multiply_reduce_fusion.7
  141.1 3.6 fusion.93
  145.0 1.1 multiply_reduce_fusion.6
  146.4 1.3 multiply_reduce_fusion.7
  147.8 3.6 fusion.93
  151.7 1.1 multiply_reduce_fusion.6
  153.1 1.3 multiply_reduce_fusion.7
  154.5 3.6 fusion.93
  158.3 1.1 multiply_reduce_fusion.6
  159.8 1.3 multiply_reduce_fusion.7
  161.1 3.6 fusion.93
  164.8 3.4 collective-permute-start.4
  168.2 2.4 collective-permute-start.5
  170.7 3.1 collective-permute-done.5
  174.3 4.1 collective-permute-start.7
  178.4 2.1 collective-permute-done.6
  182.3 1.3 convolution_bitcast_fusion.1
  183.6 1.3 fusion.31
  186.4 203.6 %all-reduce.8.cloned.1.call-done = f32[64,4,128]{2,1,0:T(4,128)} async-done(((f32[64,4,128]{2,1,0:T(4,128)}), f32[64,4,128]{2,1,0:T(4,128)}) %all-reduce.8.cloned.1.call-update) | async-done | bytes 131088
  391.7 4.7 convolution_bitcast_fusion
  396.5 84.6 %all-reduce.6.cloned.1.call-done = f32[2,4,5120]{2,1,0:T(4,128)} async-done(((f32[2,4,5120]{2,1,0:T(4,128)}), f32[2,4,5120]{2,1,0:T(4,128)}) %all-reduce.6.cloned.1.call-update) | async-done | bytes 163856 | tf_op jit(solution)/shard_map/psum | solution.py:179
  481.1 1.6 multiply_reduce_fusion.2
  482.7 53.6 %all-reduce.2 = (f32[]{:T(128)}, f32[]{:T(128)}) all-reduce(f32[]{:T(128)} %get-tuple-element.258, f32[]{:T(128)} %get-tuple-element.257), channel_id=1, replica_groups=mesh['harm'=32,'band'=8] {'harm'}, use_global_device_ids=true, to_apply=%region_1.2 | all-reduce | flops 2 | bytes 16 | tf_op jit(solution)/shard_map/psum | solution.py:181
  (136 shorter events, 18.4 us)
Async XLA Ops:
  9.3 33.4 %all-to-all-start = ((f32[2,1,1,32,128]{4,0,2,1,3:T(2,128)}), f32[2,1,1,32,128]{4,0,2,1,3:T(2,128)S(1)}, u32[]{:S(2)}, u32[]{:S(2)}) async-start(f32[2,1,1,32,128]{4,0,2,1,3:T(2,128)} %copy_select_fusion.1), calls=%async_computation | async-start | bytes 65536 | tf_op jit(solution)/shard_map/all_to_all | solution.py:92
  19.2 3.5 copy-start.5
  19.2 4.7 copy-start.6
  19.2 21.9 %copy-start.1 = (f32[16,1,1,32,128]{4,3,2,1,0:T(8,128)S(1)}, f32[16,1,1,32,128]{4,3,2,1,0:T(8,128)}, u32[]{:S(2)}) copy-start(f32[16,1,1,32,128]{4,3,2,1,0:T(8,128)} %param.24) | copy-start | bytes 786436
  22.6 74.6 %copy-start.4 = (s32[2,1,1,32,128]{4,3,2,1,0:T(8,128)S(1)}, s32[2,1,1,32,128]{4,3,2,1,0:T(8,128)}, u32[]{:S(2)}) copy-start(s32[2,1,1,32,128]{4,3,2,1,0:T(8,128)} %param.25) | copy-start | bytes 98308
  42.7 55.1 %all-to-all-start.2 = ((f32[16,1,1,32,128]{4,0,2,1,3:T(8,128)}), f32[16,1,1,32,128]{4,0,2,1,3:T(8,128)S(1)}, u32[]{:S(2)}, u32[]{:S(2)}) async-start(f32[16,1,1,32,128]{4,0,2,1,3:T(8,128)} %copy_select_fusion), calls=%async_computation.2 | async-start | bytes 524288 | tf_op jit(solution)/shard_map/all_to_all | solution.py:91
  85.4 5.9 %collective-permute-start = (bf16[2,128,2]{2,1,0:T(8,128)(2,1)S(1)}, bf16[2,128,2]{2,1,0:T(8,128)(2,1)S(1)}, u32[]{:S(2)}, u32[]{:S(2)}) collective-permute-start(bf16[2,128,2]{2,1,0:T(8,128)(2,1)S(1)} %get-tuple-element.282), channel_id=1, source_target_pairs={{0,8},{8,16},{16,24},{24,32},{32,40},{40,48},{48,56},{56,64},{64,7... | collective-permute-start | bytes 3080 | tf_op jit(solution)/shard_map/ppermute | solution.py:18
  85.8 5.5 %collective-permute-start.1 = (bf16[2,128,2]{2,1,0:T(8,128)(2,1)S(1)}, bf16[2,128,2]{2,1,0:T(8,128)(2,1)S(1)}, u32[]{:S(2)}, u32[]{:S(2)}) collective-permute-start(bf16[2,128,2]{2,1,0:T(8,128)(2,1)S(1)} %get-tuple-element.283), channel_id=1, source_target_pairs={{8,0},{16,8},{24,16},{32,24},{40,32},{48,40},{56,48},{64,56},{72,6... | collective-permute-start | bytes 3080 | tf_op jit(solution)/shard_map/ppermute | solution.py:21
  91.4 11.7 %collective-permute-start.2 = (bf16[2,2,644]{2,1,0:T(2,128)(2,1)S(1)}, bf16[2,2,644]{2,1,0:T(2,128)(2,1)S(1)}, u32[]{:S(2)}, u32[]{:S(2)}) collective-permute-start(bf16[2,2,644]{2,1,0:T(2,128)(2,1)S(1)} %get-tuple-element.280), channel_id=1, source_target_pairs={{0,1},{1,2},{2,3},{3,4},{4,5},{5,6},{6,7},{8,9},{9,10},{10,11},{11... | collective-permute-start | bytes 15464 | tf_op jit(solution)/shard_map/ppermute | solution.py:18
  94.8 8.3 %collective-permute-start.3 = (bf16[2,2,644]{2,1,0:T(2,128)(2,1)S(1)}, bf16[2,2,644]{2,1,0:T(2,128)(2,1)S(1)}, u32[]{:S(2)}, u32[]{:S(2)}) collective-permute-start(bf16[2,2,644]{2,1,0:T(2,128)(2,1)S(1)} %get-tuple-element.281), channel_id=1, source_target_pairs={{1,0},{2,1},{3,2},{4,3},{5,4},{6,5},{7,6},{9,8},{10,9},{11,10},{12... | collective-permute-start | bytes 15464 | tf_op jit(solution)/shard_map/ppermute | solution.py:21
  97.9 13.6 %all-to-all-start.1 = ((s32[2,1,1,32,128]{4,0,2,1,3:T(2,128)}), s32[2,1,1,32,128]{4,0,2,1,3:T(2,128)S(1)}, u32[]{:S(2)}, u32[]{:S(2)}) async-start(s32[2,1,1,32,128]{4,0,2,1,3:T(2,128)} %copy.89), calls=%async_computation.1 | async-start | bytes 65536 | tf_op jit(solution)/shard_map/all_to_all | solution.py:93
  102.8 287.2 %all-reduce.8.cloned.1.call-start = ((), (), s32[]{:S(2)}) async-start(), calls=%async_computation.4 | async-start | bytes 262144
  164.8 5.9 %collective-permute-start.4 = (f32[2,2,644]{2,1,0:T(2,128)S(1)}, f32[2,2,644]{2,1,0:T(2,128)S(1)}, u32[]{:S(2)}, u32[]{:S(2)}) collective-permute-start(f32[2,2,644]{2,1,0:T(2,128)S(1)} %get-tuple-element.277), channel_id=1, source_target_pairs={{0,1},{1,2},{2,3},{3,4},{4,5},{5,6},{6,7},{8,9},{9,10},{10,11},{11... | collective-permute-start | bytes 30920 | tf_op jit(solution)/shard_map/ppermute | solution.py:29
  168.2 5.6 %collective-permute-start.5 = (f32[2,2,644]{2,1,0:T(2,128)S(1)}, f32[2,2,644]{2,1,0:T(2,128)S(1)}, u32[]{:S(2)}, u32[]{:S(2)}) collective-permute-start(f32[2,2,644]{2,1,0:T(2,128)S(1)} %get-tuple-element.276), channel_id=1, source_target_pairs={{1,0},{2,1},{3,2},{4,3},{5,4},{6,5},{7,6},{9,8},{10,9},{11,10},{12... | collective-permute-start | bytes 30920 | tf_op jit(solution)/shard_map/ppermute | solution.py:29
  173.9 6.6 %collective-permute-start.6 = (f32[2,128,2]{2,1,0:T(8,128)S(1)}, f32[2,128,2]{2,1,0:T(8,128)S(1)}, u32[]{:S(2)}, u32[]{:S(2)}) collective-permute-start(f32[2,128,2]{2,1,0:T(8,128)S(1)} %get-tuple-element.279), channel_id=1, source_target_pairs={{248,0},{0,8},{8,16},{16,24},{24,32},{32,40},{40,48},{48,56},{56,6... | collective-permute-start | bytes 6152 | tf_op jit(solution)/shard_map/ppermute | solution.py:35
  174.3 7.0 %collective-permute-start.7 = (f32[2,128,2]{2,1,0:T(8,128)S(1)}, f32[2,128,2]{2,1,0:T(8,128)S(1)}, u32[]{:S(2)}, u32[]{:S(2)}) collective-permute-start(f32[2,128,2]{2,1,0:T(8,128)S(1)} %get-tuple-element.278), channel_id=1, source_target_pairs={{8,0},{16,8},{24,16},{32,24},{40,32},{48,40},{56,48},{64,56},{72,6... | collective-permute-start | bytes 6152 | tf_op jit(solution)/shard_map/ppermute | solution.py:35
  185.7 295.3 %all-reduce.6.cloned.1.call-start = ((), (), s32[]{:S(2)}) async-start(), calls=%async_computation.3 | async-start | bytes 327680 | tf_op jit(solution)/shard_map/psum | solution.py:179
  391.7 4.7 copy-start.3
  391.7 89.4 %copy-start = (f32[2,4,5120]{2,1,0:T(4,128)S(1)}, f32[2,4,5120]{2,1,0:T(4,128)}, u32[]{:S(2)}) copy-start(f32[2,4,5120]{2,1,0:T(4,128)} %param.19) | copy-start | bytes 491524
  391.7 89.4 %copy-start.2 = (f32[5120]{0:T(1024)S(1)}, f32[5120]{0:T(1024)}, u32[]{:S(2)}) copy-start(f32[5120]{0:T(1024)} %param.21) | copy-start | bytes 61444
Sparse Core Ops, SparseCore 0:
  185.9 204.1 all-reduce.7
  396.5 84.5 all-reduce.5
where the time goes:
time: 547 us; the launch traced here: 545 us
  waiting for transfers between devices  303 us (55%)
  blocking collectives  107 us (20%)
  matrix products  50.9 us (9%)
  starting transfers between devices  39.5 us (7%)
  other arithmetic  17.2 us (3%)
  between operations  17.1 us (3%)
  local copies, waits for them, and re-layouts  10.1 us (2%)
    unnamed x3, waiting for transfers between devices  204 us
    psum x1, waiting for transfers between devices, local(): total_harm = lax.psum(harmonic, 'band')  84.6 us
    psum x1, blocking collectives, local(): lax.psum((jnp.sum(right_side * right_side), jnp.sum(right_side * image_ve...  53.6 us
    all_gather x1, blocking collectives, local(): piece_fields = lax.all_gather(fields, 'harm', axis=0, tiled=True)  36.1 us
    dot_general x8, matrix products, block_step(): jnp.einsum('cpj,fcpi->fij', col_hit.astype(jnp.float32), row_terms, preci...  28.6 us
    unnamed x1, blocking collectives  16.9 us
  transfers between devices with their start and end apart: 13, of which 6 were waited for; matrix products, arithmetic and copies ran while one was open for 2% of the time, Pallas kernels for 0%

commit v1 on v0

v1 whole, which is shorter than its diff:
```python
import functools
import math

import jax
import jax.numpy as jnp
from jax import lax
from jax.experimental import pallas as pl
from jax.experimental.pallas import tpu as pltpu
from jax.sharding import PartitionSpec as P

NPHI = 20480
ROWS = 144
LANES = 256
BLOCK = 256
F32 = jnp.float32
BF16 = jnp.bfloat16


def split3(value):
    first = value.astype(BF16).astype(F32)
    rest = value - first
    second = rest.astype(BF16).astype(F32)
    third = (rest - second).astype(BF16).astype(F32)
    return first, second, third


def trig_tables(modes):
    lane = lax.broadcasted_iota(jnp.int32, (64, 128), 1)
    digit = lane & 31
    steps = jnp.where(
        lane < 32, digit * 1024, jnp.where(lane < 64, digit * 32, jnp.where(lane < 96, digit, lane & 3))
    )
    product = modes * steps
    high = product >> 12
    turn = (high - 5 * ((high * 52429) >> 18)) * 4096 + (product & 4095)
    quarter = jnp.zeros_like(turn)
    for edge in (2560, 7680, 12800, 17920):
        quarter = quarter + (turn >= edge).astype(jnp.int32)
    angle = (turn - 5120 * quarter).astype(F32) * (2.0 * math.pi / NPHI)
    quarter = quarter & 3
    sq = angle * angle
    sine = angle * (1.0 + sq * (-1.0 / 6 + sq * (1.0 / 120 + sq * (-1.0 / 5040 + sq * (1.0 / 362880)))))
    cosine = 1.0 + sq * (
        -0.5 + sq * (1.0 / 24 + sq * (-1.0 / 720 + sq * (1.0 / 40320 - sq * (1.0 / 3628800))))
    )
    cos_out = jnp.where(
        quarter == 0, cosine, jnp.where(quarter == 1, -sine, jnp.where(quarter == 2, -cosine, sine))
    )
    sin_out = jnp.where(
        quarter == 0, sine, jnp.where(quarter == 1, cosine, jnp.where(quarter == 2, -sine, -cosine))
    )
    return cos_out, sin_out


def points_kernel(blocks_ref, sums_ref, x_ref, data_ref, out_ref, table_ref, field_ref, acc_ref, curv_ref):
    row_id = lax.broadcasted_iota(jnp.int32, (256, 256), 0)
    col_id = lax.broadcasted_iota(jnp.int32, (256, 256), 1)
    to_mode_last = (col_id == 4 * (row_id & 63) + (row_id >> 6)).astype(F32).astype(BF16)
    to_mode_first = (row_id == 4 * (col_id & 63) + (col_id >> 6)).astype(F32).astype(BF16)
    fields = jnp.dot(to_mode_last, x_ref[...], preferred_element_type=F32)
    field_ref[...] = fields.astype(BF16)
    head = fields[:64]
    head_lane = lax.broadcasted_iota(jnp.int32, (64, LANES), 1)
    mode_value = jnp.sum(
        jnp.where(head_lane == 132, head * 64.0, jnp.where(head_lane == 133, head, 0.0)),
        axis=1,
        keepdims=True,
    )
    modes = jnp.broadcast_to(mode_value, (64, 128)).astype(jnp.int32)
    cos_tab, sin_tab = trig_tables(modes)
    weight = jnp.where(modes == 0, 1.0, 2.0).astype(F32) * 128.0**-0.5
    lane = lax.broadcasted_iota(jnp.int32, (64, 128), 1)
    groups = [
        (lane < 32, weight),
        ((lane >= 32) & (lane < 64), None),
        ((lane >= 64) & (lane < 96), None),
    ]
    for a in range(4):
        groups.append(((lane >= 96) & (((lane - 96) & 15) >> 2 == a), None))
    for index, (mask, gain) in enumerate(groups):
        for part, table in enumerate((cos_tab, sin_tab)):
            value = table if gain is None else table * gain
            value = jnp.where(mask, value, 0.0)
            rounded = value.astype(BF16)
            start = (2 * index + part) * 64
            table_ref[pl.ds(start, 64), 0:128] = rounded
            table_ref[pl.ds(start, 64), 128:256] = (value - rounded.astype(F32)).astype(BF16)
    acc_ref[...] = jnp.zeros_like(acc_ref)
    curv_ref[...] = jnp.zeros_like(curv_ref)

    def block_step(index, carry):
        data = data_ref[:, pl.ds(pl.multiple_of(index * BLOCK, BLOCK), BLOCK)]
        pixel = data[17:18].astype(jnp.int32)
        first_row = data[16:17].astype(jnp.int32)
        digit_id = lax.broadcasted_iota(jnp.int32, (96, BLOCK), 0)
        hit = (
            (digit_id == (pixel >> 10))
            | (digit_id == ((pixel >> 5) & 31) + 32)
            | (digit_id == (pixel & 31) + 64)
        )
        weights = data[0:16]
        weights_high = weights.astype(BF16)
        weights_low = (weights - weights_high.astype(F32)).astype(BF16)
        chosen = jnp.concatenate([hit.astype(F32).astype(BF16), weights_high, weights_low], axis=0)
        phases = jnp.dot(
            table_ref[...], jnp.concatenate([chosen, chosen], axis=0), preferred_element_type=F32
        )
        part = [phases[64 * i : 64 * (i + 1)] for i in range(14)]
        mid_re = part[0] * part[2] - part[1] * part[3]
        mid_im = part[0] * part[3] + part[1] * part[2]
        turn_re = mid_re * part[4] - mid_im * part[5]
        turn_im = mid_re * part[5] + mid_im * part[4]
        grid_row = lax.broadcasted_iota(jnp.int32, (ROWS, BLOCK), 0)
        total = [jnp.zeros((64, BLOCK), F32), jnp.zeros((64, BLOCK), F32)]
        hits = []
        waves = []
        for a in range(4):
            wave_re = turn_re * part[6 + 2 * a] - turn_im * part[7 + 2 * a]
            wave_im = turn_re * part[7 + 2 * a] + turn_im * part[6 + 2 * a]
            row_hit = (grid_row == first_row + a).astype(F32).astype(BF16)
            picked = jnp.dot(field_ref[:, 0:ROWS], row_hit, preferred_element_type=F32)
            for f in range(2):
                total[f] = (
                    total[f]
                    + picked[128 * f : 128 * f + 64] * wave_re
                    - picked[128 * f + 64 : 128 * f + 128] * wave_im
                )
            hits.append(row_hit)
            waves.append((wave_re, wave_im))
        weighted = []
        for f in range(2):
            sampled = jnp.sum(total[f], axis=0, keepdims=True)
            value = data[18 + f : 19 + f] * sampled
            curv_ref[f : f + 1, :] += value * sampled
            weighted.append(value)
        update = jnp.zeros((256, ROWS), F32)
        for a in range(4):
            wave_re, wave_im = waves[a]
            terms = jnp.concatenate(
                [
                    weighted[0] * wave_re,
                    -(weighted[0] * wave_im),
                    weighted[1] * wave_re,
                    -(weighted[1] * wave_im),
                ],
                axis=0,
            ).astype(BF16)
            update = update + lax.dot_general(
                terms, hits[a], (((1,), (1,)), ((), ())), preferred_element_type=F32
            )
        acc_ref[:, 0:ROWS] += update
        return carry

    lax.fori_loop(0, blocks_ref[0], block_step, 0)
    back = jnp.dot(to_mode_first, acc_ref[...].astype(BF16), preferred_element_type=F32)
    curvature = jnp.sum(curv_ref[...], axis=(0, 1), keepdims=True) + sums_ref[1]
    norm = jnp.zeros((1, 1), F32) + sums_ref[0]
    for offset, piece in enumerate(split3(curvature) + split3(norm)):
        back = jnp.where(col_id == 132 + offset, piece, back)
    out_ref[...] = back.astype(BF16)


def analysis_kernel(got_ref, legendre_ref, edge_ref, out_ref, own_ref, rim_ref, sums_ref):
    @pl.when(pl.program_id(0) == 0)
    def _():
        total = got_ref[0].astype(F32)
        for source in range(1, 32):
            total = total + got_ref[source].astype(F32)
        lane = lax.broadcasted_iota(jnp.int32, (8, 128), 1)
        row = lax.broadcasted_iota(jnp.int32, (8, 128), 0)
        low, high = total[:, 0:128], total[:, 128:256]
        curvature = jnp.sum(jnp.where((lane >= 4) & (lane < 7), high, 0.0), axis=1, keepdims=True)
        norm = jnp.sum(jnp.where((lane >= 7) & (lane < 10), high, 0.0), axis=1, keepdims=True)
        sums_ref[...] = jnp.where(lane == 0, curvature, jnp.where(lane == 1, norm, 0.0))
        own = pltpu.roll(total, 254, 1)[:, 0:128]
        rim = jnp.where(lane < 2, low, jnp.where(lane < 4, high, 0.0))
        for ref, value in ((own_ref, own), (rim_ref, rim)):
            plus = -value
            minus = jnp.concatenate(
                [
                    value[3:4],
                    -value[2:3],
                    -value[1:2],
                    value[0:1],
                    value[7:8],
                    -value[6:7],
                    -value[5:6],
                    value[4:5],
                ],
                axis=0,
            )
            for m in range(2):
                keep = (row >> 2) == m
                ref[2 * m] = jnp.where(keep, plus, 0.0).astype(BF16)
                ref[2 * m + 1] = jnp.where(keep, minus, 0.0).astype(BF16)

    chunk = legendre_ref.shape[2]
    result = jnp.zeros((8, chunk), F32)
    for m in range(2):
        for t in range(2):
            result = result + lax.dot_general(
                own_ref[2 * m + t],
                legendre_ref[m, t],
                (((1,), (1,)), ((), ())),
                preferred_element_type=F32,
            )
            result = result + jnp.dot(
                rim_ref[2 * m + t][:, 0:16], edge_ref[m, t], preferred_element_type=F32
            )
    out_ref[0, :, 0:chunk] = result
    out_ref[0, :, chunk : chunk + 128] = sums_ref[...]


def spin_fields(cycle_modes):
    q_real = -(cycle_modes[:, 0, 0] - cycle_modes[:, 3, 1])
    q_imag = -(cycle_modes[:, 1, 0] + cycle_modes[:, 2, 1])
    u_real = -(cycle_modes[:, 2, 0] + cycle_modes[:, 1, 1])
    u_imag = -(cycle_modes[:, 3, 0] - cycle_modes[:, 0, 1])
    return jnp.stack([q_real, q_imag, u_real, u_imag], axis=1)


def local(
    right_side,
    inv_spectra,
    beam,
    m_values,
    legendre,
    stencil_weights,
    stencil_base,
    inv_noise,
    slot_counts,
):
    band_count = lax.axis_size("band")
    lmax_len = right_side.shape[2]
    share_len = lmax_len // band_count

    pick_row = lax.broadcasted_iota(jnp.int32, (4, 128), 0)
    pick_col = lax.broadcasted_iota(jnp.int32, (4, 128), 1)
    pick = (pick_col == jnp.where(pick_row < 2, pick_row, pick_row + 124)).astype(BF16)
    edges = jnp.einsum("kr,mtlr->mtkl", pick, legendre, preferred_element_type=F32).astype(BF16)
    up = [(i, i + 1) for i in range(band_count - 1)]
    down = [(i + 1, i) for i in range(band_count - 1)]
    low_rim = lax.ppermute(edges[:, :, 2:4], "band", up)
    high_rim = lax.ppermute(edges[:, :, 0:2], "band", down)
    rim = jnp.concatenate([low_rim, high_rim], axis=2)

    coef_in = (right_side * beam[None, None, :]).astype(BF16)
    own_modes = jnp.einsum("mcl,mtlr->mctr", coef_in, legendre, preferred_element_type=F32)
    rim_modes = jnp.einsum("mcl,mtkl->mctk", coef_in, rim, preferred_element_type=F32)
    cycle_modes = jnp.concatenate([rim_modes[..., 0:2], own_modes, rim_modes[..., 2:4]], axis=3)
    fields = spin_fields(cycle_modes)
    mode_parts = jnp.stack([m_values >> 6, m_values & 63], axis=1).astype(F32)
    mode_parts = jnp.broadcast_to(mode_parts[:, None, :], (2, 4, 2))
    sent = jnp.concatenate([fields, mode_parts, jnp.zeros((2, 4, LANES - 134), F32)], axis=2)
    sent = sent.astype(BF16).reshape(1, 8, LANES)
    got = lax.all_to_all(
        jnp.broadcast_to(sent, (32, 8, LANES)), "harm", split_axis=0, concat_axis=0, tiled=True
    )

    slots = stencil_weights.shape[4]
    alive = lax.broadcasted_iota(jnp.int32, (32, slots), 1) < slot_counts.reshape(32, 1)
    weights = jnp.where(alive[None], stencil_weights.reshape(16, 32, slots), 0.0)
    noise = jnp.where(alive[None], inv_noise.reshape(2, 32, slots), 0.0)
    base = stencil_base.reshape(2, 32, slots)
    owner = lax.broadcasted_iota(jnp.int32, (32, slots), 0)
    pixel = owner * 640 + base[1] - 2
    pixel = jnp.where(pixel < 0, pixel + NPHI, jnp.where(pixel >= NPHI, pixel - NPHI, pixel))
    data = jnp.concatenate(
        [
            weights,
            base[0:1].astype(F32),
            pixel[None].astype(F32),
            noise,
            jnp.zeros((4, 32, slots), F32),
        ],
        axis=0,
    ).reshape(24, 32 * slots)

    spectra = jnp.repeat(inv_spectra, 2, axis=0)
    norm_part = jnp.sum(right_side * right_side)
    prior_part = jnp.sum(spectra[None] * right_side * right_side)
    sums = jnp.stack([norm_part, prior_part]) / band_count
    blocks = jnp.full((1,), 32 * slots // BLOCK, jnp.int32)
    back = pl.pallas_call(
        points_kernel,
        out_shape=jax.ShapeDtypeStruct((256, LANES), BF16),
        in_specs=[
            pl.BlockSpec(memory_space=pltpu.SMEM),
            pl.BlockSpec(memory_space=pltpu.SMEM),
            pl.BlockSpec(memory_space=pltpu.VMEM),
            pl.BlockSpec(memory_space=pltpu.VMEM),
        ],
        out_specs=pl.BlockSpec(memory_space=pltpu.VMEM),
        scratch_shapes=[
            pltpu.VMEM((896, 256), BF16),
            pltpu.VMEM((256, LANES), BF16),
            pltpu.VMEM((256, LANES), F32),
            pltpu.VMEM((2, BLOCK), F32),
        ],
        compiler_params=pltpu.CompilerParams(vmem_limit_bytes=32 * 1024 * 1024),
        name="points",
    )(blocks, sums, got.reshape(256, LANES), data)

    back_got = lax.all_to_all(
        back.reshape(32, 8, LANES), "harm", split_axis=0, concat_axis=0, tiled=True
    )
    rim_rows = jnp.concatenate([rim, jnp.zeros((2, 2, 12, lmax_len), BF16)], axis=2)
    harmonic = pl.pallas_call(
        analysis_kernel,
        grid=(band_count,),
        out_shape=jax.ShapeDtypeStruct((band_count, 8, share_len + 128), F32),
        in_specs=[
            pl.BlockSpec((32, 8, LANES), lambda i: (0, 0, 0)),
            pl.BlockSpec((2, 2, share_len, 128), lambda i: (0, 0, i, 0)),
            pl.BlockSpec((2, 2, 16, share_len), lambda i: (0, 0, 0, i)),
        ],
        out_specs=pl.BlockSpec((1, 8, share_len + 128), lambda i: (i, 0, 0)),
        scratch_shapes=[
            pltpu.VMEM((4, 8, 128), BF16),
            pltpu.VMEM((4, 8, 128), BF16),
            pltpu.VMEM((8, 128), F32),
        ],
        compiler_params=pltpu.CompilerParams(vmem_limit_bytes=32 * 1024 * 1024),
        name="analysis",
    )(back_got, legendre, rim_rows)

    parts = lax.all_to_all(harmonic, "band", split_axis=0, concat_axis=0, tiled=True)
    total = jnp.sum(parts, axis=0)
    step_size = total[0, share_len + 1] / total[0, share_len]
    offset = lax.axis_index("band") * share_len
    own_rhs = lax.dynamic_slice_in_dim(right_side, offset, share_len, 2)
    own_spectra = lax.dynamic_slice_in_dim(spectra, offset, share_len, 1)
    own_beam = lax.dynamic_slice_in_dim(beam, offset, share_len, 0)
    own_image = own_spectra[None] * own_rhs + own_beam[None, None] * total[:, 0:share_len].reshape(
        2, 4, share_len
    )
    return (step_size * own_rhs, own_rhs - step_size * own_image)


def solution(mesh):
    placed = (
        P("harm", None, None),
        P(),
        P(),
        P("harm"),
        P("harm", None, None, "band"),
        P(None, "harm", "band", None, None),
        P(None, "harm", "band", None, None),
        P(None, "harm", "band", None, None),
        P("harm", "band", None),
    )
    return jax.shard_map(
        local,
        mesh=mesh,
        in_specs=placed,
        out_specs=(P("harm", None, "band"), P("harm", None, "band")),
        check_vma=False,
    )
```

time: 547 us -> 94.6 us (0.17)
  waiting for transfers between devices: 303 us -> 25.3 us
  blocking collectives: 107 us -> 0 us
  matrix products: 50.9 us -> 7.6 us
  Pallas kernels: 0 us -> 22.1 us
  between operations: 17.1 us -> 2.3 us
  other arithmetic: 17.2 us -> 3.48 us
  starting transfers between devices: 39.5 us -> 28.4 us
    unnamed x3 -> x0, waiting for transfers between devices: 204 us -> none
    psum x1 -> x0, waiting for transfers between devices: 84.6 us -> none  [local(): total_harm = lax.psum(harmonic, 'band')]
    psum x1 -> x0, blocking collectives: 53.6 us -> none  [local(): lax.psum((jnp.sum(right_side * right_side), jnp.sum(right_side * image_ve...]
    dot_general x21 -> x3, matrix products: 50.9 us -> 7.6 us  [the longest x1 4.05 us: local(): jnp.einsum('kr,mtlr->mtkl', pick, legendre, preferred_element_type=F32)]
    all_gather x1 -> x0, blocking collectives: 36.1 us -> none  [local(): piece_fields = lax.all_gather(fields, 'harm', axis=0, tiled=True)]
    pallas_call x0 -> x2, Pallas kernels: none -> 22.1 us  [the longest x1 17.4 us: local(): pl.pallas_call(points_kernel, out_shape=jax.ShapeDtypeStruct((256, LANES)...]
    all_to_all x3, waiting for transfers between devices: 7.79 us -> 25.3 us  [the longest x1 10.2 us: local(): lax.all_to_all(back.reshape(32, 8, LANES), 'harm', split_axis=0, concat_a...]
    unnamed x1 -> x0, blocking collectives: 16.9 us -> none
  transfers between devices with their start and end apart: 13 -> 5, of which waited for: 6 -> 3; matrix products, arithmetic and copies ran while one was open for 2% -> 7% of each run, Pallas kernels for 0% -> 0%
where the time goes in v1:
time: 94.6 us; the launch traced here: 94.1 us
  starting transfers between devices  28.4 us (30%)
  waiting for transfers between devices  25.3 us (27%)
  Pallas kernels  22.1 us (23%)
  matrix products  7.6 us (8%)
  local copies, waits for them, and re-layouts  4.93 us (5%)
  other arithmetic  3.48 us (4%)
  between operations  2.3 us (2%)
    pallas_call x1, Pallas kernels, local(): pl.pallas_call(points_kernel, out_shape=jax.ShapeDtypeStruct((256, LANES)...  17.4 us
    all_to_all x1, waiting for transfers between devices, local(): lax.all_to_all(back.reshape(32, 8, LANES), 'harm', split_axis=0, concat_a...  10.2 us
    all_to_all x1, starting transfers between devices, local(): lax.all_to_all(jnp.broadcast_to(sent, (32, 8, LANES)), 'harm', split_axis...  9.87 us
    all_to_all x1, starting transfers between devices, local(): lax.all_to_all(harmonic, 'band', split_axis=0, concat_axis=0, tiled=True)  8.85 us
    all_to_all x1, waiting for transfers between devices, local(): lax.all_to_all(jnp.broadcast_to(sent, (32, 8, LANES)), 'harm', split_axis...  7.9 us
    all_to_all x1, waiting for transfers between devices, local(): lax.all_to_all(harmonic, 'band', split_axis=0, concat_axis=0, tiled=True)  7.19 us
    pallas_call x1, Pallas kernels, local(): pl.pallas_call(analysis_kernel, grid=(band_count,), out_shape=jax.ShapeDt...  4.64 us
    dot_general x1, matrix products, local(): jnp.einsum('kr,mtlr->mtkl', pick, legendre, preferred_element_type=F32)  4.05 us
  transfers between devices with their start and end apart: 5, of which 3 were waited for; matrix products, arithmetic and copies ran while one was open for 7% of the time, Pallas kernels for 0%

profile of v1, /device:TPU:2, one launch (start us, length us, event | category | flops | bytes accessed | tf_op | source)
XLA Modules:
  0.0 94.1 jit_solution(11285484462634636432)
XLA Ops:
  0.6 0.0 copy-start.8
  0.6 0.0 copy-start.7
  0.7 0.0 copy-start.5
  0.7 0.0 copy-start.2
  0.7 0.0 copy-start.6
  0.7 0.0 copy-start.3
  0.7 0.0 copy-start.1
  0.7 4.0 %fusion = bf16[2,2,4,5120]{3,2,1,0:T(4,128)(2,1)S(1)} fusion(bf16[2,2,5120,128]{3,2,1,0:T(8,128)(2,1)} %legendre_ref.1, s32[4]{0:T(128)S(1)} %iota_add_fusion, pred[4]{0:T(512)(128)(4,1)S(1)} %iota_compare_fusion), kind=kOutput, calls=%fused_computation.1 | convolution fusion | flops 21054464 | bytes 5406740 | tf_op jit(solution)/shard_map/kr,mtlr->mtkl/dot_general | solution.py:240
  4.8 0.1 fusion.22
  4.9 3.4 %collective-permute-start = (bf16[2,2,2,5120]{3,2,1,0:T(2,128)(2,1)S(1)}, bf16[2,2,2,5120]{3,2,1,0:T(2,128)(2,1)S(1)}, u32[]{:S(2)}, u32[]{:S(2)}) collective-permute-start(bf16[2,2,2,5120]{3,2,1,0:T(2,128)(2,1)S(1)} %get-tuple-element.6), channel_id=1, source_target_pairs={{0,1},{1,2},{2,3},{3,4},{4,5},{5,6},{6,7},{8,9},{9,10},{10,11},{11... | collective-permute-start | bytes 245768 | tf_op jit(solution)/shard_map/ppermute | solution.py:243
  8.3 2.4 %collective-permute-start.1 = (bf16[2,2,2,5120]{3,2,1,0:T(2,128)(2,1)S(1)}, bf16[2,2,2,5120]{3,2,1,0:T(2,128)(2,1)S(1)}, u32[]{:S(2)}, u32[]{:S(2)}) collective-permute-start(bf16[2,2,2,5120]{3,2,1,0:T(2,128)(2,1)S(1)} %get-tuple-element.7), channel_id=1, source_target_pairs={{1,0},{2,1},{3,2},{4,3},{5,4},{6,5},{7,6},{9,8},{10,9},{11,10},{12... | collective-permute-start | bytes 245768 | tf_op jit(solution)/shard_map/ppermute | solution.py:244
  10.8 0.0 copy-done.8
  10.8 0.1 copy.49
  10.9 0.0 copy-done.7
  10.9 0.1 lt.45
  11.0 0.0 copy-done.5
  11.1 0.2 bitcast_select_fusion
  11.3 0.0 copy-done.3
  11.3 0.0 copy-done.1
  11.3 3.3 %fusion.19 = f32[2,4,2,128]{3,1,2,0:T(4,128)S(1)} fusion(bf16[2,2,5120,128]{3,2,1,0:T(8,128)(2,1)} %legendre_ref.1, f32[2,4,5120]{2,1,0:T(4,128)S(1)} %copy-done.1, f32[5120]{0:T(1024)S(1)} %copy-done.3), kind=kOutput, calls=%fused_computation.52 | convolution fusion | flops 21053440 | bytes 5435392 | tf_op jit(solution)/shard_map/mcl,mtlr->mctr/dot_general | solution.py:248
  14.6 0.1 pad.5.clone
  14.7 0.0 collective-permute-done
  14.7 0.0 collective-permute-done.1
  14.7 0.3 fusion.2
  15.0 0.1 copy.38
  15.1 0.1 copy.39
  15.2 0.1 pad_maximum_fusion.2
  15.4 0.1 maximum_maximum_fusion.1
  15.5 0.7 broadcast_in_dim.56
  16.2 9.9 %all-to-all-start = ((bf16[32,8,256]{2,1,0:T(8,128)(2,1)}), bf16[32,8,256]{2,1,0:T(8,128)(2,1)S(1)}, u32[]{:S(2)}, u32[]{:S(2)}) async-start(bf16[32,8,256]{2,1,0:T(8,128)(2,1)} %broadcast_in_dim.56), calls=%async_computation | async-start | bytes 262144 | tf_op jit(solution)/shard_map/all_to_all | solution.py:256
  26.0 0.1 iota.42
  26.2 0.1 mul.61
  26.3 0.1 pad.2.clone
  26.4 0.1 concatenate.35.data_ref
  26.5 0.7 multiply_reduce_fusion
  27.2 1.4 %maximum_multiply_fusion.sums_ref = f32[2]{0:T(128)S(1)} fusion(f32[1]{0:T(128)} %bitcast.1, f32[1]{0:T(128)} %bitcast), kind=kLoop, calls=%fused_computation.46 | loop fusion | flops 4 | bytes 16 | tf_op jit(solution)/shard_map/div | solution.py:282
  28.6 7.9 %all-to-all-done = bf16[32,8,256]{2,1,0:T(8,128)(2,1)S(1)} async-done(((bf16[32,8,256]{2,1,0:T(8,128)(2,1)}), bf16[32,8,256]{2,1,0:T(8,128)(2,1)S(1)}, u32[]{:S(2)}, u32[]{:S(2)}) %all-to-all-start) | async-done | bytes 131104 | tf_op jit(solution)/shard_map/all_to_all | solution.py:256
  36.5 17.4 %points.1 = bf16[256,256]{1,0:T(8,128)(2,1)} custom-call(s32[1]{0:T(128)} %constant.16.clone.1.blocks_ref, f32[2]{0:T(128)S(1)} %maximum_multiply_fusion.sums_ref, bf16[256,256]{1,0:T(8,128)(2,1)S(1)} %bitcast.48, f32[24,4096]{1,0:T(8,128)S(1)} %concatenate.35.data_ref), custom_call_target="tpu_custom_call" | custom-call | tf_op jit(solution)/shard_map/points/pallas_call | solution.py:284
  53.9 3.8 %all-to-all-start.1 = ((bf16[32,8,256]{2,1,0:T(8,128)(2,1)}), bf16[32,8,256]{2,1,0:T(8,128)(2,1)S(1)}, u32[]{:S(2)}, u32[]{:S(2)}) async-start(bf16[32,8,256]{2,1,0:T(8,128)(2,1)} %bitcast.18), calls=%async_computation.1 | async-start | bytes 262144 | tf_op jit(solution)/shard_map/all_to_all | solution.py:304
  57.8 0.3 maximum_maximum_fusion.edge_ref
  58.1 10.2 %all-to-all-done.1.got_ref = bf16[32,8,256]{2,1,0:T(8,128)(2,1)S(1)} async-done(((bf16[32,8,256]{2,1,0:T(8,128)(2,1)}), bf16[32,8,256]{2,1,0:T(8,128)(2,1)S(1)}, u32[]{:S(2)}, u32[]{:S(2)}) %all-to-all-start.1) | async-done | bytes 131104 | tf_op jit(solution)/shard_map/all_to_all | solution.py:304
  68.2 2.5 %copy-done = bf16[2,2,5120,128]{3,2,1,0:T(8,128)(2,1)S(1)} copy-done((bf16[2,2,5120,128]{3,2,1,0:T(8,128)(2,1)S(1)}, bf16[2,2,5120,128]{3,2,1,0:T(8,128)(2,1)}, u32[]{:S(2)}) %copy-start) | copy-done | bytes 5242904
  70.7 4.6 %analysis.1 = f32[8,8,768]{2,1,0:T(8,128)} custom-call(bf16[32,8,256]{2,1,0:T(8,128)(2,1)S(1)} %all-to-all-done.1.got_ref, bf16[2,2,5120,128]{3,2,1,0:T(8,128)(2,1)S(1)} %copy-done, bf16[2,2,16,5120]{3,2,1,0:T(8,128)(2,1)S(1)} %maximum_maximum_fusion.edge_ref), custom_call_target="tpu_custom_call" | custom-call | tf_op jit(solution)/shard_map/analysis/pallas_call | solution.py:308
  75.4 8.9 %all-to-all-start.2 = ((f32[8,8,768]{2,1,0:T(8,128)}), f32[8,8,768]{2,1,0:T(8,128)S(1)}, u32[]{:S(2)}, u32[]{:S(2)}) async-start(f32[8,8,768]{2,1,0:T(8,128)} %analysis.1), calls=%async_computation.2 | async-start | bytes 393216 | tf_op jit(solution)/shard_map/all_to_all | solution.py:327
  84.2 0.1 dynamic_slice.11
  84.3 7.2 %all-to-all-done.2 = f32[8,8,768]{2,1,0:T(8,128)S(1)} async-done(((f32[8,8,768]{2,1,0:T(8,128)}), f32[8,8,768]{2,1,0:T(8,128)S(1)}, u32[]{:S(2)}, u32[]{:S(2)}) %all-to-all-start.2) | async-done | bytes 196640 | tf_op jit(solution)/shard_map/all_to_all | solution.py:327
  91.5 0.6 fusion.24
  93.4 0.6 multiply_subtract_fusion
  (30 shorter events, 0.3 us)
Async XLA Ops:
  0.6 10.1 %copy-start.8 = (s32[2]{0:T(128)S(1)}, s32[2]{0:T(128)}, u32[]{:S(2)}) copy-start(s32[2]{0:T(128)} %param.12) | copy-start | bytes 28
  0.6 10.3 %copy-start.7 = (s32[1,1,32]{2,1,0:T(1,128)S(1)}, s32[1,1,32]{2,1,0:T(1,128)}, u32[]{:S(2)}) copy-start(s32[1,1,32]{2,1,0:T(1,128)} %param.17) | copy-start | bytes 388
  0.7 10.4 %copy-start.5 = (s32[2,1,1,32,128]{4,3,2,1,0:T(8,128)S(1)}, s32[2,1,1,32,128]{4,3,2,1,0:T(8,128)}, u32[]{:S(2)}) copy-start(s32[2,1,1,32,128]{4,3,2,1,0:T(8,128)} %param.15) | copy-start | bytes 98308
  0.7 10.4 %copy-start.2 = (f32[16,1,1,32,128]{4,3,2,1,0:T(8,128)S(1)}, f32[16,1,1,32,128]{4,3,2,1,0:T(8,128)}, u32[]{:S(2)}) copy-start(f32[16,1,1,32,128]{4,3,2,1,0:T(8,128)} %param.14) | copy-start | bytes 786436
  0.7 10.6 %copy-start.6 = (f32[2,1,1,32,128]{4,3,2,1,0:T(8,128)S(1)}, f32[2,1,1,32,128]{4,3,2,1,0:T(8,128)}, u32[]{:S(2)}) copy-start(f32[2,1,1,32,128]{4,3,2,1,0:T(8,128)} %param.16) | copy-start | bytes 98308
  0.7 10.6 %copy-start.3 = (f32[5120]{0:T(1024)S(1)}, f32[5120]{0:T(1024)}, u32[]{:S(2)}) copy-start(f32[5120]{0:T(1024)} %param.11) | copy-start | bytes 61444
  0.7 10.6 %copy-start.1 = (f32[2,4,5120]{2,1,0:T(4,128)S(1)}, f32[2,4,5120]{2,1,0:T(4,128)}, u32[]{:S(2)}) copy-start(f32[2,4,5120]{2,1,0:T(4,128)} %param.9) | copy-start | bytes 491524
  4.8 21.4 %copy-start.4 = (f32[2,5120]{1,0:T(2,128)S(1)}, f32[2,5120]{1,0:T(2,128)}, u32[]{:S(2)}) copy-start(f32[2,5120]{1,0:T(2,128)} %param.10) | copy-start | bytes 122884
  4.9 9.8 %collective-permute-start = (bf16[2,2,2,5120]{3,2,1,0:T(2,128)(2,1)S(1)}, bf16[2,2,2,5120]{3,2,1,0:T(2,128)(2,1)S(1)}, u32[]{:S(2)}, u32[]{:S(2)}) collective-permute-start(bf16[2,2,2,5120]{3,2,1,0:T(2,128)(2,1)S(1)} %get-tuple-element.6), channel_id=1, source_target_pairs={{0,1},{1,2},{2,3},{3,4},{4,5},{5,6},{6,7},{8,9},{9,10},{10,11},{11... | collective-permute-start | bytes 245768 | tf_op jit(solution)/shard_map/ppermute | solution.py:243
  8.3 6.4 %collective-permute-start.1 = (bf16[2,2,2,5120]{3,2,1,0:T(2,128)(2,1)S(1)}, bf16[2,2,2,5120]{3,2,1,0:T(2,128)(2,1)S(1)}, u32[]{:S(2)}, u32[]{:S(2)}) collective-permute-start(bf16[2,2,2,5120]{3,2,1,0:T(2,128)(2,1)S(1)} %get-tuple-element.7), channel_id=1, source_target_pairs={{1,0},{2,1},{3,2},{4,3},{5,4},{6,5},{7,6},{9,8},{10,9},{11,10},{12... | collective-permute-start | bytes 245768 | tf_op jit(solution)/shard_map/ppermute | solution.py:244
  16.2 20.3 %all-to-all-start = ((bf16[32,8,256]{2,1,0:T(8,128)(2,1)}), bf16[32,8,256]{2,1,0:T(8,128)(2,1)S(1)}, u32[]{:S(2)}, u32[]{:S(2)}) async-start(bf16[32,8,256]{2,1,0:T(8,128)(2,1)} %broadcast_in_dim.56), calls=%async_computation | async-start | bytes 262144 | tf_op jit(solution)/shard_map/all_to_all | solution.py:256
  53.9 14.3 %all-to-all-start.1 = ((bf16[32,8,256]{2,1,0:T(8,128)(2,1)}), bf16[32,8,256]{2,1,0:T(8,128)(2,1)S(1)}, u32[]{:S(2)}, u32[]{:S(2)}) async-start(bf16[32,8,256]{2,1,0:T(8,128)(2,1)} %bitcast.18), calls=%async_computation.1 | async-start | bytes 262144 | tf_op jit(solution)/shard_map/all_to_all | solution.py:304
  68.2 2.5 %copy-start = (bf16[2,2,5120,128]{3,2,1,0:T(8,128)(2,1)S(1)}, bf16[2,2,5120,128]{3,2,1,0:T(8,128)(2,1)}, u32[]{:S(2)}) copy-start(bf16[2,2,5120,128]{3,2,1,0:T(8,128)(2,1)} %legendre_ref.1) | copy-start | bytes 15728644
  75.4 16.1 %all-to-all-start.2 = ((f32[8,8,768]{2,1,0:T(8,128)}), f32[8,8,768]{2,1,0:T(8,128)S(1)}, u32[]{:S(2)}, u32[]{:S(2)}) async-start(f32[8,8,768]{2,1,0:T(8,128)} %analysis.1), calls=%async_computation.2 | async-start | bytes 393216 | tf_op jit(solution)/shard_map/all_to_all | solution.py:327

commit v2 on v1

v2 whole, which is shorter than its diff:
```python
import functools
import math

import jax
import jax.numpy as jnp
from jax import lax
from jax.experimental import pallas as pl
from jax.experimental.pallas import tpu as pltpu
from jax.sharding import PartitionSpec as P

NPHI = 20480
ROWS = 144
LANES = 256
BLOCK = 256
VMEM_LIMIT = 16 * 1024 * 1024
POINTS_LIMIT = 46 * 1024 * 1024
AHEAD = 4
PARTS = 2
STREAM_LIMIT = 60 * 1024 * 1024
F32 = jnp.float32
BF16 = jnp.bfloat16


def split3(value):
    first = value.astype(BF16).astype(F32)
    rest = value - first
    second = rest.astype(BF16).astype(F32)
    third = (rest - second).astype(BF16).astype(F32)
    return first, second, third


def trig_tables(modes):
    lane = lax.broadcasted_iota(jnp.int32, (64, 128), 1)
    digit = lane & 31
    steps = jnp.where(
        lane < 32, digit * 1024, jnp.where(lane < 64, digit * 32, jnp.where(lane < 96, digit, lane & 3))
    )
    product = modes * steps
    high = product >> 12
    turn = (high - 5 * ((high * 52429) >> 18)) * 4096 + (product & 4095)
    quarter = jnp.zeros_like(turn)
    for edge in (2560, 7680, 12800, 17920):
        quarter = quarter + (turn >= edge).astype(jnp.int32)
    angle = (turn - 5120 * quarter).astype(F32) * (2.0 * math.pi / NPHI)
    quarter = quarter & 3
    sq = angle * angle
    sine = angle * (1.0 + sq * (-1.0 / 6 + sq * (1.0 / 120 + sq * (-1.0 / 5040 + sq * (1.0 / 362880)))))
    cosine = 1.0 + sq * (
        -0.5 + sq * (1.0 / 24 + sq * (-1.0 / 720 + sq * (1.0 / 40320 - sq * (1.0 / 3628800))))
    )
    cos_out = jnp.where(
        quarter == 0, cosine, jnp.where(quarter == 1, -sine, jnp.where(quarter == 2, -cosine, sine))
    )
    sin_out = jnp.where(
        quarter == 0, sine, jnp.where(quarter == 1, cosine, jnp.where(quarter == 2, -sine, -cosine))
    )
    return cos_out, sin_out


def pack_kernel(counts_ref, weights_ref, base_ref, noise_ref, data_ref, blocks_ref):
    data_ref[...] = jnp.zeros_like(data_ref)
    lane = lax.broadcasted_iota(jnp.int32, (24, 128), 1)
    used = jnp.int32(0)
    for owner in range(32):
        count = counts_ref[0, 0, owner]
        pixel = base_ref[1, owner : owner + 1, :] + (owner * 640 - 2)
        if owner == 0:
            pixel = jnp.where(pixel < 0, pixel + NPHI, pixel)
        if owner == 31:
            pixel = jnp.where(pixel >= NPHI, pixel - NPHI, pixel)
        live = jnp.concatenate(
            [
                weights_ref[:, owner, :],
                base_ref[0, owner : owner + 1, :].astype(F32),
                pixel.astype(F32),
                noise_ref[:, owner, :],
                jnp.zeros((4, 128), F32),
            ],
            axis=0,
        )
        live = jnp.where(lane < count, live, 0.0)
        shift = used & 127
        live = pltpu.roll(live, shift, 1)
        start = pl.multiple_of((used >> 7) * 128, 128)
        here = data_ref[:, pl.ds(start, 128)]
        data_ref[:, pl.ds(start, 128)] = jnp.where(lane >= shift, live, here)
        after = pl.multiple_of(start + 128, 128)
        data_ref[:, pl.ds(after, 128)] = jnp.where(lane < shift, live, 0.0)
        used = used + count
    blocks_ref[0] = (used + (BLOCK - 1)) // BLOCK


def points_kernel(
    blocks_ref, sums_ref, x_ref, data_ref, source_ref, out_ref, legendre_ref, table_ref, field_ref, acc_ref, curv_ref, grid_ref, wave_ref, term_ref, hit_ref, sem
):
    move = pltpu.make_async_copy(source_ref, legendre_ref, sem)
    move.start()
    row_id = lax.broadcasted_iota(jnp.int32, (256, 256), 0)
    col_id = lax.broadcasted_iota(jnp.int32, (256, 256), 1)
    to_mode_last = (col_id == 4 * (row_id & 63) + (row_id >> 6)).astype(F32).astype(BF16)
    to_mode_first = (row_id == 4 * (col_id & 63) + (col_id >> 6)).astype(F32).astype(BF16)
    fields = jnp.dot(to_mode_last, x_ref[...], preferred_element_type=F32)
    field_ref[...] = fields.astype(BF16)
    grid_ref[...] = lax.broadcasted_iota(jnp.int32, (ROWS, BLOCK), 0).astype(F32).astype(BF16)
    head = fields[:64, 128:256]
    head_lane = lax.broadcasted_iota(jnp.int32, (64, 128), 1)
    mode_value = jnp.sum(
        jnp.where(head_lane == 4, head * 64.0, jnp.where(head_lane == 5, head, 0.0)),
        axis=1,
        keepdims=True,
    )
    modes = jnp.broadcast_to(mode_value, (64, 128)).astype(jnp.int32)
    cos_tab, sin_tab = trig_tables(modes)
    weight = jnp.where(modes == 0, 1.0, 2.0).astype(F32) * 128.0**-0.5
    lane = lax.broadcasted_iota(jnp.int32, (64, 128), 1)
    groups = [
        (lane < 32, weight),
        ((lane >= 32) & (lane < 64), None),
        ((lane >= 64) & (lane < 96), None),
    ]
    for a in range(4):
        groups.append(((lane >= 96) & (((lane - 96) & 15) >> 2 == a), None))
    for index, (mask, gain) in enumerate(groups):
        for part, table in enumerate((cos_tab, -sin_tab)):
            value = table if gain is None else table * gain
            value = jnp.where(mask, value, 0.0)
            rounded = value.astype(BF16)
            start = (2 * index + part) * 64
            table_ref[pl.ds(start, 64), 0:128] = rounded
            table_ref[pl.ds(start, 64), 128:256] = (value - rounded.astype(F32)).astype(BF16)
    acc_ref[...] = jnp.zeros_like(acc_ref)
    curv_ref[...] = jnp.zeros_like(curv_ref)
    one = jnp.ones((), BF16)
    zero = jnp.zeros((), BF16)

    wave_ref[...] = jnp.zeros_like(wave_ref)
    term_ref[...] = jnp.zeros_like(term_ref)
    hit_ref[...] = jnp.zeros_like(hit_ref)

    def spread():
        acc_ref[:, 0:ROWS] += lax.dot_general(
            term_ref[...], hit_ref[...], (((1,), (1,)), ((), ())), preferred_element_type=F32
        )

    def sample(index):
        start = pl.multiple_of(jnp.maximum(index, 0) * BLOCK, BLOCK)
        info = data_ref[16:24, pl.ds(start, BLOCK)]
        first_row = info[0:1]
        grid_row = grid_ref[...]
        total = [None, None]
        for a in range(4):
            row_hit = jnp.where(grid_row == (first_row + float(a)).astype(BF16), one, zero)
            hit_ref[:, a * BLOCK : (a + 1) * BLOCK] = row_hit
            picked = jnp.dot(field_ref[:, 0:ROWS], row_hit, preferred_element_type=F32)
            wave_re = wave_ref[2 * a]
            wave_im = wave_ref[2 * a + 1]
            for f in range(2):
                term = (
                    picked[128 * f : 128 * f + 64] * wave_re
                    + picked[128 * f + 64 : 128 * f + 128] * wave_im
                )
                total[f] = term if a == 0 else total[f] + term
        weighted = []
        for f in range(2):
            sampled = jnp.sum(total[f], axis=0, keepdims=True)
            value = info[2 + f : 3 + f] * sampled
            curv_ref[f : f + 1, :] += value * sampled
            weighted.append(value)
        for a in range(4):
            for f in range(2):
                for part in range(2):
                    row = 128 * f + 64 * part
                    term_ref[row : row + 64, a * BLOCK : (a + 1) * BLOCK] = (
                        weighted[f] * wave_ref[2 * a + part]
                    ).astype(BF16)

    def turn(index):
        data = data_ref[:, pl.ds(pl.multiple_of(index * BLOCK, BLOCK), BLOCK)]
        pixel = data[17:18].astype(jnp.int32)
        digit_id = grid_ref[0:32, :]
        hit = [
            jnp.where(digit_id == digit.astype(F32).astype(BF16), one, zero)
            for digit in (pixel >> 10, (pixel >> 5) & 31, pixel & 31)
        ]
        weights = data[0:16]
        weights_high = weights.astype(BF16)
        weights_low = (weights - weights_high.astype(F32)).astype(BF16)
        chosen = jnp.concatenate(hit + [weights_high, weights_low], axis=0)
        phases = jnp.dot(
            table_ref[...], jnp.concatenate([chosen, chosen], axis=0), preferred_element_type=F32
        )
        part = [phases[64 * i : 64 * (i + 1)] for i in range(14)]
        mid_re = part[0] * part[2] - part[1] * part[3]
        mid_im = part[0] * part[3] + part[1] * part[2]
        turn_re = mid_re * part[4] - mid_im * part[5]
        turn_im = mid_re * part[5] + mid_im * part[4]
        for a in range(4):
            wave_ref[2 * a] = turn_re * part[6 + 2 * a] - turn_im * part[7 + 2 * a]
            wave_ref[2 * a + 1] = turn_re * part[7 + 2 * a] + turn_im * part[6 + 2 * a]

    def block_step(index, carry):
        spread()
        sample(index - 1)
        turn(index)
        return carry

    lax.fori_loop(0, blocks_ref[0] + 2, block_step, 0)
    back = jnp.dot(to_mode_first, acc_ref[...].astype(BF16), preferred_element_type=F32)
    curvature = jnp.sum(curv_ref[...], axis=(0, 1), keepdims=True) + jnp.sum(
        sums_ref[8:16], axis=(0, 1), keepdims=True
    )
    norm = jnp.sum(sums_ref[0:8], axis=(0, 1), keepdims=True)
    for offset, piece in enumerate(split3(curvature) + split3(norm)):
        back = jnp.where(col_id == 132 + offset, piece, back)
    out_ref[...] = back.astype(BF16)
    move.wait()


def swap_rows(value):
    return jnp.concatenate(
        [
            value[3:4],
            -value[2:3],
            -value[1:2],
            value[0:1],
            value[7:8],
            -value[6:7],
            -value[5:6],
            value[4:5],
        ],
        axis=0,
    )


def scaled_rows(side_ref, beam_ref):
    rows = jnp.concatenate([side_ref[0], side_ref[1]], axis=0)
    return rows, (rows * beam_ref[...]).astype(BF16)


def fetch(source_ref, target_ref, sems, part, m, t):
    chunk = source_ref.shape[2] // sems.shape[0]
    place = pl.ds(part * chunk, chunk)
    return pltpu.make_async_copy(
        source_ref.at[m, t, place], target_ref.at[m, t, place], sems.at[part, m, t]
    )


def start_fetch(source_ref, target_ref, sems, part):
    if part < sems.shape[0]:
        for m in range(2):
            for t in range(2):
                fetch(source_ref, target_ref, sems, part, m, t).start()


def next_part(source_ref, target_ref, sems, part):
    for m in range(2):
        for t in range(2):
            fetch(source_ref, target_ref, sems, part, m, t).wait()
    start_fetch(source_ref, target_ref, sems, part + AHEAD)


def edge_kernel(source_ref, low_ref, high_ref, legendre_ref, sems):
    parts = sems.shape[0]
    chunk = source_ref.shape[2] // parts
    for part in range(AHEAD):
        start_fetch(source_ref, legendre_ref, sems, part)
    row = lax.broadcasted_iota(jnp.int32, (16, 256), 0)
    lane = lax.broadcasted_iota(jnp.int32, (16, 256), 1)
    cycle = (row & 1) + jnp.where(row >= 8, 126, 0)
    picks = []
    for m in range(2):
        pick = (((row >> 1) & 3) == 2 * m + (lane >> 7)) & ((lane & 127) == cycle)
        picks.append(pick.astype(F32).astype(BF16))
    for part in range(parts):
        place = slice(part * chunk, (part + 1) * chunk)
        edges = jnp.zeros((16, chunk), F32)
        next_part(source_ref, legendre_ref, sems, part)
        for m in range(2):
            table = jnp.concatenate([legendre_ref[m, 0, place], legendre_ref[m, 1, place]], axis=1)
            edges = edges + lax.dot_general(
                picks[m], table, (((1,), (1,)), ((), ())), preferred_element_type=F32
            )
        high_ref[:, place] = edges[0:8].astype(BF16)
        low_ref[:, place] = edges[8:16].astype(BF16)


def synth_kernel(side_ref, beam_ref, spectra_ref, legendre_ref, modes_ref, sums_ref):
    rows, coef = scaled_rows(side_ref, beam_ref)
    square = rows * rows
    spectra = spectra_ref[...]
    pair = jnp.concatenate([spectra[0:1]] * 2 + [spectra[1:2]] * 2, axis=0)
    prior = square * jnp.concatenate([pair, pair], axis=0)
    norm_sum = square[:, 0:128]
    prior_sum = prior[:, 0:128]
    for start in range(128, rows.shape[1], 128):
        norm_sum = norm_sum + square[:, start : start + 128]
        prior_sum = prior_sum + prior[:, start : start + 128]
    sums_ref[...] = jnp.concatenate([norm_sum, prior_sum], axis=0) * 0.125
    own = []
    for m in range(2):
        table = jnp.concatenate([legendre_ref[m, 0], legendre_ref[m, 1]], axis=1)
        own.append(jnp.dot(coef, table, preferred_element_type=F32)[4 * m : 4 * m + 4])
    modes_ref[...] = jnp.concatenate(own, axis=0)


def fields_kernel(m_ref, side_ref, beam_ref, low_ref, high_ref, modes_ref, out_ref):
    _, coef = scaled_rows(side_ref, beam_ref)
    rims = jnp.concatenate([low_ref[...], high_ref[...]], axis=0)
    rim = lax.dot_general(coef, rims, (((1,), (1,)), ((), ())), preferred_element_type=F32)
    rim = jnp.concatenate([rim, jnp.zeros((8, 112), F32)], axis=1)
    row = lax.broadcasted_iota(jnp.int32, (8, 128), 0)
    lane = lax.broadcasted_iota(jnp.int32, (8, 128), 1)
    rim = jnp.where(row < 4, rim, pltpu.roll(rim, 124, 1))
    low, high = [], []
    for t in range(2):
        own = pltpu.roll(modes_ref[:, 128 * t : 128 * t + 128], 2, 1)
        below = pltpu.roll(rim, 126, 1) if t else rim
        above = pltpu.roll(rim, 120 if t else 122, 1)
        low.append(jnp.where(lane < 2, below, own))
        high.append(jnp.where(lane < 2, own, jnp.where(lane < 4, above, 0.0)))
    low = swap_rows(low[1]) - low[0]
    high = swap_rows(high[1]) - high[0]
    mode = jnp.where(row < 4, m_ref[0], m_ref[1])
    high = jnp.where(lane == 4, (mode >> 6).astype(F32), high)
    high = jnp.where(lane == 5, (mode & 63).astype(F32), high)
    sent = jnp.concatenate([low, high], axis=1).astype(BF16)
    for target in range(32):
        out_ref[target] = sent


def analysis_kernel(got_ref, low_ref, high_ref, legendre_ref, out_ref):
    total = got_ref[0].astype(F32)
    for source in range(1, 32):
        total = total + got_ref[source].astype(F32)
    lane = lax.broadcasted_iota(jnp.int32, (8, 128), 1)
    row = lax.broadcasted_iota(jnp.int32, (8, 128), 0)
    low, high = total[:, 0:128], total[:, 128:256]
    curvature = jnp.sum(jnp.where((lane >= 4) & (lane < 7), high, 0.0), axis=1, keepdims=True)
    norm = jnp.sum(jnp.where((lane >= 7) & (lane < 10), high, 0.0), axis=1, keepdims=True)
    sums = jnp.where(lane == 0, curvature, jnp.where(lane == 1, norm, 0.0))
    own = jnp.where(lane < 126, pltpu.roll(low, 126, 1), pltpu.roll(high, 126, 1))
    own_both = jnp.concatenate([-own, swap_rows(own)], axis=1)
    row_both = lax.broadcasted_iota(jnp.int32, (8, 256), 0)
    owns = []
    for m in range(2):
        owns.append(jnp.where((row_both >> 2) == m, own_both, 0.0).astype(BF16))
    low_swap, high_swap = swap_rows(low), swap_rows(high)
    rim = jnp.where(lane < 2, -low, jnp.where(lane < 4, pltpu.roll(low_swap, 2, 1), 0.0))
    rim = jnp.where((lane >= 8) & (lane < 10), pltpu.roll(-high, 6, 1), rim)
    rim = jnp.where((lane >= 10) & (lane < 12), pltpu.roll(high_swap, 8, 1), rim)
    rim = jnp.where(row < 4, rim, pltpu.roll(rim, 4, 1)).astype(BF16)


    bands = out_ref.shape[0]
    chunk = legendre_ref.shape[2] // bands
    for band in range(bands):
        place = slice(band * chunk, (band + 1) * chunk)
        rims = jnp.concatenate([low_ref[:, place], high_ref[:, place]], axis=0)
        result = jnp.dot(rim[:, 0:16], rims, preferred_element_type=F32)
        for m in range(2):
            table = jnp.concatenate([legendre_ref[m, 0, place], legendre_ref[m, 1, place]], axis=1)
            result = result + lax.dot_general(
                owns[m], table, (((1,), (1,)), ((), ())), preferred_element_type=F32
            )
        out_ref[band, :, 0:chunk] = result
        out_ref[band, :, chunk : chunk + 128] = sums


def update_kernel(band_ref, parts_ref, side_ref, beam_ref, spectra_ref, solution_ref, residual_ref):
    del band_ref
    total = parts_ref[0]
    for source in range(1, parts_ref.shape[0]):
        total = total + parts_ref[source]
    share = side_ref.shape[2]
    step = total[0:1, share + 1 : share + 2] / total[0:1, share : share + 1]
    spectra = spectra_ref[...]
    pair = jnp.concatenate([spectra[0:1]] * 2 + [spectra[1:2]] * 2, axis=0)
    beam = beam_ref[...]
    for m in range(2):
        side = side_ref[m]
        image = pair * side + beam * total[4 * m : 4 * m + 4, 0:share]
        solution_ref[m] = step * side
        residual_ref[m] = side - step * image


def local(
    right_side,
    inv_spectra,
    beam,
    m_values,
    legendre,
    stencil_weights,
    stencil_base,
    inv_noise,
    slot_counts,
):
    band_count = lax.axis_size("band")
    lmax_len = right_side.shape[2]
    share_len = lmax_len // band_count
    smem = pl.BlockSpec(memory_space=pltpu.SMEM)
    vmem = pl.BlockSpec(memory_space=pltpu.VMEM)
    params = pltpu.CompilerParams(vmem_limit_bytes=VMEM_LIMIT)
    stream_params = pltpu.CompilerParams(vmem_limit_bytes=STREAM_LIMIT)
    hbm = pl.BlockSpec(memory_space=pl.ANY)
    beam_row = beam.reshape(1, lmax_len)

    low_edge, high_edge = pl.pallas_call(
        edge_kernel,
        out_shape=(
            jax.ShapeDtypeStruct((8, lmax_len), BF16),
            jax.ShapeDtypeStruct((8, lmax_len), BF16),
        ),
        in_specs=[hbm],
        out_specs=(vmem, vmem),
        scratch_shapes=[pltpu.VMEM(legendre.shape, BF16), pltpu.SemaphoreType.DMA((PARTS, 2, 2))],
        compiler_params=stream_params,
        name="edges",
    )(legendre)
    own_modes, sums = pl.pallas_call(
        synth_kernel,
        out_shape=(
            jax.ShapeDtypeStruct((8, 256), F32),
            jax.ShapeDtypeStruct((16, 128), F32),
        ),
        in_specs=[vmem, vmem, vmem, vmem],
        out_specs=(vmem, vmem),
        compiler_params=params,
        cost_estimate=pl.CostEstimate(flops=10**7, bytes_accessed=6 * 10**6, transcendentals=0),
        name="synth",
    )(right_side, beam_row, inv_spectra, legendre)
    up = [(i, i + 1) for i in range(band_count - 1)]
    down = [(i + 1, i) for i in range(band_count - 1)]
    low_rim = lax.ppermute(low_edge, "band", up)
    high_rim = lax.ppermute(high_edge, "band", down)

    data, blocks = pl.pallas_call(
        pack_kernel,
        out_shape=(
            jax.ShapeDtypeStruct((24, 4096 + 128 + 3 * BLOCK), F32),
            jax.ShapeDtypeStruct((1,), jnp.int32),
        ),
        in_specs=[smem, vmem, vmem, vmem],
        out_specs=(vmem, smem),
        compiler_params=params,
        cost_estimate=pl.CostEstimate(flops=10**6, bytes_accessed=3 * 10**6, transcendentals=0),
        name="pack",
    )(
        slot_counts,
        stencil_weights.reshape(16, 32, 128),
        stencil_base.reshape(2, 32, 128),
        inv_noise.reshape(2, 32, 128),
    )

    sent = pl.pallas_call(
        fields_kernel,
        out_shape=jax.ShapeDtypeStruct((32, 8, LANES), BF16),
        in_specs=[smem, vmem, vmem, vmem, vmem, vmem],
        out_specs=vmem,
        compiler_params=params,
        name="fields",
    )(m_values, right_side, beam_row, low_rim, high_rim, own_modes)
    got = lax.all_to_all(sent, "harm", split_axis=0, concat_axis=0, tiled=True)

    back, table = pl.pallas_call(
        points_kernel,
        out_shape=(
            jax.ShapeDtypeStruct((256, LANES), BF16),
            jax.ShapeDtypeStruct(legendre.shape, BF16),
        ),
        in_specs=[smem, vmem, vmem, vmem, hbm],
        out_specs=(vmem, vmem),
        scratch_shapes=[
            pltpu.VMEM((896, 256), BF16),
            pltpu.VMEM((256, LANES), BF16),
            pltpu.VMEM((256, LANES), F32),
            pltpu.VMEM((2, BLOCK), F32),
            pltpu.VMEM((ROWS, BLOCK), BF16),
            pltpu.VMEM((8, 64, BLOCK), F32),
            pltpu.VMEM((256, 4 * BLOCK), BF16),
            pltpu.VMEM((ROWS, 4 * BLOCK), BF16),
            pltpu.SemaphoreType.DMA(()),
        ],
        compiler_params=pltpu.CompilerParams(vmem_limit_bytes=POINTS_LIMIT),
        name="points",
    )(blocks, sums, got.reshape(256, LANES), data, legendre)
    back_got = lax.all_to_all(
        back.reshape(32, 8, LANES), "harm", split_axis=0, concat_axis=0, tiled=True
    )

    harmonic = pl.pallas_call(
        analysis_kernel,
        out_shape=jax.ShapeDtypeStruct((band_count, 8, share_len + 128), F32),
        in_specs=[vmem, vmem, vmem, vmem],
        out_specs=vmem,
        compiler_params=params,
        name="analysis",
    )(back_got, low_rim, high_rim, table)
    parts = lax.all_to_all(harmonic, "band", split_axis=0, concat_axis=0, tiled=True)

    band = lax.axis_index("band").astype(jnp.int32).reshape(1)
    return pl.pallas_call(
        update_kernel,
        grid_spec=pltpu.PrefetchScalarGridSpec(
            num_scalar_prefetch=1,
            grid=(1,),
            in_specs=[
                pl.BlockSpec((band_count, 8, share_len + 128), lambda i, b: (0, 0, 0)),
                pl.BlockSpec((2, 4, share_len), lambda i, b: (0, 0, b[0])),
                pl.BlockSpec((1, share_len), lambda i, b: (0, b[0])),
                pl.BlockSpec((2, share_len), lambda i, b: (0, b[0])),
            ],
            out_specs=(
                pl.BlockSpec((2, 4, share_len), lambda i, b: (0, 0, 0)),
                pl.BlockSpec((2, 4, share_len), lambda i, b: (0, 0, 0)),
            ),
        ),
        out_shape=(
            jax.ShapeDtypeStruct((2, 4, share_len), F32),
            jax.ShapeDtypeStruct((2, 4, share_len), F32),
        ),
        compiler_params=params,
        name="update",
    )(band, parts, right_side, beam_row, inv_spectra)


def solution(mesh):
    placed = (
        P("harm", None, None),
        P(),
        P(),
        P("harm"),
        P("harm", None, None, "band"),
        P(None, "harm", "band", None, None),
        P(None, "harm", "band", None, None),
        P(None, "harm", "band", None, None),
        P("harm", "band", None),
    )
    return jax.shard_map(
        local,
        mesh=mesh,
        in_specs=placed,
        out_specs=(P("harm", None, "band"), P("harm", None, "band")),
        check_vma=False,
    )
```

time: 94.6 us -> 77.4 us (0.82)
  blocking collectives: 0 us -> 13.4 us
  waiting for transfers between devices: 25.3 us -> 17.1 us
  matrix products: 7.6 us -> 0 us
  starting transfers between devices: 28.4 us -> 23.6 us
  other arithmetic: 3.48 us -> 0 us
  Pallas kernels: 22.1 us -> 19.6 us
  local copies, waits for them, and re-layouts: 4.93 us -> 2.52 us
  between operations: 2.3 us -> 0.81 us
    all_to_all x0 -> x1, blocking collectives: none -> 13.4 us  [local(): lax.all_to_all(back.reshape(32, 8, LANES), 'harm', split_axis=0, concat_a...]
    all_to_all x2 -> x1, waiting for transfers between devices: 18.1 us -> 9.08 us  [local(): got = lax.all_to_all(sent, 'harm', split_axis=0, concat_axis=0, tiled=True)]
    dot_general x3 -> x0, matrix products: 7.6 us -> none  [the longest x1 4.05 us: local(): jnp.einsum('kr,mtlr->mtkl', pick, legendre, preferred_element_type=F32)]
    all_to_all x2 -> x1, starting transfers between devices: 13.7 us -> 9.87 us  [local(): got = lax.all_to_all(sent, 'harm', split_axis=0, concat_axis=0, tiled=True)]
    pallas_call x2 -> x7, Pallas kernels: 22.1 us -> 19.6 us  [the longest x1 8.57 us: local(): pl.pallas_call(points_kernel, out_shape=(jax.ShapeDtypeStruct((256, LANES...]
    div x1 -> x0, other arithmetic: 1.37 us -> none  [local(): sums = jnp.stack([norm_part, prior_part]) / band_count]
    unnamed x21 -> x18, local copies, waits for them, and re-layouts: 2.64 us -> 2.52 us
  transfers between devices with their start and end apart: 5 -> 4, of which waited for: 3 -> 3; matrix products, arithmetic and copies ran while one was open for 7% -> 0% of each run, Pallas kernels for 0% -> 3%
where the time goes in v2:
time: 77.4 us; the launch traced here: 77.1 us
  starting transfers between devices  23.6 us (30%)
  Pallas kernels  19.6 us (25%)
  waiting for transfers between devices  17.1 us (22%)
  blocking collectives  13.4 us (17%)
  local copies, waits for them, and re-layouts  2.52 us (3%)
  between operations  0.81 us (1%)
    all_to_all x1, blocking collectives, local(): lax.all_to_all(back.reshape(32, 8, LANES), 'harm', split_axis=0, concat_a...  13.4 us
    all_to_all x1, starting transfers between devices, local(): got = lax.all_to_all(sent, 'harm', split_axis=0, concat_axis=0, tiled=True)  9.87 us
    all_to_all x1, waiting for transfers between devices, local(): got = lax.all_to_all(sent, 'harm', split_axis=0, concat_axis=0, tiled=True)  9.08 us
    pallas_call x1, Pallas kernels, local(): pl.pallas_call(points_kernel, out_shape=(jax.ShapeDtypeStruct((256, LANES...  8.57 us
    all_to_all x1, starting transfers between devices, local(): lax.all_to_all(harmonic, 'band', split_axis=0, concat_axis=0, tiled=True)  7.93 us
    all_to_all x1, waiting for transfers between devices, local(): lax.all_to_all(harmonic, 'band', split_axis=0, concat_axis=0, tiled=True)  7.27 us
    pallas_call x1, Pallas kernels, local(): pl.pallas_call(edge_kernel, out_shape=(jax.ShapeDtypeStruct((8, lmax_len)...  4.12 us
    ppermute x1, starting transfers between devices, local(): low_rim = lax.ppermute(low_edge, 'band', up)  3.4 us
  transfers between devices with their start and end apart: 4, of which 3 were waited for; matrix products, arithmetic and copies ran while one was open for 0% of the time, Pallas kernels for 3%

profile of v2, /device:TPU:2, one launch (start us, length us, event | category | flops | bytes accessed | tf_op | source)
XLA Modules:
  0.0 77.1 jit_solution(7857953147334275)
XLA Ops:
  0.6 0.0 copy-start.3
  0.6 0.0 copy-start.4
  0.7 0.0 copy-start.1
  0.7 0.0 copy-start.7
  0.7 0.0 copy-start.2
  0.7 0.0 copy-start.5
  0.7 0.0 copy-start.6
  0.7 0.0 copy-start.8
  0.7 4.1 %edges.1 = (bf16[8,5120]{1,0:T(8,128)(2,1)}, bf16[8,5120]{1,0:T(8,128)(2,1)}) custom-call(bf16[2,2,5120,128]{3,2,1,0:T(8,128)(2,1)} %source_ref.3), custom_call_target="tpu_custom_call" | custom-call | tf_op jit(solution)/shard_map/edges/pallas_call | solution.py:407
  4.8 3.4 %collective-permute-start = (bf16[8,5120]{1,0:T(8,128)(2,1)}, bf16[8,5120]{1,0:T(8,128)(2,1)S(1)}, u32[]{:S(2)}, u32[]{:S(2)}) collective-permute-start(bf16[8,5120]{1,0:T(8,128)(2,1)} %get-tuple-element.12), channel_id=1, source_target_pairs={{0,1},{1,2},{2,3},{3,4},{4,5},{5,6},{6,7},{8,9},{9,10},{10,11},{11... | collective-permute-start | bytes 245768 | tf_op jit(solution)/shard_map/ppermute | solution.py:433
  8.2 2.4 %collective-permute-start.1 = (bf16[8,5120]{1,0:T(8,128)(2,1)}, bf16[8,5120]{1,0:T(8,128)(2,1)S(1)}, u32[]{:S(2)}, u32[]{:S(2)}) collective-permute-start(bf16[8,5120]{1,0:T(8,128)(2,1)} %get-tuple-element.13), channel_id=1, source_target_pairs={{1,0},{2,1},{3,2},{4,3},{5,4},{6,5},{7,6},{9,8},{10,9},{11,10},{12... | collective-permute-start | bytes 245768 | tf_op jit(solution)/shard_map/ppermute | solution.py:434
  10.7 0.0 copy-done.3
  10.7 0.0 copy-done.4
  10.7 0.0 copy-done.1
  10.7 0.0 copy-start
  10.7 2.5 %copy-done = bf16[2,2,5120,128]{3,2,1,0:T(8,128)(2,1)S(1)} copy-done((bf16[2,2,5120,128]{3,2,1,0:T(8,128)(2,1)S(1)}, bf16[2,2,5120,128]{3,2,1,0:T(8,128)(2,1)}, u32[]{:S(2)}) %copy-start) | copy-done | bytes 5242904
  13.2 0.8 %synth.1 = (f32[8,256]{1,0:T(8,128)S(1)}, f32[16,128]{1,0:T(8,128)S(1)}) custom-call(f32[2,4,5120]{2,1,0:T(4,128)S(1)} %copy-done.1, f32[1,5120]{1,0:T(1,128)S(1)} %bitcast.9, f32[2,5120]{1,0:T(2,128)S(1)} %copy-done.4, bf16[2,2,5120,128]{3,2,1,0:T(8,128)(2,1)S(1)} %copy-done), custom_call_target="tpu_custom_call" | custom-call | flops 10000000 | bytes 6000000 | tf_op jit(solution)/shard_map/synth/pallas_call | solution.py:419
  14.0 0.0 collective-permute-done.low_ref
  14.0 0.8 %collective-permute-done.1.high_ref = bf16[8,5120]{1,0:T(8,128)(2,1)S(1)} collective-permute-done((bf16[8,5120]{1,0:T(8,128)(2,1)}, bf16[8,5120]{1,0:T(8,128)(2,1)S(1)}, u32[]{:S(2)}, u32[]{:S(2)}) %collective-permute-start.1) | collective-permute-done | bytes 81952 | tf_op jit(solution)/shard_map/ppermute | solution.py:434
  14.8 0.0 copy-done.7
  14.8 1.6 %fields.1 = bf16[32,8,256]{2,1,0:T(8,128)(2,1)} custom-call(s32[2]{0:T(128)S(1)} %copy-done.7, f32[2,4,5120]{2,1,0:T(4,128)S(1)} %copy-done.1, f32[1,5120]{1,0:T(1,128)S(1)} %bitcast.10, bf16[8,5120]{1,0:T(8,128)(2,1)S(1)} %collective-permute-done.low_ref, bf16[8,5120]{1,0:T(8,128)(2,1)S(1)} %collective-permute-done.1.high_ref, ...), custom_call_target="tpu_custom_call" | custom-call | tf_op jit(solution)/shard_map/fields/pallas_call | solution.py:454
  16.4 9.9 %all-to-all-start = ((bf16[32,8,256]{2,1,0:T(8,128)(2,1)}), bf16[32,8,256]{2,1,0:T(8,128)(2,1)S(1)}, u32[]{:S(2)}, u32[]{:S(2)}) async-start(bf16[32,8,256]{2,1,0:T(8,128)(2,1)} %fields.1), calls=%async_computation | async-start | bytes 262144 | tf_op jit(solution)/shard_map/all_to_all | solution.py:462
  26.2 0.0 copy-done.2
  26.2 0.0 copy-done.5
  26.3 0.0 copy-done.6
  26.3 0.0 copy-done.8
  26.3 1.3 %pack.1 = (f32[24,4992]{1,0:T(8,128)S(1)}, s32[1]{0:T(128)}) custom-call(s32[1,1,32]{2,1,0:T(1,128)S(1)} %copy-done.8, f32[16,32,128]{2,1,0:T(8,128)S(1)} %bitcast.8, s32[2,32,128]{2,1,0:T(8,128)S(1)} %bitcast.13, f32[2,32,128]{2,1,0:T(8,128)S(1)} %bitcast.14), custom_call_target="tpu_custom_call" | custom-call | flops 1000000 | bytes 3000000 | tf_op jit(solution)/shard_map/pack/pallas_call | solution.py:436
  27.6 9.1 %all-to-all-done = bf16[32,8,256]{2,1,0:T(8,128)(2,1)S(1)} async-done(((bf16[32,8,256]{2,1,0:T(8,128)(2,1)}), bf16[32,8,256]{2,1,0:T(8,128)(2,1)S(1)}, u32[]{:S(2)}, u32[]{:S(2)}) %all-to-all-start) | async-done | bytes 131104 | tf_op jit(solution)/shard_map/all_to_all | solution.py:462
  36.7 8.6 %points.1 = (bf16[256,256]{1,0:T(8,128)(2,1)S(1)}, bf16[2,2,5120,128]{3,2,1,0:T(8,128)(2,1)S(1)}) custom-call(s32[1]{0:T(128)} %get-tuple-element.10.blocks_ref, f32[16,128]{1,0:T(8,128)S(1)} %get-tuple-element.11.sums_ref, bf16[256,256]{1,0:T(8,128)(2,1)S(1)} %bitcast.7, f32[24,4992]{1,0:T(8,128)S(1)} %get-tuple-element.15.data_ref, ...), custom_call_target="tpu_custom_call" | custom-call | tf_op jit(solution)/shard_map/points/pallas_call | solution.py:464
  45.3 13.4 %all_to_all.15.got_ref = bf16[32,8,256]{2,1,0:T(8,128)(2,1)S(1)} all-to-all(bf16[32,8,256]{2,1,0:T(8,128)(2,1)S(1)} %bitcast.12), channel_id=1, replica_groups=mesh['harm'=32,'band'=8] {'harm'}, dimensions={0} | all-to-all | bytes 262144 | tf_op jit(solution)/shard_map/all_to_all | solution.py:486
  58.7 2.4 %analysis.1 = f32[8,8,768]{2,1,0:T(8,128)} custom-call(bf16[32,8,256]{2,1,0:T(8,128)(2,1)S(1)} %all_to_all.15.got_ref, bf16[8,5120]{1,0:T(8,128)(2,1)S(1)} %collective-permute-done.low_ref, bf16[8,5120]{1,0:T(8,128)(2,1)S(1)} %collective-permute-done.1.high_ref, bf16[2,2,5120,128]{3,2,1,0:T(8,128)(2,1)S(1)} %get-tuple-element.17.legendre_ref), custom_call_target="tpu_custom_call" | custom-call | tf_op jit(solution)/shard_map/analysis/pallas_call | solution.py:490
  61.1 7.9 %all-to-all-start.2 = ((f32[8,8,768]{2,1,0:T(8,128)}), f32[8,8,768]{2,1,0:T(8,128)S(1)}, u32[]{:S(2)}, u32[]{:S(2)}) async-start(f32[8,8,768]{2,1,0:T(8,128)} %analysis.1), calls=%async_computation.2 | async-start | bytes 393216 | tf_op jit(solution)/shard_map/all_to_all | solution.py:498
  69.0 7.3 %all-to-all-done.2.parts_ref = f32[8,8,768]{2,1,0:T(8,128)S(1)} async-done(((f32[8,8,768]{2,1,0:T(8,128)}), f32[8,8,768]{2,1,0:T(8,128)S(1)}, u32[]{:S(2)}, u32[]{:S(2)}) %all-to-all-start.2) | async-done | bytes 196640 | tf_op jit(solution)/shard_map/all_to_all | solution.py:498
  76.3 0.8 %update.1 = (f32[2,4,640]{2,1,0:T(4,128)}, f32[2,4,640]{2,1,0:T(4,128)}) custom-call(s32[1]{0:T(128)} %bitcast.band_ref, f32[8,8,768]{2,1,0:T(8,128)S(1)} %all-to-all-done.2.parts_ref, f32[2,4,5120]{2,1,0:T(4,128)S(1)} %copy-done.1, f32[1,5120]{1,0:T(1,128)S(1)} %bitcast.11, f32[2,5120]{1,0:T(2,128)S(1)} %copy-done.4), custom_call_target="tpu_custom_call" | custom-call | tf_op jit(solution)/shard_map/update/pallas_call | solution.py:501
Async XLA Ops:
  0.6 10.1 %copy-start.3 = (f32[5120]{0:T(1024)S(1)}, f32[5120]{0:T(1024)}, u32[]{:S(2)}) copy-start(f32[5120]{0:T(1024)} %param.11) | copy-start | bytes 61444
  0.6 10.1 %copy-start.4 = (f32[2,5120]{1,0:T(2,128)S(1)}, f32[2,5120]{1,0:T(2,128)}, u32[]{:S(2)}) copy-start(f32[2,5120]{1,0:T(2,128)} %spectra_ref.3) | copy-start | bytes 122884
  0.7 10.1 %copy-start.1 = (f32[2,4,5120]{2,1,0:T(4,128)S(1)}, f32[2,4,5120]{2,1,0:T(4,128)}, u32[]{:S(2)}) copy-start(f32[2,4,5120]{2,1,0:T(4,128)} %side_ref.5) | copy-start | bytes 491524
  0.7 14.1 %copy-start.7 = (s32[2]{0:T(128)S(1)}, s32[2]{0:T(128)}, u32[]{:S(2)}) copy-start(s32[2]{0:T(128)} %m_ref.1) | copy-start | bytes 28
  0.7 25.6 %copy-start.2 = (f32[16,1,1,32,128]{4,3,2,1,0:T(8,128)S(1)}, f32[16,1,1,32,128]{4,3,2,1,0:T(8,128)}, u32[]{:S(2)}) copy-start(f32[16,1,1,32,128]{4,3,2,1,0:T(8,128)} %param.14) | copy-start | bytes 786436
  0.7 25.6 %copy-start.5 = (s32[2,1,1,32,128]{4,3,2,1,0:T(8,128)S(1)}, s32[2,1,1,32,128]{4,3,2,1,0:T(8,128)}, u32[]{:S(2)}) copy-start(s32[2,1,1,32,128]{4,3,2,1,0:T(8,128)} %param.15) | copy-start | bytes 98308
  0.7 25.6 %copy-start.6 = (f32[2,1,1,32,128]{4,3,2,1,0:T(8,128)S(1)}, f32[2,1,1,32,128]{4,3,2,1,0:T(8,128)}, u32[]{:S(2)}) copy-start(f32[2,1,1,32,128]{4,3,2,1,0:T(8,128)} %param.16) | copy-start | bytes 98308
  0.7 25.6 %copy-start.8 = (s32[1,1,32]{2,1,0:T(1,128)S(1)}, s32[1,1,32]{2,1,0:T(1,128)}, u32[]{:S(2)}) copy-start(s32[1,1,32]{2,1,0:T(1,128)} %counts_ref.1) | copy-start | bytes 388
  4.8 9.2 %collective-permute-start = (bf16[8,5120]{1,0:T(8,128)(2,1)}, bf16[8,5120]{1,0:T(8,128)(2,1)S(1)}, u32[]{:S(2)}, u32[]{:S(2)}) collective-permute-start(bf16[8,5120]{1,0:T(8,128)(2,1)} %get-tuple-element.12), channel_id=1, source_target_pairs={{0,1},{1,2},{2,3},{3,4},{4,5},{5,6},{6,7},{8,9},{9,10},{10,11},{11... | collective-permute-start | bytes 245768 | tf_op jit(solution)/shard_map/ppermute | solution.py:433
  8.2 6.5 %collective-permute-start.1 = (bf16[8,5120]{1,0:T(8,128)(2,1)}, bf16[8,5120]{1,0:T(8,128)(2,1)S(1)}, u32[]{:S(2)}, u32[]{:S(2)}) collective-permute-start(bf16[8,5120]{1,0:T(8,128)(2,1)} %get-tuple-element.13), channel_id=1, source_target_pairs={{1,0},{2,1},{3,2},{4,3},{5,4},{6,5},{7,6},{9,8},{10,9},{11,10},{12... | collective-permute-start | bytes 245768 | tf_op jit(solution)/shard_map/ppermute | solution.py:434
  10.7 2.5 %copy-start = (bf16[2,2,5120,128]{3,2,1,0:T(8,128)(2,1)S(1)}, bf16[2,2,5120,128]{3,2,1,0:T(8,128)(2,1)}, u32[]{:S(2)}) copy-start(bf16[2,2,5120,128]{3,2,1,0:T(8,128)(2,1)} %source_ref.3) | copy-start | bytes 15728644
  16.4 20.3 %all-to-all-start = ((bf16[32,8,256]{2,1,0:T(8,128)(2,1)}), bf16[32,8,256]{2,1,0:T(8,128)(2,1)S(1)}, u32[]{:S(2)}, u32[]{:S(2)}) async-start(bf16[32,8,256]{2,1,0:T(8,128)(2,1)} %fields.1), calls=%async_computation | async-start | bytes 262144 | tf_op jit(solution)/shard_map/all_to_all | solution.py:462
  61.1 15.2 %all-to-all-start.2 = ((f32[8,8,768]{2,1,0:T(8,128)}), f32[8,8,768]{2,1,0:T(8,128)S(1)}, u32[]{:S(2)}, u32[]{:S(2)}) async-start(f32[8,8,768]{2,1,0:T(8,128)} %analysis.1), calls=%async_computation.2 | async-start | bytes 393216 | tf_op jit(solution)/shard_map/all_to_all | solution.py:498

commit v3 on v2

--- a/solution.py
+++ b/solution.py
@@ -11,12 +11,12 @@
 NPHI = 20480
 ROWS = 144
 LANES = 256
+PIECE = 640
 BLOCK = 256
 VMEM_LIMIT = 16 * 1024 * 1024
-POINTS_LIMIT = 46 * 1024 * 1024
 AHEAD = 4
 PARTS = 2
-STREAM_LIMIT = 60 * 1024 * 1024
+STREAM_LIMIT = 46 * 1024 * 1024
 F32 = jnp.float32
 BF16 = jnp.bfloat16
 
@@ -90,29 +90,35 @@
     blocks_ref[0] = (used + (BLOCK - 1)) // BLOCK
 
 
+def to_pieces(low, high, extra, first, count):
+    lane = lax.broadcasted_iota(jnp.int32, low[0].shape, 1)
+    rest = jnp.where((lane >= 16) & (lane < 16 + count), pltpu.roll(extra, 16 - first, 1), 0.0)
+    for q in range(4):
+        moved = pltpu.roll(high[q], 4 * q, 1) if q else high[q]
+        rest = jnp.where((lane >= 4 * q) & (lane < 4 * q + 4), moved, rest)
+    return jnp.concatenate(low + [rest], axis=1)
+
+
 def points_kernel(
     blocks_ref, sums_ref, x_ref, data_ref, source_ref, out_ref, legendre_ref, table_ref, field_ref, acc_ref, curv_ref, grid_ref, wave_ref, term_ref, hit_ref, sem
 ):
     move = pltpu.make_async_copy(source_ref, legendre_ref, sem)
     move.start()
-    row_id = lax.broadcasted_iota(jnp.int32, (256, 256), 0)
-    col_id = lax.broadcasted_iota(jnp.int32, (256, 256), 1)
-    to_mode_last = (col_id == 4 * (row_id & 63) + (row_id >> 6)).astype(F32).astype(BF16)
-    to_mode_first = (row_id == 4 * (col_id & 63) + (col_id >> 6)).astype(F32).astype(BF16)
-    fields = jnp.dot(to_mode_last, x_ref[...], preferred_element_type=F32)
-    field_ref[...] = fields.astype(BF16)
+    got = jnp.concatenate([x_ref[source].astype(F32) for source in range(32)], axis=0)
+    rest = got[:, 512:640]
+    lane = lax.broadcasted_iota(jnp.int32, (64, 128), 1)
+    for q in range(4):
+        rows = slice(64 * q, 64 * q + 64)
+        field_ref[rows, 0:128] = got[:, 128 * q : 128 * q + 128].astype(BF16)
+        moved = pltpu.roll(rest, 128 - 4 * q, 1) if q else rest
+        field_ref[rows, 128:256] = jnp.where(lane < 4, moved, 0.0).astype(BF16)
     grid_ref[...] = lax.broadcasted_iota(jnp.int32, (ROWS, BLOCK), 0).astype(F32).astype(BF16)
-    head = fields[:64, 128:256]
-    head_lane = lax.broadcasted_iota(jnp.int32, (64, 128), 1)
     mode_value = jnp.sum(
-        jnp.where(head_lane == 4, head * 64.0, jnp.where(head_lane == 5, head, 0.0)),
-        axis=1,
-        keepdims=True,
+        jnp.where(lane == 16, rest * 64.0, jnp.where(lane == 17, rest, 0.0)), axis=1, keepdims=True
     )
     modes = jnp.broadcast_to(mode_value, (64, 128)).astype(jnp.int32)
     cos_tab, sin_tab = trig_tables(modes)
     weight = jnp.where(modes == 0, 1.0, 2.0).astype(F32) * 128.0**-0.5
-    lane = lax.broadcasted_iota(jnp.int32, (64, 128), 1)
     groups = [
         (lane < 32, weight),
         ((lane >= 32) & (lane < 64), None),
@@ -133,7 +139,6 @@
     one = jnp.ones((), BF16)
     zero = jnp.zeros((), BF16)
 
-    wave_ref[...] = jnp.zeros_like(wave_ref)
     term_ref[...] = jnp.zeros_like(term_ref)
     hit_ref[...] = jnp.zeros_like(hit_ref)
 
@@ -143,7 +148,7 @@
         )
 
     def sample(index):
-        start = pl.multiple_of(jnp.maximum(index, 0) * BLOCK, BLOCK)
+        start = pl.multiple_of(index * BLOCK, BLOCK)
         info = data_ref[16:24, pl.ds(start, BLOCK)]
         first_row = info[0:1]
         grid_row = grid_ref[...]
@@ -200,19 +205,24 @@
 
     def block_step(index, carry):
         spread()
-        sample(index - 1)
-        turn(index)
+        sample(index)
+        turn(index + 1)
         return carry
 
-    lax.fori_loop(0, blocks_ref[0] + 2, block_step, 0)
-    back = jnp.dot(to_mode_first, acc_ref[...].astype(BF16), preferred_element_type=F32)
+    turn(0)
+    lax.fori_loop(0, blocks_ref[0], block_step, 0)
+    spread()
     curvature = jnp.sum(curv_ref[...], axis=(0, 1), keepdims=True) + jnp.sum(
         sums_ref[8:16], axis=(0, 1), keepdims=True
     )
     norm = jnp.sum(sums_ref[0:8], axis=(0, 1), keepdims=True)
+    extra = jnp.zeros((64, 128), F32)
     for offset, piece in enumerate(split3(curvature) + split3(norm)):
-        back = jnp.where(col_id == 132 + offset, piece, back)
-    out_ref[...] = back.astype(BF16)
+        extra = jnp.where(lane == offset, piece, extra)
+    back = [acc_ref[64 * q : 64 * q + 64] for q in range(4)]
+    sent = to_pieces([b[:, 0:128] for b in back], [b[:, 128:256] for b in back], extra, 0, 6)
+    for target in range(32):
+        out_ref[target] = sent[2 * target : 2 * target + 2].astype(BF16)
     move.wait()
 
 
@@ -284,7 +294,9 @@
         low_ref[:, place] = edges[8:16].astype(BF16)
 
 
-def synth_kernel(side_ref, beam_ref, spectra_ref, legendre_ref, modes_ref, sums_ref):
+def synth_kernel(
+    m_ref, side_ref, beam_ref, spectra_ref, legendre_ref, own_ref, coef_ref, sums_ref
+):
     rows, coef = scaled_rows(side_ref, beam_ref)
     square = rows * rows
     spectra = spectra_ref[...]
@@ -300,30 +312,36 @@
     for m in range(2):
         table = jnp.concatenate([legendre_ref[m, 0], legendre_ref[m, 1]], axis=1)
         own.append(jnp.dot(coef, table, preferred_element_type=F32)[4 * m : 4 * m + 4])
-    modes_ref[...] = jnp.concatenate(own, axis=0)
-
-
-def fields_kernel(m_ref, side_ref, beam_ref, low_ref, high_ref, modes_ref, out_ref):
-    _, coef = scaled_rows(side_ref, beam_ref)
+    modes = jnp.concatenate(own, axis=0)
+    fields = pltpu.roll(swap_rows(modes[:, 128:256]) - modes[:, 0:128], 2, 1)
+    row = lax.broadcasted_iota(jnp.int32, (8, 128), 0)
+    lane = lax.broadcasted_iota(jnp.int32, (8, 128), 1)
+    own_ref[0:8] = jnp.where(lane < 2, 0.0, fields)
+    mode = jnp.where(row < 4, m_ref[0], m_ref[1])
+    high = jnp.where(lane < 2, fields, 0.0)
+    high = jnp.where(lane == 4, (mode >> 6).astype(F32), high)
+    own_ref[8:16] = jnp.where(lane == 5, (mode & 63).astype(F32), high)
+    coef_ref[...] = coef
+
+
+def both_modes(value, q):
+    return jnp.concatenate([value[q : q + 1], value[q + 4 : q + 5]], axis=0)
+
+
+def fields_kernel(coef_ref, low_ref, high_ref, own_ref, out_ref):
     rims = jnp.concatenate([low_ref[...], high_ref[...]], axis=0)
-    rim = lax.dot_general(coef, rims, (((1,), (1,)), ((), ())), preferred_element_type=F32)
+    rim = lax.dot_general(
+        coef_ref[...], rims, (((1,), (1,)), ((), ())), preferred_element_type=F32
+    )
     rim = jnp.concatenate([rim, jnp.zeros((8, 112), F32)], axis=1)
     row = lax.broadcasted_iota(jnp.int32, (8, 128), 0)
     lane = lax.broadcasted_iota(jnp.int32, (8, 128), 1)
     rim = jnp.where(row < 4, rim, pltpu.roll(rim, 124, 1))
-    low, high = [], []
-    for t in range(2):
-        own = pltpu.roll(modes_ref[:, 128 * t : 128 * t + 128], 2, 1)
-        below = pltpu.roll(rim, 126, 1) if t else rim
-        above = pltpu.roll(rim, 120 if t else 122, 1)
-        low.append(jnp.where(lane < 2, below, own))
-        high.append(jnp.where(lane < 2, own, jnp.where(lane < 4, above, 0.0)))
-    low = swap_rows(low[1]) - low[0]
-    high = swap_rows(high[1]) - high[0]
-    mode = jnp.where(row < 4, m_ref[0], m_ref[1])
-    high = jnp.where(lane == 4, (mode >> 6).astype(F32), high)
-    high = jnp.where(lane == 5, (mode & 63).astype(F32), high)
-    sent = jnp.concatenate([low, high], axis=1).astype(BF16)
+    rim = swap_rows(pltpu.roll(rim, 126, 1)) - rim
+    low = jnp.where(lane < 2, rim, own_ref[0:8])
+    high = jnp.where((lane == 2) | (lane == 3), pltpu.roll(rim, 122, 1), own_ref[8:16])
+    sent = to_pieces([both_modes(low, q) for q in range(4)], [both_modes(high, q) for q in range(4)], both_modes(high, 0), 4, 2)
+    sent = sent.astype(BF16)
     for target in range(32):
         out_ref[target] = sent
 
@@ -334,9 +352,17 @@
         total = total + got_ref[source].astype(F32)
     lane = lax.broadcasted_iota(jnp.int32, (8, 128), 1)
     row = lax.broadcasted_iota(jnp.int32, (8, 128), 0)
-    low, high = total[:, 0:128], total[:, 128:256]
-    curvature = jnp.sum(jnp.where((lane >= 4) & (lane < 7), high, 0.0), axis=1, keepdims=True)
-    norm = jnp.sum(jnp.where((lane >= 7) & (lane < 10), high, 0.0), axis=1, keepdims=True)
+    rest = total[:, 512:640]
+    low = jnp.concatenate(
+        [total[m : m + 1, 128 * q : 128 * q + 128] for m in range(2) for q in range(4)], axis=0
+    )
+    moved = [pltpu.roll(rest, 128 - 4 * q, 1) if q else rest for q in range(4)]
+    high = jnp.concatenate([moved[q][m : m + 1] for m in range(2) for q in range(4)], axis=0)
+    extra = jnp.broadcast_to(rest[0:1], (8, 128))
+    curvature = jnp.sum(
+        jnp.where((lane >= 16) & (lane < 19), extra, 0.0), axis=1, keepdims=True
+    )
+    norm = jnp.sum(jnp.where((lane >= 19) & (lane < 22), extra, 0.0), axis=1, keepdims=True)
     sums = jnp.where(lane == 0, curvature, jnp.where(lane == 1, norm, 0.0))
     own = jnp.where(lane < 126, pltpu.roll(low, 126, 1), pltpu.roll(high, 126, 1))
     own_both = jnp.concatenate([-own, swap_rows(own)], axis=1)
@@ -404,30 +430,32 @@
     hbm = pl.BlockSpec(memory_space=pl.ANY)
     beam_row = beam.reshape(1, lmax_len)
 
-    low_edge, high_edge = pl.pallas_call(
+    low_edge, high_edge, near_table = pl.pallas_call(
         edge_kernel,
         out_shape=(
             jax.ShapeDtypeStruct((8, lmax_len), BF16),
             jax.ShapeDtypeStruct((8, lmax_len), BF16),
+            jax.ShapeDtypeStruct(legendre.shape, BF16),
         ),
         in_specs=[hbm],
-        out_specs=(vmem, vmem),
-        scratch_shapes=[pltpu.VMEM(legendre.shape, BF16), pltpu.SemaphoreType.DMA((PARTS, 2, 2))],
+        out_specs=(vmem, vmem, vmem),
+        scratch_shapes=[pltpu.SemaphoreType.DMA((PARTS, 2, 2))],
         compiler_params=stream_params,
         name="edges",
     )(legendre)
-    own_modes, sums = pl.pallas_call(
+    own_fields, coef, sums = pl.pallas_call(
         synth_kernel,
         out_shape=(
-            jax.ShapeDtypeStruct((8, 256), F32),
+            jax.ShapeDtypeStruct((16, 128), F32),
+            jax.ShapeDtypeStruct((8, lmax_len), BF16),
             jax.ShapeDtypeStruct((16, 128), F32),
         ),
-        in_specs=[vmem, vmem, vmem, vmem],
-        out_specs=(vmem, vmem),
+        in_specs=[smem, vmem, vmem, vmem, vmem],
+        out_specs=(vmem, vmem, vmem),
         compiler_params=params,
         cost_estimate=pl.CostEstimate(flops=10**7, bytes_accessed=6 * 10**6, transcendentals=0),
         name="synth",
-    )(right_side, beam_row, inv_spectra, legendre)
+    )(m_values, right_side, beam_row, inv_spectra, near_table)
     up = [(i, i + 1) for i in range(band_count - 1)]
     down = [(i + 1, i) for i in range(band_count - 1)]
     low_rim = lax.ppermute(low_edge, "band", up)
@@ -453,18 +481,19 @@
 
     sent = pl.pallas_call(
         fields_kernel,
-        out_shape=jax.ShapeDtypeStruct((32, 8, LANES), BF16),
-        in_specs=[smem, vmem, vmem, vmem, vmem, vmem],
+        out_shape=jax.ShapeDtypeStruct((32, 2, PIECE), BF16),
+        in_specs=[vmem, vmem, vmem, vmem],
         out_specs=vmem,
         compiler_params=params,
         name="fields",
-    )(m_values, right_side, beam_row, low_rim, high_rim, own_modes)
+    )(coef, low_rim, high_rim, own_fields)
+    band = lax.axis_index("band").astype(jnp.int32).reshape(1)
     got = lax.all_to_all(sent, "harm", split_axis=0, concat_axis=0, tiled=True)
 
     back, table = pl.pallas_call(
         points_kernel,
         out_shape=(
-            jax.ShapeDtypeStruct((256, LANES), BF16),
+            jax.ShapeDtypeStruct((32, 2, PIECE), BF16),
             jax.ShapeDtypeStruct(legendre.shape, BF16),
         ),
         in_specs=[smem, vmem, vmem, vmem, hbm],
@@ -480,12 +509,11 @@
             pltpu.VMEM((ROWS, 4 * BLOCK), BF16),
             pltpu.SemaphoreType.DMA(()),
         ],
-        compiler_params=pltpu.CompilerParams(vmem_limit_bytes=POINTS_LIMIT),
+        compiler_params=stream_params,
         name="points",
-    )(blocks, sums, got.reshape(256, LANES), data, legendre)
-    back_got = lax.all_to_all(
-        back.reshape(32, 8, LANES), "harm", split_axis=0, concat_axis=0, tiled=True
-    )
+    )(blocks, sums, got, data, legendre)
+    back, band = lax.optimization_barrier((back, band))
+    back_got = lax.all_to_all(back, "harm", split_axis=0, concat_axis=0, tiled=True)
 
     harmonic = pl.pallas_call(
         analysis_kernel,
@@ -497,7 +525,6 @@
     )(back_got, low_rim, high_rim, table)
     parts = lax.all_to_all(harmonic, "band", split_axis=0, concat_axis=0, tiled=True)
 
-    band = lax.axis_index("band").astype(jnp.int32).reshape(1)
     return pl.pallas_call(
         update_kernel,
         grid_spec=pltpu.PrefetchScalarGridSpec(

time: 77.4 us -> 72.4 us (0.935)
  blocking collectives: 13.4 us -> 30.1 us
  starting transfers between devices: 23.6 us -> 15.7 us
  waiting for transfers between devices: 17.1 us -> 10.5 us
  Pallas kernels: 19.6 us -> 15.1 us
  local copies, waits for them, and re-layouts: 2.52 us -> 0.03 us
    all_to_all x1 -> x2, blocking collectives: 13.4 us -> 30.1 us  [the longest x1 15.5 us: local(): lax.all_to_all(harmonic, 'band', split_axis=0, concat_axis=0, tiled=True)]
    all_to_all x1 -> x0, starting transfers between devices: 7.93 us -> none  [local(): lax.all_to_all(harmonic, 'band', split_axis=0, concat_axis=0, tiled=True)]
    all_to_all x1 -> x0, waiting for transfers between devices: 7.27 us -> none  [local(): lax.all_to_all(harmonic, 'band', split_axis=0, concat_axis=0, tiled=True)]
    pallas_call x3, Pallas kernels: 10.9 us -> 7.8 us  [the longest x1 5.27 us: local(): pl.pallas_call(points_kernel, out_shape=(jax.ShapeDtypeStruct((32, 2, PIE...]
    unnamed x18 -> x16, local copies, waits for them, and re-layouts: 2.52 us -> 0.03 us
    ppermute x1, waiting for transfers between devices: 0.78 us -> 2.43 us  [local(): high_rim = lax.ppermute(high_edge, 'band', down)]
    all_to_all x1, waiting for transfers between devices: 9.08 us -> 8.05 us  [local(): got = lax.all_to_all(sent, 'harm', split_axis=0, concat_axis=0, tiled=True)]
  transfers between devices with their start and end apart: 4 -> 3, of which waited for: 3 -> 2; matrix products, arithmetic and copies ran while one was open for 0% -> 0% of each run, Pallas kernels for 3% -> 4%
where the time goes in v3:
time: 72.4 us; the launch traced here: 72.3 us
  blocking collectives  30.1 us (42%)
  starting transfers between devices  15.7 us (22%)
  Pallas kernels  15.1 us (21%)
  waiting for transfers between devices  10.5 us (15%)
  between operations  0.81 us (1%)
    all_to_all x1, blocking collectives, local(): lax.all_to_all(harmonic, 'band', split_axis=0, concat_axis=0, tiled=True)  15.5 us
    all_to_all x1, blocking collectives, local(): lax.all_to_all(back, 'harm', split_axis=0, concat_axis=0, tiled=True)  14.6 us
    all_to_all x1, starting transfers between devices, local(): got = lax.all_to_all(sent, 'harm', split_axis=0, concat_axis=0, tiled=True)  9.87 us
    all_to_all x1, waiting for transfers between devices, local(): got = lax.all_to_all(sent, 'harm', split_axis=0, concat_axis=0, tiled=True)  8.05 us
    pallas_call x1, Pallas kernels, local(): pl.pallas_call(points_kernel, out_shape=(jax.ShapeDtypeStruct((32, 2, PIE...  5.27 us
    pallas_call x1, Pallas kernels, local(): pl.pallas_call(edge_kernel, out_shape=(jax.ShapeDtypeStruct((8, lmax_len)...  3.42 us
    ppermute x1, starting transfers between devices, local(): low_rim = lax.ppermute(low_edge, 'band', up)  3.4 us
    ppermute x1, starting transfers between devices, local(): high_rim = lax.ppermute(high_edge, 'band', down)  2.44 us
  transfers between devices with their start and end apart: 3, of which 2 were waited for; matrix products, arithmetic and copies ran while one was open for 0% of the time, Pallas kernels for 4%

profile of v3, /device:TPU:2, one launch (start us, length us, event | category | flops | bytes accessed | tf_op | source)
XLA Modules:
  0.0 72.3 jit_solution(15373757300388834565)
XLA Ops:
  0.6 0.0 copy-start.3
  0.6 0.0 copy-start.2
  0.7 0.0 copy-start.6
  0.7 0.0 copy-start
  0.7 0.0 copy-start.1
  0.7 0.0 copy-start.4
  0.7 0.0 copy-start.5
  0.7 0.0 copy-start.7
  0.7 3.4 %edges.1 = (bf16[8,5120]{1,0:T(8,128)(2,1)S(1)}, bf16[8,5120]{1,0:T(8,128)(2,1)S(1)}, bf16[2,2,5120,128]{3,2,1,0:T(8,128)(2,1)S(1)}) custom-call(bf16[2,2,5120,128]{3,2,1,0:T(8,128)(2,1)} %source_ref.3), custom_call_target="tpu_custom_call" | custom-call | tf_op jit(solution)/shard_map/edges/pallas_call | solution.py:433
  4.1 3.4 %collective-permute-start = (bf16[8,5120]{1,0:T(8,128)(2,1)S(1)}, bf16[8,5120]{1,0:T(8,128)(2,1)S(1)}, u32[]{:S(2)}, u32[]{:S(2)}) collective-permute-start(bf16[8,5120]{1,0:T(8,128)(2,1)S(1)} %get-tuple-element.18), channel_id=1, source_target_pairs={{0,1},{1,2},{2,3},{3,4},{4,5},{5,6},{6,7},{8,9},{9,10},{10,11},{11... | collective-permute-start | bytes 245768 | tf_op jit(solution)/shard_map/ppermute | solution.py:461
  7.6 2.4 %collective-permute-start.1 = (bf16[8,5120]{1,0:T(8,128)(2,1)S(1)}, bf16[8,5120]{1,0:T(8,128)(2,1)S(1)}, u32[]{:S(2)}, u32[]{:S(2)}) collective-permute-start(bf16[8,5120]{1,0:T(8,128)(2,1)S(1)} %get-tuple-element.19), channel_id=1, source_target_pairs={{1,0},{2,1},{3,2},{4,3},{5,4},{6,5},{7,6},{9,8},{10,9},{11,10},{12... | collective-permute-start | bytes 245768 | tf_op jit(solution)/shard_map/ppermute | solution.py:462
  10.0 0.0 copy-done.3
  10.0 0.0 copy-done.2
  10.0 0.0 copy-done.6
  10.0 0.0 copy-done
  10.0 1.4 %synth.1 = (f32[16,128]{1,0:T(8,128)S(1)}, bf16[8,5120]{1,0:T(8,128)(2,1)S(1)}, f32[16,128]{1,0:T(8,128)S(1)}) custom-call(s32[2]{0:T(128)S(1)} %copy-done.6, f32[2,4,5120]{2,1,0:T(4,128)S(1)} %copy-done, f32[1,5120]{1,0:T(1,128)S(1)} %bitcast.6, f32[2,5120]{1,0:T(2,128)S(1)} %copy-done.2, bf16[2,2,5120,128]{3,2,1,0:T(8,128)(2,1)S(1)} %get-tuple-element.15.legendre_ref), custom_call_target="tpu_custom_call" | custom-call | flops 10000000 | bytes 6000000 | tf_op jit(solution)/shard_map/synth/pallas_call | solution.py:446
  11.4 0.0 collective-permute-done.low_ref
  11.5 2.4 %collective-permute-done.1.high_ref = bf16[8,5120]{1,0:T(8,128)(2,1)S(1)} collective-permute-done((bf16[8,5120]{1,0:T(8,128)(2,1)S(1)}, bf16[8,5120]{1,0:T(8,128)(2,1)S(1)}, u32[]{:S(2)}, u32[]{:S(2)}) %collective-permute-start.1) | collective-permute-done | bytes 81952 | tf_op jit(solution)/shard_map/ppermute | solution.py:462
  13.9 1.1 %fields.1 = bf16[32,2,640]{2,1,0:T(2,128)(2,1)} custom-call(bf16[8,5120]{1,0:T(8,128)(2,1)S(1)} %get-tuple-element.17.coef_ref, bf16[8,5120]{1,0:T(8,128)(2,1)S(1)} %collective-permute-done.low_ref, bf16[8,5120]{1,0:T(8,128)(2,1)S(1)} %collective-permute-done.1.high_ref, f32[16,128]{1,0:T(8,128)S(1)} %get-tuple-element.20.own_ref), custom_call_target="tpu_custom_call" | custom-call | tf_op jit(solution)/shard_map/fields/pallas_call | solution.py:482
  15.0 9.9 %all-to-all-start = ((bf16[32,2,640]{2,1,0:T(2,128)(2,1)}), bf16[32,2,640]{2,1,0:T(2,128)(2,1)S(1)}, u32[]{:S(2)}, u32[]{:S(2)}) async-start(bf16[32,2,640]{2,1,0:T(2,128)(2,1)} %fields.1), calls=%async_computation | async-start | bytes 163840 | tf_op jit(solution)/shard_map/all_to_all | solution.py:491
  24.9 0.0 copy-done.1
  24.9 0.0 copy-done.4
  24.9 0.0 copy-done.5
  24.9 0.0 copy-done.7
  24.9 1.3 %pack.1 = (f32[24,4992]{1,0:T(8,128)S(1)}, s32[1]{0:T(128)}) custom-call(s32[1,1,32]{2,1,0:T(1,128)S(1)} %copy-done.7, f32[16,32,128]{2,1,0:T(8,128)S(1)} %bitcast.5, s32[2,32,128]{2,1,0:T(8,128)S(1)} %bitcast.8, f32[2,32,128]{2,1,0:T(8,128)S(1)} %bitcast.9), custom_call_target="tpu_custom_call" | custom-call | flops 1000000 | bytes 3000000 | tf_op jit(solution)/shard_map/pack/pallas_call | solution.py:464
  26.3 8.0 %all-to-all-done.x_ref = bf16[32,2,640]{2,1,0:T(2,128)(2,1)S(1)} async-done(((bf16[32,2,640]{2,1,0:T(2,128)(2,1)}), bf16[32,2,640]{2,1,0:T(2,128)(2,1)S(1)}, u32[]{:S(2)}, u32[]{:S(2)}) %all-to-all-start) | async-done | bytes 81952 | tf_op jit(solution)/shard_map/all_to_all | solution.py:491
  34.3 5.3 %points.1 = (bf16[32,2,640]{2,1,0:T(2,128)(2,1)S(1)}, bf16[2,2,5120,128]{3,2,1,0:T(8,128)(2,1)S(1)}) custom-call(s32[1]{0:T(128)} %get-tuple-element.14.blocks_ref, f32[16,128]{1,0:T(8,128)S(1)} %get-tuple-element.16.sums_ref, bf16[32,2,640]{2,1,0:T(2,128)(2,1)S(1)} %all-to-all-done.x_ref, f32[24,4992]{1,0:T(8,128)S(1)} %get-tuple-element.21.data_ref, ...), custom_call_target="tpu_custom_call" | custom-call | tf_op jit(solution)/shard_map/points/pallas_call | solution.py:493
  39.6 14.6 %all_to_all.15.got_ref = bf16[32,2,640]{2,1,0:T(2,128)(2,1)S(1)} all-to-all(bf16[32,2,640]{2,1,0:T(2,128)(2,1)S(1)} %get-tuple-element.24), channel_id=1, replica_groups=mesh['harm'=32,'band'=8] {'harm'}, dimensions={0} | all-to-all | bytes 163840 | tf_op jit(solution)/shard_map/all_to_all | solution.py:516
  54.1 1.8 %analysis.1 = f32[8,8,768]{2,1,0:T(8,128)S(1)} custom-call(bf16[32,2,640]{2,1,0:T(2,128)(2,1)S(1)} %all_to_all.15.got_ref, bf16[8,5120]{1,0:T(8,128)(2,1)S(1)} %collective-permute-done.low_ref, bf16[8,5120]{1,0:T(8,128)(2,1)S(1)} %collective-permute-done.1.high_ref, bf16[2,2,5120,128]{3,2,1,0:T(8,128)(2,1)S(1)} %get-tuple-element.25.legendre_ref), custom_call_target="tpu_custom_call" | custom-call | tf_op jit(solution)/shard_map/analysis/pallas_call | solution.py:518
  55.9 15.5 %all_to_all.16.parts_ref = f32[8,8,768]{2,1,0:T(8,128)S(1)} all-to-all(f32[8,8,768]{2,1,0:T(8,128)S(1)} %analysis.1), channel_id=1, replica_groups=mesh['harm'=32,'band'=8] {'band'}, dimensions={0} | all-to-all | bytes 393216 | tf_op jit(solution)/shard_map/all_to_all | solution.py:526
  71.5 0.8 %update.1 = (f32[2,4,640]{2,1,0:T(4,128)}, f32[2,4,640]{2,1,0:T(4,128)}) custom-call(s32[1]{0:T(128)} %bitcast.4.band_ref, f32[8,8,768]{2,1,0:T(8,128)S(1)} %all_to_all.16.parts_ref, f32[2,4,5120]{2,1,0:T(4,128)S(1)} %copy-done, f32[1,5120]{1,0:T(1,128)S(1)} %bitcast.7, f32[2,5120]{1,0:T(2,128)S(1)} %copy-done.2), custom_call_target="tpu_custom_call" | custom-call | tf_op jit(solution)/shard_map/update/pallas_call | solution.py:528
Async XLA Ops:
  0.6 9.4 %copy-start.3 = (f32[5120]{0:T(1024)S(1)}, f32[5120]{0:T(1024)}, u32[]{:S(2)}) copy-start(f32[5120]{0:T(1024)} %param.11) | copy-start | bytes 61444
  0.6 9.4 %copy-start.2 = (f32[2,5120]{1,0:T(2,128)S(1)}, f32[2,5120]{1,0:T(2,128)}, u32[]{:S(2)}) copy-start(f32[2,5120]{1,0:T(2,128)} %spectra_ref.3) | copy-start | bytes 122884
  0.7 9.4 %copy-start.6 = (s32[2]{0:T(128)S(1)}, s32[2]{0:T(128)}, u32[]{:S(2)}) copy-start(s32[2]{0:T(128)} %m_ref.1) | copy-start | bytes 28
  0.7 9.4 %copy-start = (f32[2,4,5120]{2,1,0:T(4,128)S(1)}, f32[2,4,5120]{2,1,0:T(4,128)}, u32[]{:S(2)}) copy-start(f32[2,4,5120]{2,1,0:T(4,128)} %side_ref.3) | copy-start | bytes 491524
  0.7 24.2 %copy-start.1 = (f32[16,1,1,32,128]{4,3,2,1,0:T(8,128)S(1)}, f32[16,1,1,32,128]{4,3,2,1,0:T(8,128)}, u32[]{:S(2)}) copy-start(f32[16,1,1,32,128]{4,3,2,1,0:T(8,128)} %param.14) | copy-start | bytes 786436
  0.7 24.2 %copy-start.4 = (s32[2,1,1,32,128]{4,3,2,1,0:T(8,128)S(1)}, s32[2,1,1,32,128]{4,3,2,1,0:T(8,128)}, u32[]{:S(2)}) copy-start(s32[2,1,1,32,128]{4,3,2,1,0:T(8,128)} %param.15) | copy-start | bytes 98308
  0.7 24.2 %copy-start.5 = (f32[2,1,1,32,128]{4,3,2,1,0:T(8,128)S(1)}, f32[2,1,1,32,128]{4,3,2,1,0:T(8,128)}, u32[]{:S(2)}) copy-start(f32[2,1,1,32,128]{4,3,2,1,0:T(8,128)} %param.16) | copy-start | bytes 98308
  0.7 24.2 %copy-start.7 = (s32[1,1,32]{2,1,0:T(1,128)S(1)}, s32[1,1,32]{2,1,0:T(1,128)}, u32[]{:S(2)}) copy-start(s32[1,1,32]{2,1,0:T(1,128)} %counts_ref.1) | copy-start | bytes 388
  4.1 7.3 %collective-permute-start = (bf16[8,5120]{1,0:T(8,128)(2,1)S(1)}, bf16[8,5120]{1,0:T(8,128)(2,1)S(1)}, u32[]{:S(2)}, u32[]{:S(2)}) collective-permute-start(bf16[8,5120]{1,0:T(8,128)(2,1)S(1)} %get-tuple-element.18), channel_id=1, source_target_pairs={{0,1},{1,2},{2,3},{3,4},{4,5},{5,6},{6,7},{8,9},{9,10},{10,11},{11... | collective-permute-start | bytes 245768 | tf_op jit(solution)/shard_map/ppermute | solution.py:461
  7.6 6.3 %collective-permute-start.1 = (bf16[8,5120]{1,0:T(8,128)(2,1)S(1)}, bf16[8,5120]{1,0:T(8,128)(2,1)S(1)}, u32[]{:S(2)}, u32[]{:S(2)}) collective-permute-start(bf16[8,5120]{1,0:T(8,128)(2,1)S(1)} %get-tuple-element.19), channel_id=1, source_target_pairs={{1,0},{2,1},{3,2},{4,3},{5,4},{6,5},{7,6},{9,8},{10,9},{11,10},{12... | collective-permute-start | bytes 245768 | tf_op jit(solution)/shard_map/ppermute | solution.py:462
  15.0 19.3 %all-to-all-start = ((bf16[32,2,640]{2,1,0:T(2,128)(2,1)}), bf16[32,2,640]{2,1,0:T(2,128)(2,1)S(1)}, u32[]{:S(2)}, u32[]{:S(2)}) async-start(bf16[32,2,640]{2,1,0:T(2,128)(2,1)} %fields.1), calls=%async_computation | async-start | bytes 163840 | tf_op jit(solution)/shard_map/all_to_all | solution.py:491

commit v4 on v3

--- a/solution.py
+++ b/solution.py
@@ -57,7 +57,10 @@
     return cos_out, sin_out
 
 
-def pack_kernel(counts_ref, weights_ref, base_ref, noise_ref, data_ref, blocks_ref):
+def pack_kernel(
+    band_ref, counts_ref, weights_ref, base_ref, noise_ref, side_ref, beam_ref, spectra_ref,
+    data_ref, blocks_ref, share_ref,
+):
     data_ref[...] = jnp.zeros_like(data_ref)
     lane = lax.broadcasted_iota(jnp.int32, (24, 128), 1)
     used = jnp.int32(0)
@@ -87,7 +90,14 @@
         after = pl.multiple_of(start + 128, 128)
         data_ref[:, pl.ds(after, 128)] = jnp.where(lane < shift, live, 0.0)
         used = used + count
-    blocks_ref[0] = (used + (BLOCK - 1)) // BLOCK
+    blocks_ref[...] = jnp.full(blocks_ref.shape, (used + (BLOCK - 1)) // BLOCK, jnp.int32)
+    length = share_ref.shape[1]
+    place = pl.ds(pl.multiple_of(band_ref[0] * length, 128), length)
+    share_ref[0:4] = side_ref[0, :, place]
+    share_ref[4:8] = side_ref[1, :, place]
+    share_ref[8:9] = beam_ref[:, place]
+    share_ref[9:11] = spectra_ref[:, place]
+    share_ref[11:16] = jnp.zeros((5, length), F32)
 
 
 def to_pieces(low, high, extra, first, count):
@@ -210,7 +220,7 @@
         return carry
 
     turn(0)
-    lax.fori_loop(0, blocks_ref[0], block_step, 0)
+    lax.fori_loop(0, jnp.max(blocks_ref[...]), block_step, 0)
     spread()
     curvature = jnp.sum(curv_ref[...], axis=(0, 1), keepdims=True) + jnp.sum(
         sums_ref[8:16], axis=(0, 1), keepdims=True
@@ -317,7 +327,7 @@
     row = lax.broadcasted_iota(jnp.int32, (8, 128), 0)
     lane = lax.broadcasted_iota(jnp.int32, (8, 128), 1)
     own_ref[0:8] = jnp.where(lane < 2, 0.0, fields)
-    mode = jnp.where(row < 4, m_ref[0], m_ref[1])
+    mode = jnp.where(row < 4, m_ref[:, 0:1], m_ref[:, 1:2])
     high = jnp.where(lane < 2, fields, 0.0)
     high = jnp.where(lane == 4, (mode >> 6).astype(F32), high)
     own_ref[8:16] = jnp.where(lane == 5, (mode & 63).astype(F32), high)
@@ -392,19 +402,18 @@
         out_ref[band, :, chunk : chunk + 128] = sums
 
 
-def update_kernel(band_ref, parts_ref, side_ref, beam_ref, spectra_ref, solution_ref, residual_ref):
-    del band_ref
+def update_kernel(parts_ref, share_ref, solution_ref, residual_ref):
     total = parts_ref[0]
     for source in range(1, parts_ref.shape[0]):
         total = total + parts_ref[source]
-    share = side_ref.shape[2]
-    step = total[0:1, share + 1 : share + 2] / total[0:1, share : share + 1]
-    spectra = spectra_ref[...]
+    length = share_ref.shape[1]
+    step = total[0:1, length + 1 : length + 2] / total[0:1, length : length + 1]
+    beam = share_ref[8:9]
+    spectra = share_ref[9:11]
     pair = jnp.concatenate([spectra[0:1]] * 2 + [spectra[1:2]] * 2, axis=0)
-    beam = beam_ref[...]
     for m in range(2):
-        side = side_ref[m]
-        image = pair * side + beam * total[4 * m : 4 * m + 4, 0:share]
+        side = share_ref[4 * m : 4 * m + 4]
+        image = pair * side + beam * total[4 * m : 4 * m + 4, 0:length]
         solution_ref[m] = step * side
         residual_ref[m] = side - step * image
 
@@ -450,33 +459,39 @@
             jax.ShapeDtypeStruct((8, lmax_len), BF16),
             jax.ShapeDtypeStruct((16, 128), F32),
         ),
-        in_specs=[smem, vmem, vmem, vmem, vmem],
+        in_specs=[vmem] * 5,
         out_specs=(vmem, vmem, vmem),
         compiler_params=params,
         cost_estimate=pl.CostEstimate(flops=10**7, bytes_accessed=6 * 10**6, transcendentals=0),
         name="synth",
-    )(m_values, right_side, beam_row, inv_spectra, near_table)
+    )(m_values.reshape(1, 2), right_side, beam_row, inv_spectra, near_table)
     up = [(i, i + 1) for i in range(band_count - 1)]
     down = [(i + 1, i) for i in range(band_count - 1)]
     low_rim = lax.ppermute(low_edge, "band", up)
     high_rim = lax.ppermute(high_edge, "band", down)
 
-    data, blocks = pl.pallas_call(
+    band = lax.axis_index("band").astype(jnp.int32).reshape(1)
+    data, blocks, share = pl.pallas_call(
         pack_kernel,
         out_shape=(
             jax.ShapeDtypeStruct((24, 4096 + 128 + 3 * BLOCK), F32),
-            jax.ShapeDtypeStruct((1,), jnp.int32),
+            jax.ShapeDtypeStruct((8, 128), jnp.int32),
+            jax.ShapeDtypeStruct((16, share_len), F32),
         ),
-        in_specs=[smem, vmem, vmem, vmem],
-        out_specs=(vmem, smem),
+        in_specs=[smem, smem] + [vmem] * 6,
+        out_specs=(vmem, vmem, vmem),
         compiler_params=params,
         cost_estimate=pl.CostEstimate(flops=10**6, bytes_accessed=3 * 10**6, transcendentals=0),
         name="pack",
     )(
+        band,
         slot_counts,
         stencil_weights.reshape(16, 32, 128),
         stencil_base.reshape(2, 32, 128),
         inv_noise.reshape(2, 32, 128),
+        right_side,
+        beam_row,
+        inv_spectra,
     )
 
     sent = pl.pallas_call(
@@ -487,7 +502,6 @@
         compiler_params=params,
         name="fields",
     )(coef, low_rim, high_rim, own_fields)
-    band = lax.axis_index("band").astype(jnp.int32).reshape(1)
     got = lax.all_to_all(sent, "harm", split_axis=0, concat_axis=0, tiled=True)
 
     back, table = pl.pallas_call(
@@ -496,7 +510,7 @@
             jax.ShapeDtypeStruct((32, 2, PIECE), BF16),
             jax.ShapeDtypeStruct(legendre.shape, BF16),
         ),
-        in_specs=[smem, vmem, vmem, vmem, hbm],
+        in_specs=[vmem, vmem, vmem, vmem, hbm],
         out_specs=(vmem, vmem),
         scratch_shapes=[
             pltpu.VMEM((896, 256), BF16),
@@ -512,7 +526,6 @@
         compiler_params=stream_params,
         name="points",
     )(blocks, sums, got, data, legendre)
-    back, band = lax.optimization_barrier((back, band))
     back_got = lax.all_to_all(back, "harm", split_axis=0, concat_axis=0, tiled=True)
 
     harmonic = pl.pallas_call(
@@ -527,27 +540,15 @@
 
     return pl.pallas_call(
         update_kernel,
-        grid_spec=pltpu.PrefetchScalarGridSpec(
-            num_scalar_prefetch=1,
-            grid=(1,),
-            in_specs=[
-                pl.BlockSpec((band_count, 8, share_len + 128), lambda i, b: (0, 0, 0)),
-                pl.BlockSpec((2, 4, share_len), lambda i, b: (0, 0, b[0])),
-                pl.BlockSpec((1, share_len), lambda i, b: (0, b[0])),
-                pl.BlockSpec((2, share_len), lambda i, b: (0, b[0])),
-            ],
-            out_specs=(
-                pl.BlockSpec((2, 4, share_len), lambda i, b: (0, 0, 0)),
-                pl.BlockSpec((2, 4, share_len), lambda i, b: (0, 0, 0)),
-            ),
-        ),
         out_shape=(
             jax.ShapeDtypeStruct((2, 4, share_len), F32),
             jax.ShapeDtypeStruct((2, 4, share_len), F32),
         ),
+        in_specs=[vmem, vmem],
+        out_specs=(vmem, vmem),
         compiler_params=params,
         name="update",
-    )(band, parts, right_side, beam_row, inv_spectra)
+    )(parts, share)
 
 
 def solution(mesh):

time: 72.4 us -> 72 us (level)
  waiting for transfers between devices: 10.5 us -> 11.5 us
  Pallas kernels: 15.1 us -> 14.2 us
    all_to_all x1, blocking collectives: 14.6 us -> 13.8 us  [local(): lax.all_to_all(back, 'harm', split_axis=0, concat_axis=0, tiled=True)]
  transfers between devices with their start and end apart: 3 -> 3, of which waited for: 2 -> 2; matrix products, arithmetic and copies ran while one was open for 0% -> 0% of each run, Pallas kernels for 4% -> 2%
where the time goes in v4:
time: 72 us; the launch traced here: 71.7 us
  blocking collectives  29.6 us (41%)
  starting transfers between devices  15.7 us (22%)
  Pallas kernels  14.2 us (20%)
  waiting for transfers between devices  11.5 us (16%)
  between operations  0.81 us (1%)
    all_to_all x1, blocking collectives, local(): lax.all_to_all(harmonic, 'band', split_axis=0, concat_axis=0, tiled=True)  15.7 us
    all_to_all x1, blocking collectives, local(): lax.all_to_all(back, 'harm', split_axis=0, concat_axis=0, tiled=True)  13.8 us
    all_to_all x1, starting transfers between devices, local(): got = lax.all_to_all(sent, 'harm', split_axis=0, concat_axis=0, tiled=True)  9.86 us
    all_to_all x1, waiting for transfers between devices, local(): got = lax.all_to_all(sent, 'harm', split_axis=0, concat_axis=0, tiled=True)  8.48 us
    pallas_call x1, Pallas kernels, local(): pl.pallas_call(points_kernel, out_shape=(jax.ShapeDtypeStruct((32, 2, PIE...  5.25 us
    pallas_call x1, Pallas kernels, local(): pl.pallas_call(edge_kernel, out_shape=(jax.ShapeDtypeStruct((8, lmax_len)...  3.46 us
    ppermute x1, starting transfers between devices, local(): low_rim = lax.ppermute(low_edge, 'band', up)  3.4 us
    ppermute x1, waiting for transfers between devices, local(): high_rim = lax.ppermute(high_edge, 'band', down)  2.98 us
  transfers between devices with their start and end apart: 3, of which 2 were waited for; matrix products, arithmetic and copies ran while one was open for 0% of the time, Pallas kernels for 2%

profile of v4, /device:TPU:2, one launch (start us, length us, event | category | flops | bytes accessed | tf_op | source)
XLA Modules:
  0.0 71.7 jit_solution(16561970557390217794)
XLA Ops:
  0.6 0.0 copy-start.2
  0.6 0.0 copy-start
  0.7 0.0 copy-start.6
  0.7 0.0 copy-start.3
  0.7 0.0 copy-start.7
  0.7 0.0 copy-start.5
  0.7 0.0 copy-start.4
  0.7 0.0 copy-start.1
  0.7 3.5 %edges.1 = (bf16[8,5120]{1,0:T(8,128)(2,1)S(1)}, bf16[8,5120]{1,0:T(8,128)(2,1)S(1)}, bf16[2,2,5120,128]{3,2,1,0:T(8,128)(2,1)S(1)}) custom-call(bf16[2,2,5120,128]{3,2,1,0:T(8,128)(2,1)} %source_ref.3), custom_call_target="tpu_custom_call" | custom-call | tf_op jit(solution)/shard_map/edges/pallas_call | solution.py:442
  4.2 3.4 %collective-permute-start = (bf16[8,5120]{1,0:T(8,128)(2,1)S(1)}, bf16[8,5120]{1,0:T(8,128)(2,1)S(1)}, u32[]{:S(2)}, u32[]{:S(2)}) collective-permute-start(bf16[8,5120]{1,0:T(8,128)(2,1)S(1)} %get-tuple-element.17), channel_id=1, source_target_pairs={{0,1},{1,2},{2,3},{3,4},{4,5},{5,6},{6,7},{8,9},{9,10},{10,11},{11... | collective-permute-start | bytes 245768 | tf_op jit(solution)/shard_map/ppermute | solution.py:470
  7.6 2.4 %collective-permute-start.1 = (bf16[8,5120]{1,0:T(8,128)(2,1)S(1)}, bf16[8,5120]{1,0:T(8,128)(2,1)S(1)}, u32[]{:S(2)}, u32[]{:S(2)}) collective-permute-start(bf16[8,5120]{1,0:T(8,128)(2,1)S(1)} %get-tuple-element.18), channel_id=1, source_target_pairs={{1,0},{2,1},{3,2},{4,3},{5,4},{6,5},{7,6},{9,8},{10,9},{11,10},{12... | collective-permute-start | bytes 245768 | tf_op jit(solution)/shard_map/ppermute | solution.py:471
  10.0 0.0 copy-done.2
  10.0 0.0 copy-done
  10.1 0.0 copy-done.6
  10.1 0.0 copy-done.3
  10.1 0.9 %synth.1 = (f32[16,128]{1,0:T(8,128)S(1)}, bf16[8,5120]{1,0:T(8,128)(2,1)S(1)}, f32[16,128]{1,0:T(8,128)S(1)}) custom-call(s32[1,2]{1,0:T(1,128)S(1)} %bitcast.11, f32[2,4,5120]{2,1,0:T(4,128)S(1)} %copy-done, f32[1,5120]{1,0:T(1,128)S(1)} %bitcast.7, f32[2,5120]{1,0:T(2,128)S(1)} %copy-done.2, bf16[2,2,5120,128]{3,2,1,0:T(8,128)(2,1)S(1)} %get-tuple-element.14.legendre_ref), custom_call_target="tpu_custom_call" | custom-call | flops 10000000 | bytes 6000000 | tf_op jit(solution)/shard_map/synth/pallas_call | solution.py:455
  10.9 0.0 collective-permute-done.low_ref
  10.9 3.0 %collective-permute-done.1.high_ref = bf16[8,5120]{1,0:T(8,128)(2,1)S(1)} collective-permute-done((bf16[8,5120]{1,0:T(8,128)(2,1)S(1)}, bf16[8,5120]{1,0:T(8,128)(2,1)S(1)}, u32[]{:S(2)}, u32[]{:S(2)}) %collective-permute-start.1) | collective-permute-done | bytes 81952 | tf_op jit(solution)/shard_map/ppermute | solution.py:471
  13.9 1.1 %fields.1 = bf16[32,2,640]{2,1,0:T(2,128)(2,1)} custom-call(bf16[8,5120]{1,0:T(8,128)(2,1)S(1)} %get-tuple-element.16.coef_ref, bf16[8,5120]{1,0:T(8,128)(2,1)S(1)} %collective-permute-done.low_ref, bf16[8,5120]{1,0:T(8,128)(2,1)S(1)} %collective-permute-done.1.high_ref, f32[16,128]{1,0:T(8,128)S(1)} %get-tuple-element.19.own_ref), custom_call_target="tpu_custom_call" | custom-call | tf_op jit(solution)/shard_map/fields/pallas_call | solution.py:497
  15.0 9.9 %all-to-all-start = ((bf16[32,2,640]{2,1,0:T(2,128)(2,1)}), bf16[32,2,640]{2,1,0:T(2,128)(2,1)S(1)}, u32[]{:S(2)}, u32[]{:S(2)}) async-start(bf16[32,2,640]{2,1,0:T(2,128)(2,1)} %fields.1), calls=%async_computation | async-start | bytes 163840 | tf_op jit(solution)/shard_map/all_to_all | solution.py:505
  24.9 0.0 copy-done.7
  24.9 0.0 copy-done.5
  24.9 0.0 copy-done.4
  24.9 0.0 copy-done.1
  25.0 0.9 %pack.1 = (f32[24,4992]{1,0:T(8,128)S(1)}, s32[8,128]{1,0:T(8,128)S(1)}, f32[16,640]{1,0:T(8,128)S(1)}) custom-call(s32[1]{0:T(128)} %bitcast.band_ref, s32[1,1,32]{2,1,0:T(1,128)S(1)} %copy-done.7, f32[16,32,128]{2,1,0:T(8,128)S(1)} %bitcast.6, s32[2,32,128]{2,1,0:T(8,128)S(1)} %bitcast.9, f32[2,32,128]{2,1,0:T(8,128)S(1)} %bitcast.10, ...), custom_call_target="tpu_custom_call" | custom-call | flops 1000000 | bytes 3000000 | tf_op jit(solution)/shard_map/pack/pallas_call | solution.py:474
  25.9 8.5 %all-to-all-done.x_ref = bf16[32,2,640]{2,1,0:T(2,128)(2,1)S(1)} async-done(((bf16[32,2,640]{2,1,0:T(2,128)(2,1)}), bf16[32,2,640]{2,1,0:T(2,128)(2,1)S(1)}, u32[]{:S(2)}, u32[]{:S(2)}) %all-to-all-start) | async-done | bytes 81952 | tf_op jit(solution)/shard_map/all_to_all | solution.py:505
  34.3 5.3 %points.1 = (bf16[32,2,640]{2,1,0:T(2,128)(2,1)S(1)}, bf16[2,2,5120,128]{3,2,1,0:T(8,128)(2,1)S(1)}) custom-call(s32[8,128]{1,0:T(8,128)S(1)} %get-tuple-element.13.blocks_ref, f32[16,128]{1,0:T(8,128)S(1)} %get-tuple-element.15.sums_ref, bf16[32,2,640]{2,1,0:T(2,128)(2,1)S(1)} %all-to-all-done.x_ref, f32[24,4992]{1,0:T(8,128)S(1)} %get-tuple-element.20.data_ref, ...), custom_call_target="tpu_custom_call" | custom-call | tf_op jit(solution)/shard_map/points/pallas_call | solution.py:507
  39.6 13.8 %all_to_all.15.got_ref = bf16[32,2,640]{2,1,0:T(2,128)(2,1)S(1)} all-to-all(bf16[32,2,640]{2,1,0:T(2,128)(2,1)S(1)} %get-tuple-element.21), channel_id=1, replica_groups=mesh['harm'=32,'band'=8] {'harm'}, dimensions={0} | all-to-all | bytes 163840 | tf_op jit(solution)/shard_map/all_to_all | solution.py:529
  53.4 1.8 %analysis.1 = f32[8,8,768]{2,1,0:T(8,128)S(1)} custom-call(bf16[32,2,640]{2,1,0:T(2,128)(2,1)S(1)} %all_to_all.15.got_ref, bf16[8,5120]{1,0:T(8,128)(2,1)S(1)} %collective-permute-done.low_ref, bf16[8,5120]{1,0:T(8,128)(2,1)S(1)} %collective-permute-done.1.high_ref, bf16[2,2,5120,128]{3,2,1,0:T(8,128)(2,1)S(1)} %get-tuple-element.22.legendre_ref), custom_call_target="tpu_custom_call" | custom-call | tf_op jit(solution)/shard_map/analysis/pallas_call | solution.py:531
  55.2 15.7 %all_to_all.16.parts_ref = f32[8,8,768]{2,1,0:T(8,128)S(1)} all-to-all(f32[8,8,768]{2,1,0:T(8,128)S(1)} %analysis.1), channel_id=1, replica_groups=mesh['harm'=32,'band'=8] {'band'}, dimensions={0} | all-to-all | bytes 393216 | tf_op jit(solution)/shard_map/all_to_all | solution.py:539
  70.9 0.8 %update.1 = (f32[2,4,640]{2,1,0:T(4,128)}, f32[2,4,640]{2,1,0:T(4,128)}) custom-call(f32[8,8,768]{2,1,0:T(8,128)S(1)} %all_to_all.16.parts_ref, f32[16,640]{1,0:T(8,128)S(1)} %get-tuple-element.23.share_ref), custom_call_target="tpu_custom_call" | custom-call | tf_op jit(solution)/shard_map/update/pallas_call | solution.py:541
Async XLA Ops:
  0.6 9.4 %copy-start.2 = (f32[2,5120]{1,0:T(2,128)S(1)}, f32[2,5120]{1,0:T(2,128)}, u32[]{:S(2)}) copy-start(f32[2,5120]{1,0:T(2,128)} %spectra_ref.3) | copy-start | bytes 122884
  0.6 9.4 %copy-start = (f32[2,4,5120]{2,1,0:T(4,128)S(1)}, f32[2,4,5120]{2,1,0:T(4,128)}, u32[]{:S(2)}) copy-start(f32[2,4,5120]{2,1,0:T(4,128)} %side_ref.3) | copy-start | bytes 491524
  0.7 9.4 %copy-start.6 = (s32[2]{0:T(128)S(1)}, s32[2]{0:T(128)}, u32[]{:S(2)}) copy-start(s32[2]{0:T(128)} %param.12) | copy-start | bytes 28
  0.7 9.4 %copy-start.3 = (f32[5120]{0:T(1024)S(1)}, f32[5120]{0:T(1024)}, u32[]{:S(2)}) copy-start(f32[5120]{0:T(1024)} %param.11) | copy-start | bytes 61444
  0.7 24.2 %copy-start.7 = (s32[1,1,32]{2,1,0:T(1,128)S(1)}, s32[1,1,32]{2,1,0:T(1,128)}, u32[]{:S(2)}) copy-start(s32[1,1,32]{2,1,0:T(1,128)} %counts_ref.1) | copy-start | bytes 388
  0.7 24.2 %copy-start.5 = (f32[2,1,1,32,128]{4,3,2,1,0:T(8,128)S(1)}, f32[2,1,1,32,128]{4,3,2,1,0:T(8,128)}, u32[]{:S(2)}) copy-start(f32[2,1,1,32,128]{4,3,2,1,0:T(8,128)} %param.16) | copy-start | bytes 98308
  0.7 24.2 %copy-start.4 = (s32[2,1,1,32,128]{4,3,2,1,0:T(8,128)S(1)}, s32[2,1,1,32,128]{4,3,2,1,0:T(8,128)}, u32[]{:S(2)}) copy-start(s32[2,1,1,32,128]{4,3,2,1,0:T(8,128)} %param.15) | copy-start | bytes 98308
  0.7 24.2 %copy-start.1 = (f32[16,1,1,32,128]{4,3,2,1,0:T(8,128)S(1)}, f32[16,1,1,32,128]{4,3,2,1,0:T(8,128)}, u32[]{:S(2)}) copy-start(f32[16,1,1,32,128]{4,3,2,1,0:T(8,128)} %param.14) | copy-start | bytes 786436
  4.2 6.8 %collective-permute-start = (bf16[8,5120]{1,0:T(8,128)(2,1)S(1)}, bf16[8,5120]{1,0:T(8,128)(2,1)S(1)}, u32[]{:S(2)}, u32[]{:S(2)}) collective-permute-start(bf16[8,5120]{1,0:T(8,128)(2,1)S(1)} %get-tuple-element.17), channel_id=1, source_target_pairs={{0,1},{1,2},{2,3},{3,4},{4,5},{5,6},{6,7},{8,9},{9,10},{10,11},{11... | collective-permute-start | bytes 245768 | tf_op jit(solution)/shard_map/ppermute | solution.py:470
  7.6 6.3 %collective-permute-start.1 = (bf16[8,5120]{1,0:T(8,128)(2,1)S(1)}, bf16[8,5120]{1,0:T(8,128)(2,1)S(1)}, u32[]{:S(2)}, u32[]{:S(2)}) collective-permute-start(bf16[8,5120]{1,0:T(8,128)(2,1)S(1)} %get-tuple-element.18), channel_id=1, source_target_pairs={{1,0},{2,1},{3,2},{4,3},{5,4},{6,5},{7,6},{9,8},{10,9},{11,10},{12... | collective-permute-start | bytes 245768 | tf_op jit(solution)/shard_map/ppermute | solution.py:471
  15.0 19.3 %all-to-all-start = ((bf16[32,2,640]{2,1,0:T(2,128)(2,1)}), bf16[32,2,640]{2,1,0:T(2,128)(2,1)S(1)}, u32[]{:S(2)}, u32[]{:S(2)}) async-start(bf16[32,2,640]{2,1,0:T(2,128)(2,1)} %fields.1), calls=%async_computation | async-start | bytes 163840 | tf_op jit(solution)/shard_map/all_to_all | solution.py:505

commit v5 on v4

--- a/solution.py
+++ b/solution.py
@@ -373,7 +373,10 @@
         jnp.where((lane >= 16) & (lane < 19), extra, 0.0), axis=1, keepdims=True
     )
     norm = jnp.sum(jnp.where((lane >= 19) & (lane < 22), extra, 0.0), axis=1, keepdims=True)
-    sums = jnp.where(lane == 0, curvature, jnp.where(lane == 1, norm, 0.0))
+    sums = jnp.zeros((8, 128), F32)
+    for offset, piece in enumerate(split3(curvature) + split3(norm)):
+        sums = jnp.where(lane == offset, piece, sums)
+    sums = sums.astype(BF16)
     own = jnp.where(lane < 126, pltpu.roll(low, 126, 1), pltpu.roll(high, 126, 1))
     own_both = jnp.concatenate([-own, swap_rows(own)], axis=1)
     row_both = lax.broadcasted_iota(jnp.int32, (8, 256), 0)
@@ -398,16 +401,20 @@
             result = result + lax.dot_general(
                 owns[m], table, (((1,), (1,)), ((), ())), preferred_element_type=F32
             )
-        out_ref[band, :, 0:chunk] = result
+        out_ref[band, :, 0:chunk] = result.astype(BF16)
         out_ref[band, :, chunk : chunk + 128] = sums
 
 
 def update_kernel(parts_ref, share_ref, solution_ref, residual_ref):
-    total = parts_ref[0]
+    total = parts_ref[0].astype(F32)
     for source in range(1, parts_ref.shape[0]):
-        total = total + parts_ref[source]
+        total = total + parts_ref[source].astype(F32)
     length = share_ref.shape[1]
-    step = total[0:1, length + 1 : length + 2] / total[0:1, length : length + 1]
+    rest = total[0:1, length : length + 128]
+    lane = lax.broadcasted_iota(jnp.int32, (1, 128), 1)
+    curvature = jnp.sum(jnp.where(lane < 3, rest, 0.0), axis=1, keepdims=True)
+    norm = jnp.sum(jnp.where((lane >= 3) & (lane < 6), rest, 0.0), axis=1, keepdims=True)
+    step = norm / curvature
     beam = share_ref[8:9]
     spectra = share_ref[9:11]
     pair = jnp.concatenate([spectra[0:1]] * 2 + [spectra[1:2]] * 2, axis=0)
@@ -530,7 +537,7 @@
 
     harmonic = pl.pallas_call(
         analysis_kernel,
-        out_shape=jax.ShapeDtypeStruct((band_count, 8, share_len + 128), F32),
+        out_shape=jax.ShapeDtypeStruct((band_count, 8, share_len + 128), BF16),
         in_specs=[vmem, vmem, vmem, vmem],
         out_specs=vmem,
         compiler_params=params,

time: 72 us -> 71.1 us (0.987)
  blocking collectives: 29.6 us -> 28.5 us
    all_to_all x1, blocking collectives: 13.8 us -> 12.6 us  [local(): lax.all_to_all(back, 'harm', split_axis=0, concat_axis=0, tiled=True)]
where the time goes in v5:
time: 71.1 us
  blocking collectives  28.5 us (40%)
  starting transfers between devices  15.7 us (22%)
  Pallas kernels  14.7 us (21%)
  waiting for transfers between devices  11.5 us (16%)
  between operations  0.81 us (1%)
    all_to_all x1, blocking collectives, local(): lax.all_to_all(harmonic, 'band', split_axis=0, concat_axis=0, tiled=True)  15.9 us
    all_to_all x1, blocking collectives, local(): lax.all_to_all(back, 'harm', split_axis=0, concat_axis=0, tiled=True)  12.6 us
    all_to_all x1, starting transfers between devices, local(): got = lax.all_to_all(sent, 'harm', split_axis=0, concat_axis=0, tiled=True)  9.86 us
    all_to_all x1, waiting for transfers between devices, local(): got = lax.all_to_all(sent, 'harm', split_axis=0, concat_axis=0, tiled=True)  8.48 us
    pallas_call x1, Pallas kernels, local(): pl.pallas_call(points_kernel, out_shape=(jax.ShapeDtypeStruct((32, 2, PIE...  5.84 us
    pallas_call x1, Pallas kernels, local(): pl.pallas_call(edge_kernel, out_shape=(jax.ShapeDtypeStruct((8, lmax_len)...  3.46 us
    ppermute x1, starting transfers between devices, local(): low_rim = lax.ppermute(low_edge, 'band', up)  3.4 us
    ppermute x1, waiting for transfers between devices, local(): high_rim = lax.ppermute(high_edge, 'band', down)  2.98 us
  transfers between devices with their start and end apart: 3, of which 2 were waited for; matrix products, arithmetic and copies ran while one was open for 0% of the time, Pallas kernels for 2%

profile of v5, /device:TPU:2, one launch (start us, length us, event | category | flops | bytes accessed | tf_op | source)
XLA Modules:
  0.0 71.1 jit_solution(9129043000110498822)
XLA Ops:
  0.6 0.0 copy-start.2
  0.6 0.0 copy-start
  0.7 0.0 copy-start.6
  0.7 0.0 copy-start.3
  0.7 0.0 copy-start.7
  0.7 0.0 copy-start.5
  0.7 0.0 copy-start.4
  0.7 0.0 copy-start.1
  0.7 3.5 %edges.1 = (bf16[8,5120]{1,0:T(8,128)(2,1)S(1)}, bf16[8,5120]{1,0:T(8,128)(2,1)S(1)}, bf16[2,2,5120,128]{3,2,1,0:T(8,128)(2,1)S(1)}) custom-call(bf16[2,2,5120,128]{3,2,1,0:T(8,128)(2,1)} %source_ref.3), custom_call_target="tpu_custom_call" | custom-call | tf_op jit(solution)/shard_map/edges/pallas_call | solution.py:449
  4.2 3.4 %collective-permute-start = (bf16[8,5120]{1,0:T(8,128)(2,1)S(1)}, bf16[8,5120]{1,0:T(8,128)(2,1)S(1)}, u32[]{:S(2)}, u32[]{:S(2)}) collective-permute-start(bf16[8,5120]{1,0:T(8,128)(2,1)S(1)} %get-tuple-element.17), channel_id=1, source_target_pairs={{0,1},{1,2},{2,3},{3,4},{4,5},{5,6},{6,7},{8,9},{9,10},{10,11},{11... | collective-permute-start | bytes 245768 | tf_op jit(solution)/shard_map/ppermute | solution.py:477
  7.6 2.4 %collective-permute-start.1 = (bf16[8,5120]{1,0:T(8,128)(2,1)S(1)}, bf16[8,5120]{1,0:T(8,128)(2,1)S(1)}, u32[]{:S(2)}, u32[]{:S(2)}) collective-permute-start(bf16[8,5120]{1,0:T(8,128)(2,1)S(1)} %get-tuple-element.18), channel_id=1, source_target_pairs={{1,0},{2,1},{3,2},{4,3},{5,4},{6,5},{7,6},{9,8},{10,9},{11,10},{12... | collective-permute-start | bytes 245768 | tf_op jit(solution)/shard_map/ppermute | solution.py:478
  10.0 0.0 copy-done.2
  10.0 0.0 copy-done
  10.1 0.0 copy-done.6
  10.1 0.0 copy-done.3
  10.1 0.9 %synth.1 = (f32[16,128]{1,0:T(8,128)S(1)}, bf16[8,5120]{1,0:T(8,128)(2,1)S(1)}, f32[16,128]{1,0:T(8,128)S(1)}) custom-call(s32[1,2]{1,0:T(1,128)S(1)} %bitcast.11, f32[2,4,5120]{2,1,0:T(4,128)S(1)} %copy-done, f32[1,5120]{1,0:T(1,128)S(1)} %bitcast.7, f32[2,5120]{1,0:T(2,128)S(1)} %copy-done.2, bf16[2,2,5120,128]{3,2,1,0:T(8,128)(2,1)S(1)} %get-tuple-element.14.legendre_ref), custom_call_target="tpu_custom_call" | custom-call | flops 10000000 | bytes 6000000 | tf_op jit(solution)/shard_map/synth/pallas_call | solution.py:462
  10.9 0.0 collective-permute-done.low_ref
  10.9 3.0 %collective-permute-done.1.high_ref = bf16[8,5120]{1,0:T(8,128)(2,1)S(1)} collective-permute-done((bf16[8,5120]{1,0:T(8,128)(2,1)S(1)}, bf16[8,5120]{1,0:T(8,128)(2,1)S(1)}, u32[]{:S(2)}, u32[]{:S(2)}) %collective-permute-start.1) | collective-permute-done | bytes 81952 | tf_op jit(solution)/shard_map/ppermute | solution.py:478
  13.9 1.1 %fields.1 = bf16[32,2,640]{2,1,0:T(2,128)(2,1)} custom-call(bf16[8,5120]{1,0:T(8,128)(2,1)S(1)} %get-tuple-element.16.coef_ref, bf16[8,5120]{1,0:T(8,128)(2,1)S(1)} %collective-permute-done.low_ref, bf16[8,5120]{1,0:T(8,128)(2,1)S(1)} %collective-permute-done.1.high_ref, f32[16,128]{1,0:T(8,128)S(1)} %get-tuple-element.19.own_ref), custom_call_target="tpu_custom_call" | custom-call | tf_op jit(solution)/shard_map/fields/pallas_call | solution.py:504
  15.0 9.9 %all-to-all-start = ((bf16[32,2,640]{2,1,0:T(2,128)(2,1)}), bf16[32,2,640]{2,1,0:T(2,128)(2,1)S(1)}, u32[]{:S(2)}, u32[]{:S(2)}) async-start(bf16[32,2,640]{2,1,0:T(2,128)(2,1)} %fields.1), calls=%async_computation | async-start | bytes 163840 | tf_op jit(solution)/shard_map/all_to_all | solution.py:512
  24.9 0.0 copy-done.7
  24.9 0.0 copy-done.5
  24.9 0.0 copy-done.4
  24.9 0.0 copy-done.1
  25.0 0.9 %pack.1 = (f32[24,4992]{1,0:T(8,128)S(1)}, s32[8,128]{1,0:T(8,128)S(1)}, f32[16,640]{1,0:T(8,128)S(1)}) custom-call(s32[1]{0:T(128)} %bitcast.band_ref, s32[1,1,32]{2,1,0:T(1,128)S(1)} %copy-done.7, f32[16,32,128]{2,1,0:T(8,128)S(1)} %bitcast.6, s32[2,32,128]{2,1,0:T(8,128)S(1)} %bitcast.9, f32[2,32,128]{2,1,0:T(8,128)S(1)} %bitcast.10, ...), custom_call_target="tpu_custom_call" | custom-call | flops 1000000 | bytes 3000000 | tf_op jit(solution)/shard_map/pack/pallas_call | solution.py:481
  25.9 8.5 %all-to-all-done.x_ref = bf16[32,2,640]{2,1,0:T(2,128)(2,1)S(1)} async-done(((bf16[32,2,640]{2,1,0:T(2,128)(2,1)}), bf16[32,2,640]{2,1,0:T(2,128)(2,1)S(1)}, u32[]{:S(2)}, u32[]{:S(2)}) %all-to-all-start) | async-done | bytes 81952 | tf_op jit(solution)/shard_map/all_to_all | solution.py:512
  34.3 5.8 %points.1 = (bf16[32,2,640]{2,1,0:T(2,128)(2,1)S(1)}, bf16[2,2,5120,128]{3,2,1,0:T(8,128)(2,1)S(1)}) custom-call(s32[8,128]{1,0:T(8,128)S(1)} %get-tuple-element.13.blocks_ref, f32[16,128]{1,0:T(8,128)S(1)} %get-tuple-element.15.sums_ref, bf16[32,2,640]{2,1,0:T(2,128)(2,1)S(1)} %all-to-all-done.x_ref, f32[24,4992]{1,0:T(8,128)S(1)} %get-tuple-element.20.data_ref, ...), custom_call_target="tpu_custom_call" | custom-call | tf_op jit(solution)/shard_map/points/pallas_call | solution.py:514
  40.2 12.6 %all_to_all.15.got_ref = bf16[32,2,640]{2,1,0:T(2,128)(2,1)S(1)} all-to-all(bf16[32,2,640]{2,1,0:T(2,128)(2,1)S(1)} %get-tuple-element.21), channel_id=1, replica_groups=mesh['harm'=32,'band'=8] {'harm'}, dimensions={0} | all-to-all | bytes 163840 | tf_op jit(solution)/shard_map/all_to_all | solution.py:536
  52.8 1.8 %analysis.1 = bf16[8,8,768]{2,1,0:T(8,128)(2,1)S(1)} custom-call(bf16[32,2,640]{2,1,0:T(2,128)(2,1)S(1)} %all_to_all.15.got_ref, bf16[8,5120]{1,0:T(8,128)(2,1)S(1)} %collective-permute-done.low_ref, bf16[8,5120]{1,0:T(8,128)(2,1)S(1)} %collective-permute-done.1.high_ref, bf16[2,2,5120,128]{3,2,1,0:T(8,128)(2,1)S(1)} %get-tuple-element.22.legendre_ref), custom_call_target="tpu_custom_call" | custom-call | tf_op jit(solution)/shard_map/analysis/pallas_call | solution.py:538
  54.5 15.9 %all_to_all.16.parts_ref = bf16[8,8,768]{2,1,0:T(8,128)(2,1)S(1)} all-to-all(bf16[8,8,768]{2,1,0:T(8,128)(2,1)S(1)} %analysis.1), channel_id=1, replica_groups=mesh['harm'=32,'band'=8] {'band'}, dimensions={0} | all-to-all | bytes 196608 | tf_op jit(solution)/shard_map/all_to_all | solution.py:546
  70.4 0.7 %update.1 = (f32[2,4,640]{2,1,0:T(4,128)}, f32[2,4,640]{2,1,0:T(4,128)}) custom-call(bf16[8,8,768]{2,1,0:T(8,128)(2,1)S(1)} %all_to_all.16.parts_ref, f32[16,640]{1,0:T(8,128)S(1)} %get-tuple-element.23.share_ref), custom_call_target="tpu_custom_call" | custom-call | tf_op jit(solution)/shard_map/update/pallas_call | solution.py:548
Async XLA Ops:
  0.6 9.4 %copy-start.2 = (f32[2,5120]{1,0:T(2,128)S(1)}, f32[2,5120]{1,0:T(2,128)}, u32[]{:S(2)}) copy-start(f32[2,5120]{1,0:T(2,128)} %spectra_ref.3) | copy-start | bytes 122884
  0.6 9.4 %copy-start = (f32[2,4,5120]{2,1,0:T(4,128)S(1)}, f32[2,4,5120]{2,1,0:T(4,128)}, u32[]{:S(2)}) copy-start(f32[2,4,5120]{2,1,0:T(4,128)} %side_ref.3) | copy-start | bytes 491524
  0.7 9.4 %copy-start.6 = (s32[2]{0:T(128)S(1)}, s32[2]{0:T(128)}, u32[]{:S(2)}) copy-start(s32[2]{0:T(128)} %param.12) | copy-start | bytes 28
  0.7 9.4 %copy-start.3 = (f32[5120]{0:T(1024)S(1)}, f32[5120]{0:T(1024)}, u32[]{:S(2)}) copy-start(f32[5120]{0:T(1024)} %param.11) | copy-start | bytes 61444
  0.7 24.2 %copy-start.7 = (s32[1,1,32]{2,1,0:T(1,128)S(1)}, s32[1,1,32]{2,1,0:T(1,128)}, u32[]{:S(2)}) copy-start(s32[1,1,32]{2,1,0:T(1,128)} %counts_ref.1) | copy-start | bytes 388
  0.7 24.2 %copy-start.5 = (f32[2,1,1,32,128]{4,3,2,1,0:T(8,128)S(1)}, f32[2,1,1,32,128]{4,3,2,1,0:T(8,128)}, u32[]{:S(2)}) copy-start(f32[2,1,1,32,128]{4,3,2,1,0:T(8,128)} %param.16) | copy-start | bytes 98308
  0.7 24.2 %copy-start.4 = (s32[2,1,1,32,128]{4,3,2,1,0:T(8,128)S(1)}, s32[2,1,1,32,128]{4,3,2,1,0:T(8,128)}, u32[]{:S(2)}) copy-start(s32[2,1,1,32,128]{4,3,2,1,0:T(8,128)} %param.15) | copy-start | bytes 98308
  0.7 24.2 %copy-start.1 = (f32[16,1,1,32,128]{4,3,2,1,0:T(8,128)S(1)}, f32[16,1,1,32,128]{4,3,2,1,0:T(8,128)}, u32[]{:S(2)}) copy-start(f32[16,1,1,32,128]{4,3,2,1,0:T(8,128)} %param.14) | copy-start | bytes 786436
  4.2 6.8 %collective-permute-start = (bf16[8,5120]{1,0:T(8,128)(2,1)S(1)}, bf16[8,5120]{1,0:T(8,128)(2,1)S(1)}, u32[]{:S(2)}, u32[]{:S(2)}) collective-permute-start(bf16[8,5120]{1,0:T(8,128)(2,1)S(1)} %get-tuple-element.17), channel_id=1, source_target_pairs={{0,1},{1,2},{2,3},{3,4},{4,5},{5,6},{6,7},{8,9},{9,10},{10,11},{11... | collective-permute-start | bytes 245768 | tf_op jit(solution)/shard_map/ppermute | solution.py:477
  7.6 6.3 %collective-permute-start.1 = (bf16[8,5120]{1,0:T(8,128)(2,1)S(1)}, bf16[8,5120]{1,0:T(8,128)(2,1)S(1)}, u32[]{:S(2)}, u32[]{:S(2)}) collective-permute-start(bf16[8,5120]{1,0:T(8,128)(2,1)S(1)} %get-tuple-element.18), channel_id=1, source_target_pairs={{1,0},{2,1},{3,2},{4,3},{5,4},{6,5},{7,6},{9,8},{10,9},{11,10},{12... | collective-permute-start | bytes 245768 | tf_op jit(solution)/shard_map/ppermute | solution.py:478
  15.0 19.3 %all-to-all-start = ((bf16[32,2,640]{2,1,0:T(2,128)(2,1)}), bf16[32,2,640]{2,1,0:T(2,128)(2,1)S(1)}, u32[]{:S(2)}, u32[]{:S(2)}) async-start(bf16[32,2,640]{2,1,0:T(2,128)(2,1)} %fields.1), calls=%async_computation | async-start | bytes 163840 | tf_op jit(solution)/shard_map/all_to_all | solution.py:512

commit v6 on v5

--- a/solution.py
+++ b/solution.py
@@ -152,12 +152,12 @@
     term_ref[...] = jnp.zeros_like(term_ref)
     hit_ref[...] = jnp.zeros_like(hit_ref)
 
-    def spread():
+    def spread(slot):
         acc_ref[:, 0:ROWS] += lax.dot_general(
-            term_ref[...], hit_ref[...], (((1,), (1,)), ((), ())), preferred_element_type=F32
+            term_ref[slot], hit_ref[slot], (((1,), (1,)), ((), ())), preferred_element_type=F32
         )
 
-    def sample(index):
+    def sample(index, slot):
         start = pl.multiple_of(index * BLOCK, BLOCK)
         info = data_ref[16:24, pl.ds(start, BLOCK)]
         first_row = info[0:1]
@@ -165,10 +165,10 @@
         total = [None, None]
         for a in range(4):
             row_hit = jnp.where(grid_row == (first_row + float(a)).astype(BF16), one, zero)
-            hit_ref[:, a * BLOCK : (a + 1) * BLOCK] = row_hit
+            hit_ref[slot, :, a * BLOCK : (a + 1) * BLOCK] = row_hit
             picked = jnp.dot(field_ref[:, 0:ROWS], row_hit, preferred_element_type=F32)
-            wave_re = wave_ref[2 * a]
-            wave_im = wave_ref[2 * a + 1]
+            wave_re = wave_ref[slot, 2 * a]
+            wave_im = wave_ref[slot, 2 * a + 1]
             for f in range(2):
                 term = (
                     picked[128 * f : 128 * f + 64] * wave_re
@@ -185,11 +185,11 @@
             for f in range(2):
                 for part in range(2):
                     row = 128 * f + 64 * part
-                    term_ref[row : row + 64, a * BLOCK : (a + 1) * BLOCK] = (
-                        weighted[f] * wave_ref[2 * a + part]
+                    term_ref[slot, row : row + 64, a * BLOCK : (a + 1) * BLOCK] = (
+                        weighted[f] * wave_ref[slot, 2 * a + part]
                     ).astype(BF16)
 
-    def turn(index):
+    def turn(index, slot):
         data = data_ref[:, pl.ds(pl.multiple_of(index * BLOCK, BLOCK), BLOCK)]
         pixel = data[17:18].astype(jnp.int32)
         digit_id = grid_ref[0:32, :]
@@ -210,18 +210,28 @@
         turn_re = mid_re * part[4] - mid_im * part[5]
         turn_im = mid_re * part[5] + mid_im * part[4]
         for a in range(4):
-            wave_ref[2 * a] = turn_re * part[6 + 2 * a] - turn_im * part[7 + 2 * a]
-            wave_ref[2 * a + 1] = turn_re * part[7 + 2 * a] + turn_im * part[6 + 2 * a]
-
-    def block_step(index, carry):
-        spread()
-        sample(index)
-        turn(index + 1)
+            wave_ref[slot, 2 * a] = turn_re * part[6 + 2 * a] - turn_im * part[7 + 2 * a]
+            wave_ref[slot, 2 * a + 1] = turn_re * part[7 + 2 * a] + turn_im * part[6 + 2 * a]
+
+    def pair_step(index, carry):
+        turn(2 * index + 1, 1)
+        sample(2 * index, 0)
+        spread(1)
+        turn(2 * index + 2, 0)
+        sample(2 * index + 1, 1)
+        spread(0)
         return carry
 
-    turn(0)
-    lax.fori_loop(0, jnp.max(blocks_ref[...]), block_step, 0)
-    spread()
+    count = jnp.max(blocks_ref[...])
+    turn(0, 0)
+    lax.fori_loop(0, count >> 1, pair_step, 0)
+    spread(1)
+
+    @pl.when((count & 1) == 1)
+    def _():
+        sample(count - 1, 0)
+        spread(0)
+
     curvature = jnp.sum(curv_ref[...], axis=(0, 1), keepdims=True) + jnp.sum(
         sums_ref[8:16], axis=(0, 1), keepdims=True
     )
@@ -356,6 +366,11 @@
         out_ref[target] = sent
 
 
+def both_halves(value):
+    rounded = value.astype(BF16)
+    return jnp.concatenate([rounded, (value - rounded.astype(F32)).astype(BF16)], axis=0)
+
+
 def analysis_kernel(got_ref, low_ref, high_ref, legendre_ref, out_ref):
     total = got_ref[0].astype(F32)
     for source in range(1, 32):
@@ -382,12 +397,12 @@
     row_both = lax.broadcasted_iota(jnp.int32, (8, 256), 0)
     owns = []
     for m in range(2):
-        owns.append(jnp.where((row_both >> 2) == m, own_both, 0.0).astype(BF16))
+        owns.append(both_halves(jnp.where((row_both >> 2) == m, own_both, 0.0)))
     low_swap, high_swap = swap_rows(low), swap_rows(high)
     rim = jnp.where(lane < 2, -low, jnp.where(lane < 4, pltpu.roll(low_swap, 2, 1), 0.0))
     rim = jnp.where((lane >= 8) & (lane < 10), pltpu.roll(-high, 6, 1), rim)
     rim = jnp.where((lane >= 10) & (lane < 12), pltpu.roll(high_swap, 8, 1), rim)
-    rim = jnp.where(row < 4, rim, pltpu.roll(rim, 4, 1)).astype(BF16)
+    rim = both_halves(jnp.where(row < 4, rim, pltpu.roll(rim, 4, 1)))
 
 
     bands = out_ref.shape[0]
@@ -401,7 +416,7 @@
             result = result + lax.dot_general(
                 owns[m], table, (((1,), (1,)), ((), ())), preferred_element_type=F32
             )
-        out_ref[band, :, 0:chunk] = result.astype(BF16)
+        out_ref[band, :, 0:chunk] = (result[0:8] + result[8:16]).astype(BF16)
         out_ref[band, :, chunk : chunk + 128] = sums
 
 
@@ -525,9 +540,9 @@
             pltpu.VMEM((256, LANES), F32),
             pltpu.VMEM((2, BLOCK), F32),
             pltpu.VMEM((ROWS, BLOCK), BF16),
-            pltpu.VMEM((8, 64, BLOCK), F32),
-            pltpu.VMEM((256, 4 * BLOCK), BF16),
-            pltpu.VMEM((ROWS, 4 * BLOCK), BF16),
+            pltpu.VMEM((2, 8, 64, BLOCK), F32),
+            pltpu.VMEM((2, 256, 4 * BLOCK), BF16),
+            pltpu.VMEM((2, ROWS, 4 * BLOCK), BF16),
             pltpu.SemaphoreType.DMA(()),
         ],
         compiler_params=stream_params,

time: 71.1 us -> 71 us (level)
  no operation moved by 1% of the time
where the time goes in v6:
time: 71 us; the launch traced here: 71.3 us
  blocking collectives  28.3 us (40%)
  starting transfers between devices  15.7 us (22%)
  Pallas kernels  15 us (21%)
  waiting for transfers between devices  11.5 us (16%)
  between operations  0.81 us (1%)
    all_to_all x1, blocking collectives, local(): lax.all_to_all(harmonic, 'band', split_axis=0, concat_axis=0, tiled=True)  15.9 us
    all_to_all x1, blocking collectives, local(): lax.all_to_all(back, 'harm', split_axis=0, concat_axis=0, tiled=True)  12.4 us
    all_to_all x1, starting transfers between devices, local(): got = lax.all_to_all(sent, 'harm', split_axis=0, concat_axis=0, tiled=True)  9.86 us
    all_to_all x1, waiting for transfers between devices, local(): got = lax.all_to_all(sent, 'harm', split_axis=0, concat_axis=0, tiled=True)  8.48 us
    pallas_call x1, Pallas kernels, local(): pl.pallas_call(points_kernel, out_shape=(jax.ShapeDtypeStruct((32, 2, PIE...  6.23 us
    pallas_call x1, Pallas kernels, local(): pl.pallas_call(edge_kernel, out_shape=(jax.ShapeDtypeStruct((8, lmax_len)...  3.46 us
    ppermute x1, starting transfers between devices, local(): low_rim = lax.ppermute(low_edge, 'band', up)  3.4 us
    ppermute x1, waiting for transfers between devices, local(): high_rim = lax.ppermute(high_edge, 'band', down)  2.98 us
  transfers between devices with their start and end apart: 3, of which 2 were waited for; matrix products, arithmetic and copies ran while one was open for 0% of the time, Pallas kernels for 2%

profile of v6, /device:TPU:2, one launch (start us, length us, event | category | flops | bytes accessed | tf_op | source)
XLA Modules:
  0.0 71.3 jit_solution(17264559367168561292)
XLA Ops:
  0.6 0.0 copy-start.2
  0.6 0.0 copy-start
  0.7 0.0 copy-start.6
  0.7 0.0 copy-start.3
  0.7 0.0 copy-start.7
  0.7 0.0 copy-start.5
  0.7 0.0 copy-start.4
  0.7 0.0 copy-start.1
  0.7 3.5 %edges.1 = (bf16[8,5120]{1,0:T(8,128)(2,1)S(1)}, bf16[8,5120]{1,0:T(8,128)(2,1)S(1)}, bf16[2,2,5120,128]{3,2,1,0:T(8,128)(2,1)S(1)}) custom-call(bf16[2,2,5120,128]{3,2,1,0:T(8,128)(2,1)} %source_ref.3), custom_call_target="tpu_custom_call" | custom-call | tf_op jit(solution)/shard_map/edges/pallas_call | solution.py:464
  4.2 3.4 %collective-permute-start = (bf16[8,5120]{1,0:T(8,128)(2,1)S(1)}, bf16[8,5120]{1,0:T(8,128)(2,1)S(1)}, u32[]{:S(2)}, u32[]{:S(2)}) collective-permute-start(bf16[8,5120]{1,0:T(8,128)(2,1)S(1)} %get-tuple-element.17), channel_id=1, source_target_pairs={{0,1},{1,2},{2,3},{3,4},{4,5},{5,6},{6,7},{8,9},{9,10},{10,11},{11... | collective-permute-start | bytes 245768 | tf_op jit(solution)/shard_map/ppermute | solution.py:492
  7.6 2.4 %collective-permute-start.1 = (bf16[8,5120]{1,0:T(8,128)(2,1)S(1)}, bf16[8,5120]{1,0:T(8,128)(2,1)S(1)}, u32[]{:S(2)}, u32[]{:S(2)}) collective-permute-start(bf16[8,5120]{1,0:T(8,128)(2,1)S(1)} %get-tuple-element.18), channel_id=1, source_target_pairs={{1,0},{2,1},{3,2},{4,3},{5,4},{6,5},{7,6},{9,8},{10,9},{11,10},{12... | collective-permute-start | bytes 245768 | tf_op jit(solution)/shard_map/ppermute | solution.py:493
  10.0 0.0 copy-done.2
  10.0 0.0 copy-done
  10.1 0.0 copy-done.6
  10.1 0.0 copy-done.3
  10.1 0.9 %synth.1 = (f32[16,128]{1,0:T(8,128)S(1)}, bf16[8,5120]{1,0:T(8,128)(2,1)S(1)}, f32[16,128]{1,0:T(8,128)S(1)}) custom-call(s32[1,2]{1,0:T(1,128)S(1)} %bitcast.11, f32[2,4,5120]{2,1,0:T(4,128)S(1)} %copy-done, f32[1,5120]{1,0:T(1,128)S(1)} %bitcast.7, f32[2,5120]{1,0:T(2,128)S(1)} %copy-done.2, bf16[2,2,5120,128]{3,2,1,0:T(8,128)(2,1)S(1)} %get-tuple-element.14.legendre_ref), custom_call_target="tpu_custom_call" | custom-call | flops 10000000 | bytes 6000000 | tf_op jit(solution)/shard_map/synth/pallas_call | solution.py:477
  10.9 0.0 collective-permute-done.low_ref
  10.9 3.0 %collective-permute-done.1.high_ref = bf16[8,5120]{1,0:T(8,128)(2,1)S(1)} collective-permute-done((bf16[8,5120]{1,0:T(8,128)(2,1)S(1)}, bf16[8,5120]{1,0:T(8,128)(2,1)S(1)}, u32[]{:S(2)}, u32[]{:S(2)}) %collective-permute-start.1) | collective-permute-done | bytes 81952 | tf_op jit(solution)/shard_map/ppermute | solution.py:493
  13.9 1.1 %fields.1 = bf16[32,2,640]{2,1,0:T(2,128)(2,1)} custom-call(bf16[8,5120]{1,0:T(8,128)(2,1)S(1)} %get-tuple-element.16.coef_ref, bf16[8,5120]{1,0:T(8,128)(2,1)S(1)} %collective-permute-done.low_ref, bf16[8,5120]{1,0:T(8,128)(2,1)S(1)} %collective-permute-done.1.high_ref, f32[16,128]{1,0:T(8,128)S(1)} %get-tuple-element.19.own_ref), custom_call_target="tpu_custom_call" | custom-call | tf_op jit(solution)/shard_map/fields/pallas_call | solution.py:519
  15.0 9.9 %all-to-all-start = ((bf16[32,2,640]{2,1,0:T(2,128)(2,1)}), bf16[32,2,640]{2,1,0:T(2,128)(2,1)S(1)}, u32[]{:S(2)}, u32[]{:S(2)}) async-start(bf16[32,2,640]{2,1,0:T(2,128)(2,1)} %fields.1), calls=%async_computation | async-start | bytes 163840 | tf_op jit(solution)/shard_map/all_to_all | solution.py:527
  24.9 0.0 copy-done.7
  24.9 0.0 copy-done.5
  24.9 0.0 copy-done.4
  24.9 0.0 copy-done.1
  25.0 0.9 %pack.1 = (f32[24,4992]{1,0:T(8,128)S(1)}, s32[8,128]{1,0:T(8,128)S(1)}, f32[16,640]{1,0:T(8,128)S(1)}) custom-call(s32[1]{0:T(128)} %bitcast.band_ref, s32[1,1,32]{2,1,0:T(1,128)S(1)} %copy-done.7, f32[16,32,128]{2,1,0:T(8,128)S(1)} %bitcast.6, s32[2,32,128]{2,1,0:T(8,128)S(1)} %bitcast.9, f32[2,32,128]{2,1,0:T(8,128)S(1)} %bitcast.10, ...), custom_call_target="tpu_custom_call" | custom-call | flops 1000000 | bytes 3000000 | tf_op jit(solution)/shard_map/pack/pallas_call | solution.py:496
  25.9 8.5 %all-to-all-done.x_ref = bf16[32,2,640]{2,1,0:T(2,128)(2,1)S(1)} async-done(((bf16[32,2,640]{2,1,0:T(2,128)(2,1)}), bf16[32,2,640]{2,1,0:T(2,128)(2,1)S(1)}, u32[]{:S(2)}, u32[]{:S(2)}) %all-to-all-start) | async-done | bytes 81952 | tf_op jit(solution)/shard_map/all_to_all | solution.py:527
  34.3 6.2 %points.1 = (bf16[32,2,640]{2,1,0:T(2,128)(2,1)S(1)}, bf16[2,2,5120,128]{3,2,1,0:T(8,128)(2,1)S(1)}) custom-call(s32[8,128]{1,0:T(8,128)S(1)} %get-tuple-element.13.blocks_ref, f32[16,128]{1,0:T(8,128)S(1)} %get-tuple-element.15.sums_ref, bf16[32,2,640]{2,1,0:T(2,128)(2,1)S(1)} %all-to-all-done.x_ref, f32[24,4992]{1,0:T(8,128)S(1)} %get-tuple-element.20.data_ref, ...), custom_call_target="tpu_custom_call" | custom-call | tf_op jit(solution)/shard_map/points/pallas_call | solution.py:529
  40.6 12.4 %all_to_all.15.got_ref = bf16[32,2,640]{2,1,0:T(2,128)(2,1)S(1)} all-to-all(bf16[32,2,640]{2,1,0:T(2,128)(2,1)S(1)} %get-tuple-element.21), channel_id=1, replica_groups=mesh['harm'=32,'band'=8] {'harm'}, dimensions={0} | all-to-all | bytes 163840 | tf_op jit(solution)/shard_map/all_to_all | solution.py:551
  53.0 1.8 %analysis.1 = bf16[8,8,768]{2,1,0:T(8,128)(2,1)S(1)} custom-call(bf16[32,2,640]{2,1,0:T(2,128)(2,1)S(1)} %all_to_all.15.got_ref, bf16[8,5120]{1,0:T(8,128)(2,1)S(1)} %collective-permute-done.low_ref, bf16[8,5120]{1,0:T(8,128)(2,1)S(1)} %collective-permute-done.1.high_ref, bf16[2,2,5120,128]{3,2,1,0:T(8,128)(2,1)S(1)} %get-tuple-element.22.legendre_ref), custom_call_target="tpu_custom_call" | custom-call | tf_op jit(solution)/shard_map/analysis/pallas_call | solution.py:553
  54.7 15.9 %all_to_all.16.parts_ref = bf16[8,8,768]{2,1,0:T(8,128)(2,1)S(1)} all-to-all(bf16[8,8,768]{2,1,0:T(8,128)(2,1)S(1)} %analysis.1), channel_id=1, replica_groups=mesh['harm'=32,'band'=8] {'band'}, dimensions={0} | all-to-all | bytes 196608 | tf_op jit(solution)/shard_map/all_to_all | solution.py:561
  70.6 0.7 update.1
Async XLA Ops:
  0.6 9.4 %copy-start.2 = (f32[2,5120]{1,0:T(2,128)S(1)}, f32[2,5120]{1,0:T(2,128)}, u32[]{:S(2)}) copy-start(f32[2,5120]{1,0:T(2,128)} %spectra_ref.3) | copy-start | bytes 122884
  0.6 9.4 %copy-start = (f32[2,4,5120]{2,1,0:T(4,128)S(1)}, f32[2,4,5120]{2,1,0:T(4,128)}, u32[]{:S(2)}) copy-start(f32[2,4,5120]{2,1,0:T(4,128)} %side_ref.3) | copy-start | bytes 491524
  0.7 9.4 %copy-start.6 = (s32[2]{0:T(128)S(1)}, s32[2]{0:T(128)}, u32[]{:S(2)}) copy-start(s32[2]{0:T(128)} %param.12) | copy-start | bytes 28
  0.7 9.4 %copy-start.3 = (f32[5120]{0:T(1024)S(1)}, f32[5120]{0:T(1024)}, u32[]{:S(2)}) copy-start(f32[5120]{0:T(1024)} %param.11) | copy-start | bytes 61444
  0.7 24.2 %copy-start.7 = (s32[1,1,32]{2,1,0:T(1,128)S(1)}, s32[1,1,32]{2,1,0:T(1,128)}, u32[]{:S(2)}) copy-start(s32[1,1,32]{2,1,0:T(1,128)} %counts_ref.1) | copy-start | bytes 388
  0.7 24.2 %copy-start.5 = (f32[2,1,1,32,128]{4,3,2,1,0:T(8,128)S(1)}, f32[2,1,1,32,128]{4,3,2,1,0:T(8,128)}, u32[]{:S(2)}) copy-start(f32[2,1,1,32,128]{4,3,2,1,0:T(8,128)} %param.16) | copy-start | bytes 98308
  0.7 24.2 %copy-start.4 = (s32[2,1,1,32,128]{4,3,2,1,0:T(8,128)S(1)}, s32[2,1,1,32,128]{4,3,2,1,0:T(8,128)}, u32[]{:S(2)}) copy-start(s32[2,1,1,32,128]{4,3,2,1,0:T(8,128)} %param.15) | copy-start | bytes 98308
  0.7 24.2 %copy-start.1 = (f32[16,1,1,32,128]{4,3,2,1,0:T(8,128)S(1)}, f32[16,1,1,32,128]{4,3,2,1,0:T(8,128)}, u32[]{:S(2)}) copy-start(f32[16,1,1,32,128]{4,3,2,1,0:T(8,128)} %param.14) | copy-start | bytes 786436
  4.2 6.8 %collective-permute-start = (bf16[8,5120]{1,0:T(8,128)(2,1)S(1)}, bf16[8,5120]{1,0:T(8,128)(2,1)S(1)}, u32[]{:S(2)}, u32[]{:S(2)}) collective-permute-start(bf16[8,5120]{1,0:T(8,128)(2,1)S(1)} %get-tuple-element.17), channel_id=1, source_target_pairs={{0,1},{1,2},{2,3},{3,4},{4,5},{5,6},{6,7},{8,9},{9,10},{10,11},{11... | collective-permute-start | bytes 245768 | tf_op jit(solution)/shard_map/ppermute | solution.py:492
  7.6 6.3 %collective-permute-start.1 = (bf16[8,5120]{1,0:T(8,128)(2,1)S(1)}, bf16[8,5120]{1,0:T(8,128)(2,1)S(1)}, u32[]{:S(2)}, u32[]{:S(2)}) collective-permute-start(bf16[8,5120]{1,0:T(8,128)(2,1)S(1)} %get-tuple-element.18), channel_id=1, source_target_pairs={{1,0},{2,1},{3,2},{4,3},{5,4},{6,5},{7,6},{9,8},{10,9},{11,10},{12... | collective-permute-start | bytes 245768 | tf_op jit(solution)/shard_map/ppermute | solution.py:493
  15.0 19.3 %all-to-all-start = ((bf16[32,2,640]{2,1,0:T(2,128)(2,1)}), bf16[32,2,640]{2,1,0:T(2,128)(2,1)S(1)}, u32[]{:S(2)}, u32[]{:S(2)}) async-start(bf16[32,2,640]{2,1,0:T(2,128)(2,1)} %fields.1), calls=%async_computation | async-start | bytes 163840 | tf_op jit(solution)/shard_map/all_to_all | solution.py:527
